TPU v7x, 256 devices: a whole 4x4x8 slice. The times are simulated.
256 devices in a mesh: dp: 32 (over z_lo, y, core), tensor: 8 (over x, z_hi).
Axes of the slice: x: 4, y: 4, z: 8 (z_hi: 2, z_lo: 4; z = z_hi * 4 + z_lo), core: 2. Of those that a mesh axis runs over, the one named last changes fastest.
Arguments:
- grad: bfloat16 [32, 1024, 16384], P('dp', None, 'tensor'), may hold values from -6 to 6
- error: bfloat16 [32, 1024, 16384], P('dp', None, 'tensor'), may hold values from -4 to 4
- q_init: bfloat16 [16384, 32], P('tensor'), may hold values from -6 to 6
Outputs:
- p_basis: float32 [1024, 32], P(('dp', 'tensor'))
- q_factor: float32 [16384, 32], P('tensor')
- new_error: bfloat16 [32, 1024, 16384], P('dp', None, 'tensor')
All inputs are finite; a program needn't handle non-finite values.
Results may differ from a plain program's by a relative error of at most 0.03.
Values may be sent and summed in bfloat16 or wider, within the bound.
No kernel may reach another device: no remote copies, remote signals or barrier semaphores. Data moves between devices by JAX's collectives and lax.ppermute only.
A program may use at most 64 MiB of HBM per device.

v0:
```python
import math

import jax
import jax.numpy as jnp
from jax import lax
from jax.sharding import PartitionSpec as P

ROWS = 1024
ITERS = 3


def lower_factor(gram):
    return jnp.linalg.cholesky(gram)


def apply_basis(chol, left):
    return lax.linalg.triangular_solve(chol, left, left_side=False, lower=True, transpose_a=True)


def shards(grad, error, q_init):
    replicas = lax.axis_size("dp")
    groups = lax.axis_size(("dp", "tensor"))
    corrected = (grad[0].astype(jnp.float32) + error[0].astype(jnp.float32)).astype(jnp.bfloat16)
    total_rows = corrected.shape[0]
    own_rows = total_rows // groups
    qb = q_init
    own_basis = jnp.zeros((own_rows, q_init.shape[1]), jnp.float32)
    right = jnp.zeros(q_init.shape, jnp.float32)
    pb = jnp.zeros((total_rows, q_init.shape[1]), jnp.bfloat16)
    for step in range(ITERS):
        partial_value = jnp.dot(corrected, qb, preferred_element_type=jnp.float32) / replicas
        left = lax.psum(partial_value, ("dp", "tensor"))
        gram = jnp.dot(left.T, left, precision=lax.Precision.HIGHEST)
        basis = apply_basis(lower_factor(gram), left)
        start = lax.axis_index(("dp", "tensor")) * own_rows
        own_basis = lax.dynamic_slice_in_dim(basis, start, own_rows, 0)
        pb = basis.astype(jnp.bfloat16)
        term = lax.dot_general(
            corrected, pb, (((0,), (0,)), ((), ())), preferred_element_type=jnp.float32
        )
        summed = lax.psum(term.astype(jnp.bfloat16), "dp").astype(jnp.float32)
        right = summed / replicas
        qb = right.astype(jnp.bfloat16)
    approx = jnp.dot(pb, qb.T, preferred_element_type=jnp.float32)
    new_error = (corrected.astype(jnp.float32) - approx).astype(jnp.bfloat16)[None]
    return (own_basis * math.sqrt(ROWS), right / math.sqrt(ROWS), new_error)


def solution(mesh):
    placed = (P("dp", None, "tensor"), P("dp", None, "tensor"), P("tensor", None))
    return jax.shard_map(
        shards,
        mesh=mesh,
        in_specs=placed,
        out_specs=(P(("dp", "tensor"), None), P("tensor", None), P("dp", None, "tensor")),
        check_vma=False,
    )
```

profile of v0, /device:TPU:1, one launch (start us, length us, event | category | flops | bytes accessed | tf_op | source)
XLA Modules:
  0.0 1558.4 jit_solution(9974751032158719666)
XLA Ops:
  7.2 0.0 all-reduce.7.cloned.1.call-start
  7.2 5.4 fusion
  12.7 2.0 copy-done.1
  14.7 2.0 convolution_multiply_fusion.2
  16.7 0.0 all-reduce.7.cloned.1.call-update
  16.7 0.0 all-reduce.9.cloned.1.call-start
  16.7 244.8 %all-reduce.7.cloned.1.call-done = f32[1024,32]{0,1:T(8,128)} async-done(((f32[1024,32]{0,1:T(8,128)}), f32[1024,32]{0,1:T(8,128)}) %all-reduce.7.cloned.1.call-update) | async-done | bytes 131088 | tf_op jit(solution)/shard_map/psum | solution.py:32
  261.5 1.2 fusion.27
  262.7 0.1 copy.6
  262.8 2.9 cholesky.59
  265.8 0.6 compare_reduce_fusion.2
  266.4 0.7 fusion.11
  267.1 2.4 custom-call.7
  269.5 1.2 fusion.2
  270.8 3.7 convolution_convert_fusion.2
  274.4 0.0 all-reduce.9.cloned.1.call-update
  274.5 0.0 all-reduce.11.cloned.1.call-start
  274.5 250.1 %all-reduce.9.cloned.1.call-done = bf16[2048,32]{0,1:T(8,128)(2,1)} async-done(((bf16[2048,32]{0,1:T(8,128)(2,1)}), bf16[2048,32]{0,1:T(8,128)(2,1)}) %all-reduce.9.cloned.1.call-update) | async-done | bytes 131088 | tf_op jit(solution)/shard_map/psum | solution.py:41
  524.6 4.2 convolution_multiply_fusion.1
  528.9 0.0 all-reduce.13.cloned.1.call-start
  528.9 243.4 %all-reduce.11.cloned.1.call-done = f32[1024,32]{0,1:T(8,128)} async-done(((f32[1024,32]{0,1:T(8,128)}), f32[1024,32]{0,1:T(8,128)}) %all-reduce.11.cloned.1.call-update) | async-done | bytes 131088 | tf_op jit(solution)/shard_map/psum | solution.py:32
  772.4 1.2 fusion.28
  773.6 0.1 copy.7
  773.7 2.9 cholesky.70
  776.6 0.6 compare_reduce_fusion.1
  777.3 0.7 fusion.12
  777.9 2.4 custom-call.8
  780.4 1.2 fusion.3
  781.6 3.7 convolution_convert_fusion.1
  785.3 0.0 all-reduce.15.cloned.1.call-start
  785.4 250.1 %all-reduce.13.cloned.1.call-done = bf16[2048,32]{0,1:T(8,128)(2,1)} async-done(((bf16[2048,32]{0,1:T(8,128)(2,1)}), bf16[2048,32]{0,1:T(8,128)(2,1)}) %all-reduce.13.cloned.1.call-update) | async-done | bytes 131088 | tf_op jit(solution)/shard_map/psum | solution.py:41
  1035.5 4.2 convolution_multiply_fusion
  1039.7 0.0 all-reduce.15.cloned.1.call-update
  1039.7 0.0 all-reduce.17.cloned.1.call-start
  1039.7 242.4 %all-reduce.15.cloned.1.call-done = f32[1024,32]{0,1:T(8,128)} async-done(((f32[1024,32]{0,1:T(8,128)}), f32[1024,32]{0,1:T(8,128)}) %all-reduce.15.cloned.1.call-update) | async-done | bytes 131088 | tf_op jit(solution)/shard_map/psum | solution.py:32
  1282.1 1.2 fusion.29
  1283.4 0.1 copy.8
  1283.5 2.9 cholesky.81
  1286.4 0.6 compare_reduce_fusion
  1287.1 0.7 fusion.13
  1287.7 2.4 custom-call.9
  1290.1 1.2 convolution_bitcast_fusion
  1291.4 3.7 convolution_convert_fusion
  1295.1 0.1 dynamic-slice_multiply_fusion
  1295.2 0.7 copy.9
  1295.8 249.4 %all-reduce.17.cloned.1.call-done = bf16[2048,32]{0,1:T(8,128)(2,1)} async-done(((bf16[2048,32]{0,1:T(8,128)(2,1)}), bf16[2048,32]{0,1:T(8,128)(2,1)}) %all-reduce.17.cloned.1.call-update) | async-done | bytes 131088 | tf_op jit(solution)/shard_map/psum | solution.py:41
  1545.3 5.6 fusion.1
  1550.9 0.7 convert_multiply_fusion.1
  (14 shorter events, 0.2 us)
Async XLA Ops:
  7.2 7.5 copy-start
  7.2 254.3 %all-reduce.7.cloned.1.call-start = ((), (), s32[]{:S(2)}) async-start(), calls=%async_computation | async-start | bytes 262144 | tf_op jit(solution)/shard_map/psum | solution.py:32
  12.6 2.0 copy-start.1
  16.7 507.9 %all-reduce.9.cloned.1.call-start = ((), (), s32[]{:S(2)}) async-start(), calls=%async_computation.1 | async-start | bytes 262144 | tf_op jit(solution)/shard_map/psum | solution.py:41
  274.5 497.9 %all-reduce.11.cloned.1.call-start = ((), (), s32[]{:S(2)}) async-start(), calls=%async_computation.2 | async-start | bytes 262144 | tf_op jit(solution)/shard_map/psum | solution.py:32
  528.9 506.6 %all-reduce.13.cloned.1.call-start = ((), (), s32[]{:S(2)}) async-start(), calls=%async_computation.3 | async-start | bytes 262144 | tf_op jit(solution)/shard_map/psum | solution.py:41
  785.3 496.8 %all-reduce.15.cloned.1.call-start = ((), (), s32[]{:S(2)}) async-start(), calls=%async_computation.4 | async-start | bytes 262144 | tf_op jit(solution)/shard_map/psum | solution.py:32
  1039.7 505.6 %all-reduce.17.cloned.1.call-start = ((), (), s32[]{:S(2)}) async-start(), calls=%async_computation.5 | async-start | bytes 262144 | tf_op jit(solution)/shard_map/psum | solution.py:41
  1545.3 5.6 copy-start.2
Sparse Core Ops, SparseCore 0:
  16.8 244.6 all-reduce.6
  274.6 250.0 all-reduce.8
  531.6 240.6 all-reduce.10
  785.4 250.0 all-reduce.12
  1041.4 240.6 all-reduce.14
  1295.2 250.0 all-reduce.16
where the time goes:
time: 1560 us
  waiting for transfers between devices  1480 us (95%)
  matrix products  34.4 us (2%)
  other arithmetic  26.3 us (2%)
    psum x3, waiting for transfers between devices, shards(): summed = lax.psum(term.astype(jnp.bfloat16), 'dp').astype(jnp.float32)  750 us
    psum x3, waiting for transfers between devices, shards(): left = lax.psum(partial_value, ('dp', 'tensor'))  731 us
  transfers between devices with their start and end apart: 6, of which 6 were waited for; matrix products, arithmetic and copies ran while one was open for 0% of the time, Pallas kernels for 0%

commit v1 on v0

v1 whole, which is shorter than its diff:
```python
import math

import jax
import jax.numpy as jnp
from jax import lax
from jax.sharding import Mesh, PartitionSpec as P

ROWS = 1024
ITERS = 3
SWAP = [(0, 1), (1, 0)]
CHIPS = ("zl", "y", "x", "zh")


def shift(n, d):
    return [(i, (i + d) % n) for i in range(n)]


def exchange_sum(value, axis, width):
    n = lax.axis_size(axis)
    me = lax.axis_index(axis)
    rows = value.shape[0]
    total = lax.dynamic_slice(value, (0, me * width), (rows, width)).astype(jnp.float32)
    for d in (2, 1, 3):
        piece = lax.dynamic_slice(value, (0, lax.rem(me + d, n) * width), (rows, width))
        total = total + lax.ppermute(piece, axis, shift(n, d)).astype(jnp.float32)
    return total


def reduce_replicas(corrected):
    core = lax.axis_index("c")
    half = corrected.shape[0] // 2
    cols = corrected.shape[1]
    own = lax.dynamic_slice(corrected, (core * half, 0), (half, cols))
    away = lax.dynamic_slice(corrected, ((1 - core) * half, 0), (half, cols))
    got = lax.ppermute(away, "c", SWAP)
    pair = (own.astype(jnp.float32) + got.astype(jnp.float32)).astype(jnp.bfloat16)
    quarter = exchange_sum(pair, "y", cols // 4).astype(jnp.bfloat16)
    return exchange_sum(quarter, "zl", cols // 16).astype(jnp.bfloat16)


def join_cores(value):
    core = lax.axis_index("c")
    got = lax.ppermute(value, "c", SWAP)
    first = jnp.where(core == 0, value, got)
    second = jnp.where(core == 0, got, value)
    return first, second


def sum_chips(value):
    parts = lax.all_to_all(value, CHIPS, 0, 0, tiled=True)
    total = jnp.sum(parts, axis=0, keepdims=True)
    return lax.all_to_all(jnp.broadcast_to(total, value.shape), CHIPS, 0, 0, tiled=True)


def shards(grad, error, q_init):
    replicas = 32
    y, zl = lax.axis_index("y"), lax.axis_index("zl")
    corrected = (grad[0].astype(jnp.float32) + error[0].astype(jnp.float32)).astype(jnp.bfloat16)
    rank = q_init.shape[1]
    mine = reduce_replicas(corrected)
    width = mine.shape[1]
    mean = jnp.concatenate(join_cores(mine), axis=0)
    qt = lax.dynamic_slice(q_init, ((y * 4 + zl) * width, 0), (width, rank)).T
    for step in range(ITERS):
        part = lax.dot_general(qt, mine, (((1,), (1,)), ((), ())), preferred_element_type=jnp.float32)
        part = part.reshape(rank, 4, 128).transpose(1, 0, 2).reshape(4 * rank, 128)
        first, second = join_cores(sum_chips(part))
        left = jnp.concatenate([first, second], axis=0).reshape(8, rank, 128).transpose(1, 0, 2)
        left = left.reshape(rank, ROWS) / replicas
        gram = lax.dot_general(left, left, (((1,), (1,)), ((), ())), precision=lax.Precision.HIGHEST)
        basis = lax.linalg.triangular_solve(jnp.linalg.cholesky(gram), left, left_side=True, lower=True)
        pbt = basis.astype(jnp.bfloat16)
        right = jnp.dot(pbt, mean, preferred_element_type=jnp.float32) / replicas
        qt = right.astype(jnp.bfloat16)
    gathered = lax.all_to_all(
        jnp.broadcast_to(right[None], (16,) + right.shape), ("y", "zl"), 0, 0, tiled=True
    )
    right = gathered.transpose(0, 2, 1).reshape(q_init.shape)
    qb = right.astype(jnp.bfloat16)
    approx = lax.dot_general(pbt, qb, (((0,), (1,)), ((), ())), preferred_element_type=jnp.float32)
    new_error = (corrected.astype(jnp.float32) - approx).astype(jnp.bfloat16)[None]
    own_rows = ROWS // 256
    start = lax.axis_index(("zl", "y", "c", "x", "zh")) * own_rows
    own = lax.dynamic_slice(basis, (0, start), (rank, own_rows)).T
    return (own * math.sqrt(ROWS), right / math.sqrt(ROWS), new_error)


def solution(mesh):
    fine = Mesh(mesh.devices.reshape(4, 4, 2, 4, 2), ("zl", "y", "c", "x", "zh"))
    dp, tensor = ("zl", "y", "c"), ("x", "zh")
    placed = (P(dp, None, tensor), P(dp, None, tensor), P(tensor, None))
    return jax.shard_map(
        shards,
        mesh=fine,
        in_specs=placed,
        out_specs=(P(dp + tensor, None), P(tensor, None), P(dp, None, tensor)),
        check_vma=False,
    )
```

time: 1560 us -> 226 us (0.14)
  waiting for transfers between devices: 1480 us -> 67.2 us
  blocking collectives: 0 us -> 63.6 us
  starting transfers between devices: 0.25 us -> 45.5 us
  matrix products: 34.4 us -> 8.1 us
    psum x6 -> x0, waiting for transfers between devices: 1480 us -> none  [the longest x3 750 us: shards(): summed = lax.psum(term.astype(jnp.bfloat16), 'dp').astype(jnp.float32)]
    all_to_all x0 -> x4, blocking collectives: none -> 63.6 us  [the longest x2 31.8 us: sum_chips(): lax.all_to_all(jnp.broadcast_to(total, value.shape), CHIPS, 0, 0, tiled=T...]
    ppermute x0 -> x11, waiting for transfers between devices: none -> 39.8 us  [the longest x6 33.2 us: exchange_sum(): total = total + lax.ppermute(piece, axis, shift(n, d)).astype(jnp.float32)]
    all_to_all x0 -> x3, waiting for transfers between devices: none -> 27.5 us  [the longest x1 10 us: sum_chips(): lax.all_to_all(jnp.broadcast_to(total, value.shape), CHIPS, 0, 0, tiled=T...]
    dot_general x10 -> x8, matrix products: 30.7 us -> 7.08 us  [the longest x1 5.48 us: shards(): lax.dot_general(pbt, qb, (((0,), (1,)), ((), ())), preferred_element_type...]
    ppermute x0 -> x11, starting transfers between devices: none -> 23 us  [the longest x4 12.3 us: join_cores(): got = lax.ppermute(value, 'c', SWAP)]
    all_to_all x0 -> x3, starting transfers between devices: none -> 22.5 us  [the longest x1 12.6 us: sum_chips(): parts = lax.all_to_all(value, CHIPS, 0, 0, tiled=True)]
  transfers between devices with their start and end apart: 6 -> 14, of which waited for: 6 -> 13; matrix products, arithmetic and copies ran while one was open for 0% -> 1% of each run, Pallas kernels for 0% -> 0%
where the time goes in v1:
time: 226 us; the launch traced here: 225 us
  waiting for transfers between devices  67.2 us (30%)
  blocking collectives  63.6 us (28%)
  starting transfers between devices  45.5 us (20%)
  other arithmetic  33.3 us (15%)
  matrix products  8.1 us (4%)
  local copies, waits for them, and re-layouts  6.53 us (3%)
    ppermute x6, waiting for transfers between devices, exchange_sum(): total = total + lax.ppermute(piece, axis, shift(n, d)).astype(jnp.float32)  33.2 us
    all_to_all x2, blocking collectives, sum_chips(): lax.all_to_all(jnp.broadcast_to(total, value.shape), CHIPS, 0, 0, tiled=T...  31.8 us
    all_to_all x2, blocking collectives, sum_chips(): parts = lax.all_to_all(value, CHIPS, 0, 0, tiled=True)  31.8 us
    all_to_all x1, starting transfers between devices, sum_chips(): parts = lax.all_to_all(value, CHIPS, 0, 0, tiled=True)  12.6 us
    ppermute x4, starting transfers between devices, join_cores(): got = lax.ppermute(value, 'c', SWAP)  12.3 us
    another operation x9, other arithmetic, shards(): jnp.linalg.cholesky(gram)  10.8 us
    all_to_all x1, waiting for transfers between devices, sum_chips(): lax.all_to_all(jnp.broadcast_to(total, value.shape), CHIPS, 0, 0, tiled=T...  10 us
    another operation x6, other arithmetic, shards(): lax.linalg.triangular_solve(jnp.linalg.cholesky(gram), left, left_side=Tr...  9.26 us
  transfers between devices with their start and end apart: 14, of which 13 were waited for; matrix products, arithmetic and copies ran while one was open for 1% of the time, Pallas kernels for 0%

profile of v1, /device:TPU:1, one launch (start us, length us, event | category | flops | bytes accessed | tf_op | source)
XLA Modules:
  0.0 225.2 jit_solution(1004747830791694803)
XLA Ops:
  0.7 7.8 %add_convert_fusion = bf16[1,1024,2048]{2,1,0:T(8,128)(2,1)} fusion(bf16[1,1024,2048]{2,1,0:T(8,128)(2,1)} %param.7, bf16[1,1024,2048]{2,1,0:T(8,128)(2,1)} %param.6), kind=kLoop, calls=%fused_computation.2 | loop fusion | flops 8388608 | bytes 12582912 | tf_op jit(solution)/shard_map/convert_element_type | solution.py:58
  8.4 1.7 dynamic-slice_bitcast_fusion
  10.2 3.3 %collective-permute-start = (bf16[512,2048]{1,0:T(8,128)(2,1)S(1)}, bf16[512,2048]{1,0:T(8,128)(2,1)}, u32[]{:S(2)}, u32[]{:S(2)}) collective-permute-start(bf16[512,2048]{1,0:T(8,128)(2,1)S(1)} %dynamic-slice_bitcast_fusion), channel_id=1, source_target_pairs={{0,8},{8,0},{1,9},{9,1},{2,10},{10,2},{3,11},{11,3},{4,12},{12,4},... | collective-permute-start | bytes 6291464 | tf_op jit(solution)/shard_map/ppermute | solution.py:35
  13.5 3.9 %collective-permute-done = bf16[512,2048]{1,0:T(8,128)(2,1)} collective-permute-done((bf16[512,2048]{1,0:T(8,128)(2,1)S(1)}, bf16[512,2048]{1,0:T(8,128)(2,1)}, u32[]{:S(2)}, u32[]{:S(2)}) %collective-permute-start) | collective-permute-done | bytes 2097184 | tf_op jit(solution)/shard_map/ppermute | solution.py:35
  17.4 3.0 %fusion.1 = bf16[512,2048]{1,0:T(8,128)(2,1)S(1)} fusion(bf16[512,2048]{1,0:T(8,128)(2,1)} %collective-permute-done, bf16[1,1024,2048]{2,1,0:T(8,128)(2,1)} %add_convert_fusion, s32[]{:T(128)S(6)} %select_n.81), kind=kLoop, calls=%fused_computation.4 | loop fusion | flops 4194304 | bytes 6291460 | tf_op jit(solution)/shard_map/convert_element_type | solution.py:36
  20.4 1.0 constant_dynamic-slice_fusion.5
  21.4 1.0 collective-permute-start.3
  22.9 1.2 collective-permute-start.1
  24.1 10.8 %collective-permute-done.3 = bf16[512,512]{1,0:T(8,128)(2,1)} collective-permute-done((bf16[512,512]{1,0:T(8,128)(2,1)}, bf16[512,512]{1,0:T(8,128)(2,1)}, u32[]{:S(2)}, u32[]{:S(2)}) %collective-permute-start.3) | collective-permute-done | bytes 524320 | tf_op jit(solution)/shard_map/ppermute | solution.py:25
  34.9 2.7 %collective-permute-done.2 = bf16[512,512]{1,0:T(8,128)(2,1)} collective-permute-done((bf16[512,512]{1,0:T(8,128)(2,1)S(1)}, bf16[512,512]{1,0:T(8,128)(2,1)}, u32[]{:S(2)}, u32[]{:S(2)}) %collective-permute-start.2) | collective-permute-done | bytes 524320 | tf_op jit(solution)/shard_map/ppermute | solution.py:25
  37.6 9.2 %collective-permute-done.1 = bf16[512,512]{1,0:T(8,128)(2,1)} collective-permute-done((bf16[512,512]{1,0:T(8,128)(2,1)S(1)}, bf16[512,512]{1,0:T(8,128)(2,1)}, u32[]{:S(2)}, u32[]{:S(2)}) %collective-permute-start.1) | collective-permute-done | bytes 524320 | tf_op jit(solution)/shard_map/ppermute | solution.py:25
  46.8 1.7 add_convert_fusion.1
  48.6 4.4 %collective-permute-start.6 = (bf16[512,128]{1,0:T(8,128)(2,1)S(1)}, bf16[512,128]{1,0:T(8,128)(2,1)S(1)}, u32[]{:S(2)}, u32[]{:S(2)}) collective-permute-start(bf16[512,128]{1,0:T(8,128)(2,1)S(1)} %get-tuple-element.21), channel_id=1, source_target_pairs={{0,192},{64,0},{128,64},{192,128},{1,193},{65,1},{129,65},{193,129... | collective-permute-start | bytes 393224 | tf_op jit(solution)/shard_map/ppermute | solution.py:25
  53.3 1.6 collective-permute-done.6
  54.9 4.6 %collective-permute-done.5 = bf16[512,128]{1,0:T(8,128)(2,1)S(1)} collective-permute-done((bf16[512,128]{1,0:T(8,128)(2,1)S(1)}, bf16[512,128]{1,0:T(8,128)(2,1)S(1)}, u32[]{:S(2)}, u32[]{:S(2)}) %collective-permute-start.5) | collective-permute-done | bytes 131104 | tf_op jit(solution)/shard_map/ppermute | solution.py:25
  59.5 4.3 %collective-permute-done.4 = bf16[512,128]{1,0:T(8,128)(2,1)S(1)} collective-permute-done((bf16[512,128]{1,0:T(8,128)(2,1)S(1)}, bf16[512,128]{1,0:T(8,128)(2,1)S(1)}, u32[]{:S(2)}, u32[]{:S(2)}) %collective-permute-start.4) | collective-permute-done | bytes 131104 | tf_op jit(solution)/shard_map/ppermute | solution.py:25
  64.0 0.7 copy.79
  64.7 12.6 %all-to-all-start = ((f32[128,1,128]{2,1,0:T(1,128)}), f32[128,1,128]{2,1,0:T(1,128)S(1)}, u32[]{:S(2)}, u32[]{:S(2)}) async-start(f32[128,1,128]{2,1,0:T(1,128)} %bitcast.4), calls=%async_computation | async-start | bytes 131072 | tf_op jit(solution)/shard_map/all_to_all | solution.py:50
  77.3 1.8 collective-permute-start.8
  79.1 8.2 %all-to-all-done = f32[128,1,128]{2,1,0:T(1,128)S(1)} async-done(((f32[128,1,128]{2,1,0:T(1,128)}), f32[128,1,128]{2,1,0:T(1,128)S(1)}, u32[]{:S(2)}, u32[]{:S(2)}) %all-to-all-start) | async-done | bytes 65568 | tf_op jit(solution)/shard_map/all_to_all | solution.py:50
  87.5 0.7 broadcast_in_dim.11
  88.2 6.3 %all-to-all-start.1 = ((f32[128,1,128]{2,1,0:T(1,128)}), f32[128,1,128]{2,1,0:T(1,128)S(1)}, u32[]{:S(2)}, u32[]{:S(2)}) async-start(f32[128,1,128]{2,1,0:T(1,128)} %broadcast_in_dim.11), calls=%async_computation.1 | async-start | bytes 131072 | tf_op jit(solution)/shard_map/all_to_all | solution.py:52
  94.5 10.0 %all-to-all-done.1 = f32[128,1,128]{2,1,0:T(1,128)S(1)} async-done(((f32[128,1,128]{2,1,0:T(1,128)}), f32[128,1,128]{2,1,0:T(1,128)S(1)}, u32[]{:S(2)}, u32[]{:S(2)}) %all-to-all-start.1) | async-done | bytes 65568 | tf_op jit(solution)/shard_map/all_to_all | solution.py:52
  104.5 4.0 %collective-permute-start.7 = (f32[128,128]{1,0:T(8,128)S(1)}, f32[128,128]{1,0:T(8,128)S(1)}, u32[]{:S(2)}, u32[]{:S(2)}) collective-permute-start(f32[128,128]{1,0:T(8,128)S(1)} %bitcast.133), channel_id=1, source_target_pairs={{0,8},{8,0},{1,9},{9,1},{2,10},{10,2},{3,11},{11,3},{4,12},{12,4},... | collective-permute-start | bytes 196616 | tf_op jit(solution)/shard_map/ppermute | solution.py:43
  108.6 0.9 collective-permute-done.7
  109.8 2.9 %cholesky.59 = f32[32,32]{1,0:T(8,128)S(1)} custom-call(f32[32,32]{1,0:T(8,128)S(1)} %fusion.24), custom_call_target="Cholesky" | custom-call | tf_op jit(solution)/shard_map/jit(cholesky)/cholesky | solution.py:71
  113.4 0.7 fusion.16
  114.1 2.4 %custom-call.7 = f32[1,32,32]{1,2,0:T(8,128)S(1)} custom-call(f32[1,32,32]{2,1,0:T(8,128)S(1)} %fusion.16), custom_call_target="InvertDiagBlocksLowerTriangular" | custom-call | tf_op jit(solution)/shard_map/triangular_solve/custom-call.0 | solution.py:71
  117.2 15.9 %all_to_all.59 = f32[128,1,128]{2,1,0:T(1,128)S(1)} all-to-all(f32[128,1,128]{2,1,0:T(1,128)S(1)} %bitcast.131), channel_id=1, replica_groups=mesh['zl'=4,'y'=4,'c'=2,'x'=4,'zh'=2] {'zl','y','x','zh'}, dimensions={0} | all-to-all | bytes 131072 | tf_op jit(solution)/shard_map/all_to_all | solution.py:50
  133.3 15.9 %all_to_all.60 = f32[128,1,128]{2,1,0:T(1,128)S(1)} all-to-all(f32[128,1,128]{2,1,0:T(1,128)S(1)} %broadcast_in_dim.12), channel_id=1, replica_groups=mesh['zl'=4,'y'=4,'c'=2,'x'=4,'zh'=2] {'zl','y','x','zh'}, dimensions={0} | all-to-all | bytes 131072 | tf_op jit(solution)/shard_map/all_to_all | solution.py:52
  149.2 3.2 %collective-permute-start.9 = (f32[128,128]{1,0:T(8,128)S(1)}, f32[128,128]{1,0:T(8,128)S(1)}, u32[]{:S(2)}, u32[]{:S(2)}) collective-permute-start(f32[128,128]{1,0:T(8,128)S(1)} %bitcast.137), channel_id=1, source_target_pairs={{0,8},{8,0},{1,9},{9,1},{2,10},{10,2},{3,11},{11,3},{4,12},{12,4},... | collective-permute-start | bytes 196616 | tf_op jit(solution)/shard_map/ppermute | solution.py:43
  152.4 0.9 collective-permute-done.9
  153.7 2.9 %cholesky.70 = f32[32,32]{1,0:T(8,128)S(1)} custom-call(f32[32,32]{1,0:T(8,128)S(1)} %fusion.22), custom_call_target="Cholesky" | custom-call | tf_op jit(solution)/shard_map/jit(cholesky)/cholesky | solution.py:71
  157.3 0.7 fusion.17
  157.9 2.4 %custom-call.8 = f32[1,32,32]{1,2,0:T(8,128)S(1)} custom-call(f32[1,32,32]{2,1,0:T(8,128)S(1)} %fusion.17), custom_call_target="InvertDiagBlocksLowerTriangular" | custom-call | tf_op jit(solution)/shard_map/triangular_solve/custom-call.0 | solution.py:71
  161.0 15.9 %all_to_all.61 = f32[128,1,128]{2,1,0:T(1,128)S(1)} all-to-all(f32[128,1,128]{2,1,0:T(1,128)S(1)} %bitcast.132), channel_id=1, replica_groups=mesh['zl'=4,'y'=4,'c'=2,'x'=4,'zh'=2] {'zl','y','x','zh'}, dimensions={0} | all-to-all | bytes 131072 | tf_op jit(solution)/shard_map/all_to_all | solution.py:50
  177.1 15.9 %all_to_all.62 = f32[128,1,128]{2,1,0:T(1,128)S(1)} all-to-all(f32[128,1,128]{2,1,0:T(1,128)S(1)} %broadcast_in_dim.13), channel_id=1, replica_groups=mesh['zl'=4,'y'=4,'c'=2,'x'=4,'zh'=2] {'zl','y','x','zh'}, dimensions={0} | all-to-all | bytes 131072 | tf_op jit(solution)/shard_map/all_to_all | solution.py:52
  193.0 3.2 %collective-permute-start.10 = (f32[128,128]{1,0:T(8,128)S(1)}, f32[128,128]{1,0:T(8,128)S(1)}, u32[]{:S(2)}, u32[]{:S(2)}) collective-permute-start(f32[128,128]{1,0:T(8,128)S(1)} %bitcast.135), channel_id=1, source_target_pairs={{0,8},{8,0},{1,9},{9,1},{2,10},{10,2},{3,11},{11,3},{4,12},{12,4},... | collective-permute-start | bytes 196616 | tf_op jit(solution)/shard_map/ppermute | solution.py:43
  196.2 0.9 collective-permute-done.10
  197.5 2.9 %cholesky.81 = f32[32,32]{1,0:T(8,128)S(1)} custom-call(f32[32,32]{1,0:T(8,128)S(1)} %fusion.20), custom_call_target="Cholesky" | custom-call | tf_op jit(solution)/shard_map/jit(cholesky)/cholesky | solution.py:71
  201.1 0.7 fusion.18
  201.7 2.4 %custom-call.9 = f32[1,32,32]{1,2,0:T(8,128)S(1)} custom-call(f32[1,32,32]{2,1,0:T(8,128)S(1)} %fusion.18), custom_call_target="InvertDiagBlocksLowerTriangular" | custom-call | tf_op jit(solution)/shard_map/triangular_solve/custom-call.0 | solution.py:71
  204.7 0.7 broadcast_in_dim.14
  205.4 3.5 %all-to-all-start.6 = ((f32[16,32,128]{2,1,0:T(8,128)}), f32[16,32,128]{2,1,0:T(8,128)S(1)}, u32[]{:S(2)}, u32[]{:S(2)}) async-start(f32[16,32,128]{2,1,0:T(8,128)} %broadcast_in_dim.14), calls=%async_computation.6 | async-start | bytes 524288 | tf_op jit(solution)/shard_map/all_to_all | solution.py:75
  209.1 0.7 copy.47
  209.7 9.2 %all-to-all-done.6 = f32[16,32,128]{2,1,0:T(8,128)S(1)} async-done(((f32[16,32,128]{2,1,0:T(8,128)}), f32[16,32,128]{2,1,0:T(8,128)S(1)}, u32[]{:S(2)}, u32[]{:S(2)}) %all-to-all-start.6) | async-done | bytes 262176 | tf_op jit(solution)/shard_map/all_to_all | solution.py:75
  219.0 0.7 copy.76
  219.7 5.5 %fusion.2 = bf16[1,1024,2048]{2,1,0:T(8,128)(2,1)} fusion(bf16[1,1024,2048]{2,1,0:T(8,128)(2,1)} %add_convert_fusion, bf16[16,4,8,128]{3,2,1,0:T(8,128)(2,1)S(1)} %get-tuple-element.23, f32[32,1024]{1,0:T(8,128)S(1)} %fusion.7), kind=kOutput, calls=%fused_computation.5 | convolution fusion | flops 140541952 | bytes 8650752 | tf_op jit(solution)/shard_map/dot_general | solution.py:80
  (46 shorter events, 6.7 us)
Async XLA Ops:
  0.6 63.2 %copy-start = (bf16[2048,32]{0,1:T(8,128)(2,1)S(1)}, bf16[2048,32]{0,1:T(8,128)(2,1)}, u32[]{:S(2)}) copy-start(bf16[2048,32]{0,1:T(8,128)(2,1)} %param.8) | copy-start | bytes 393220
  10.2 7.2 %collective-permute-start = (bf16[512,2048]{1,0:T(8,128)(2,1)S(1)}, bf16[512,2048]{1,0:T(8,128)(2,1)}, u32[]{:S(2)}, u32[]{:S(2)}) collective-permute-start(bf16[512,2048]{1,0:T(8,128)(2,1)S(1)} %dynamic-slice_bitcast_fusion), channel_id=1, source_target_pairs={{0,8},{8,0},{1,9},{9,1},{2,10},{10,2},{3,11},{11,3},{4,12},{12,4},... | collective-permute-start | bytes 6291464 | tf_op jit(solution)/shard_map/ppermute | solution.py:35
  21.4 13.5 %collective-permute-start.3 = (bf16[512,512]{1,0:T(8,128)(2,1)}, bf16[512,512]{1,0:T(8,128)(2,1)}, u32[]{:S(2)}, u32[]{:S(2)}) collective-permute-start(bf16[512,512]{1,0:T(8,128)(2,1)} %get-tuple-element.18), channel_id=1, source_target_pairs={{0,48},{16,0},{32,16},{48,32},{1,49},{17,1},{33,17},{49,33},{2,50}... | collective-permute-start | bytes 1572872 | tf_op jit(solution)/shard_map/ppermute | solution.py:25
  22.4 15.2 %collective-permute-start.2 = (bf16[512,512]{1,0:T(8,128)(2,1)S(1)}, bf16[512,512]{1,0:T(8,128)(2,1)}, u32[]{:S(2)}, u32[]{:S(2)}) collective-permute-start(bf16[512,512]{1,0:T(8,128)(2,1)S(1)} %get-tuple-element.19), channel_id=1, source_target_pairs={{0,16},{16,32},{32,48},{48,0},{1,17},{17,33},{33,49},{49,1},{2,18}... | collective-permute-start | bytes 1572872 | tf_op jit(solution)/shard_map/ppermute | solution.py:25
  22.9 23.9 %collective-permute-start.1 = (bf16[512,512]{1,0:T(8,128)(2,1)S(1)}, bf16[512,512]{1,0:T(8,128)(2,1)}, u32[]{:S(2)}, u32[]{:S(2)}) collective-permute-start(bf16[512,512]{1,0:T(8,128)(2,1)S(1)} %get-tuple-element.17), channel_id=1, source_target_pairs={{0,32},{16,48},{32,0},{48,16},{1,33},{17,49},{33,1},{49,17},{2,34}... | collective-permute-start | bytes 1572872 | tf_op jit(solution)/shard_map/ppermute | solution.py:25
  48.6 6.4 %collective-permute-start.6 = (bf16[512,128]{1,0:T(8,128)(2,1)S(1)}, bf16[512,128]{1,0:T(8,128)(2,1)S(1)}, u32[]{:S(2)}, u32[]{:S(2)}) collective-permute-start(bf16[512,128]{1,0:T(8,128)(2,1)S(1)} %get-tuple-element.21), channel_id=1, source_target_pairs={{0,192},{64,0},{128,64},{192,128},{1,193},{65,1},{129,65},{193,129... | collective-permute-start | bytes 393224 | tf_op jit(solution)/shard_map/ppermute | solution.py:25
  53.0 6.6 %collective-permute-start.5 = (bf16[512,128]{1,0:T(8,128)(2,1)S(1)}, bf16[512,128]{1,0:T(8,128)(2,1)S(1)}, u32[]{:S(2)}, u32[]{:S(2)}) collective-permute-start(bf16[512,128]{1,0:T(8,128)(2,1)S(1)} %get-tuple-element.22), channel_id=1, source_target_pairs={{0,64},{64,128},{128,192},{192,0},{1,65},{65,129},{129,193},{193,1... | collective-permute-start | bytes 393224 | tf_op jit(solution)/shard_map/ppermute | solution.py:25
  53.0 10.8 %collective-permute-start.4 = (bf16[512,128]{1,0:T(8,128)(2,1)S(1)}, bf16[512,128]{1,0:T(8,128)(2,1)S(1)}, u32[]{:S(2)}, u32[]{:S(2)}) collective-permute-start(bf16[512,128]{1,0:T(8,128)(2,1)S(1)} %get-tuple-element.20), channel_id=1, source_target_pairs={{0,128},{64,192},{128,0},{192,64},{1,129},{65,193},{129,1},{193,65... | collective-permute-start | bytes 393224 | tf_op jit(solution)/shard_map/ppermute | solution.py:25
  64.7 22.7 %all-to-all-start = ((f32[128,1,128]{2,1,0:T(1,128)}), f32[128,1,128]{2,1,0:T(1,128)S(1)}, u32[]{:S(2)}, u32[]{:S(2)}) async-start(f32[128,1,128]{2,1,0:T(1,128)} %bitcast.4), calls=%async_computation | async-start | bytes 131072 | tf_op jit(solution)/shard_map/all_to_all | solution.py:50
  77.3 31.3 %collective-permute-start.8 = (bf16[512,128]{1,0:T(8,128)(2,1)S(1)}, bf16[512,128]{1,0:T(8,128)(2,1)S(1)}, u32[]{:S(2)}, u32[]{:S(2)}) collective-permute-start(bf16[512,128]{1,0:T(8,128)(2,1)S(1)} %add_convert_fusion.2), channel_id=1, source_target_pairs={{0,8},{8,0},{1,9},{9,1},{2,10},{10,2},{3,11},{11,3},{4,12},{12,4},... | collective-permute-start | bytes 393224 | tf_op jit(solution)/shard_map/ppermute | solution.py:43
  88.2 16.4 %all-to-all-start.1 = ((f32[128,1,128]{2,1,0:T(1,128)}), f32[128,1,128]{2,1,0:T(1,128)S(1)}, u32[]{:S(2)}, u32[]{:S(2)}) async-start(f32[128,1,128]{2,1,0:T(1,128)} %broadcast_in_dim.11), calls=%async_computation.1 | async-start | bytes 131072 | tf_op jit(solution)/shard_map/all_to_all | solution.py:52
  104.5 4.9 %collective-permute-start.7 = (f32[128,128]{1,0:T(8,128)S(1)}, f32[128,128]{1,0:T(8,128)S(1)}, u32[]{:S(2)}, u32[]{:S(2)}) collective-permute-start(f32[128,128]{1,0:T(8,128)S(1)} %bitcast.133), channel_id=1, source_target_pairs={{0,8},{8,0},{1,9},{9,1},{2,10},{10,2},{3,11},{11,3},{4,12},{12,4},... | collective-permute-start | bytes 196616 | tf_op jit(solution)/shard_map/ppermute | solution.py:43
  149.2 4.1 %collective-permute-start.9 = (f32[128,128]{1,0:T(8,128)S(1)}, f32[128,128]{1,0:T(8,128)S(1)}, u32[]{:S(2)}, u32[]{:S(2)}) collective-permute-start(f32[128,128]{1,0:T(8,128)S(1)} %bitcast.137), channel_id=1, source_target_pairs={{0,8},{8,0},{1,9},{9,1},{2,10},{10,2},{3,11},{11,3},{4,12},{12,4},... | collective-permute-start | bytes 196616 | tf_op jit(solution)/shard_map/ppermute | solution.py:43
  193.0 4.1 %collective-permute-start.10 = (f32[128,128]{1,0:T(8,128)S(1)}, f32[128,128]{1,0:T(8,128)S(1)}, u32[]{:S(2)}, u32[]{:S(2)}) collective-permute-start(f32[128,128]{1,0:T(8,128)S(1)} %bitcast.135), channel_id=1, source_target_pairs={{0,8},{8,0},{1,9},{9,1},{2,10},{10,2},{3,11},{11,3},{4,12},{12,4},... | collective-permute-start | bytes 196616 | tf_op jit(solution)/shard_map/ppermute | solution.py:43
  205.4 13.5 %all-to-all-start.6 = ((f32[16,32,128]{2,1,0:T(8,128)}), f32[16,32,128]{2,1,0:T(8,128)S(1)}, u32[]{:S(2)}, u32[]{:S(2)}) async-start(f32[16,32,128]{2,1,0:T(8,128)} %broadcast_in_dim.14), calls=%async_computation.6 | async-start | bytes 524288 | tf_op jit(solution)/shard_map/all_to_all | solution.py:75

commit v2 on v1

v2 whole, which is shorter than its diff:
```python
import functools
import math

import jax
import jax.numpy as jnp
import numpy as np
from jax import lax
from jax.experimental import pallas as pl
from jax.experimental.pallas import tpu as pltpu
from jax.sharding import Mesh, PartitionSpec as P

ROWS = 1024
RANK = 32
ITERS = 3
REPLICAS = 32
HEAD = 384
SWAP = [(0, 1), (1, 0)]
CHIPS = ("zl", "y", "x", "zh")
HOLDERS = 128
TILE = 128
SIDE = ROWS // TILE
UPPER = [(i, j) for i in range(SIDE) for j in range(i, SIDE)]
SHARE = len(UPPER) // 2
SLOTS = SHARE + 1
TABLE = np.array([UPPER[:SHARE], UPPER[SHARE:]], np.int32)
VMEM = 40 * 1024 * 1024


def shift(n, d):
    return [(i, (i + d) % n) for i in range(n)]


def exchange_sum(axis, piece):
    n = lax.axis_size(axis)
    me = lax.axis_index(axis)
    total = piece(me).astype(jnp.float32)
    for d in (2, 1, 3):
        sent = piece(lax.rem(me + d, n)).astype(jnp.bfloat16)
        total = total + lax.ppermute(sent, axis, shift(n, d)).astype(jnp.float32)
    return total


def columns(value, start, width):
    return lax.dynamic_slice(value, (0, start), (value.shape[0], width))


def reduce_replicas(grad, error):
    core = lax.axis_index("c")
    total_rows, cols = grad.shape
    half = total_rows // 2
    wide, narrow = cols // 4, cols // 16

    def corrected(start, rows):
        parts = (lax.dynamic_slice(a, (start, 0), (rows, cols)).astype(jnp.float32) for a in (grad, error))
        return sum(parts).astype(jnp.bfloat16)

    def pair(offset, rows):
        got = lax.ppermute(corrected((1 - core) * half + offset, rows), "c", SWAP)
        own = corrected(core * half + offset, rows)
        return own.astype(jnp.float32) + got.astype(jnp.float32)

    tail = pair(HEAD, half - HEAD)
    head = pair(0, HEAD)
    tail = exchange_sum(
        "zl",
        lambda i: jnp.concatenate([columns(tail, j * wide + i * narrow, narrow) for j in range(4)], axis=1),
    )
    head = exchange_sum("y", lambda i: columns(head, i * wide, wide))
    tail = exchange_sum("y", lambda i: columns(tail, i * narrow, narrow))
    head = exchange_sum("zl", lambda i: columns(head, i * narrow, narrow))
    return jnp.concatenate([head, tail], axis=0).astype(jnp.bfloat16)


def join_cores(value):
    core = lax.axis_index("c")
    got = lax.ppermute(value, "c", SWAP)
    return jnp.where(core == 0, value, got), jnp.where(core == 0, got, value)


def dot(a, b, contract, precision=None):
    return lax.dot_general(
        a, b, (contract, ((), ())), precision=precision, preferred_element_type=jnp.float32
    )


def pack_kernel(table, core, total_ref, qt_ref, out_ref):
    def rows(index):
        return total_ref[pl.ds(pl.multiple_of(index * TILE, TILE), TILE), :]

    for k in range(SHARE):
        block = dot(rows(table[k, 0]), rows(table[k, 1]), ((1,), (1,)))
        out_ref[pl.ds(k, TILE, stride=SLOTS), :] = block
    half = ROWS // 2
    for b in range(half // TILE):
        part = dot(qt_ref[...], rows(core[0] * (half // TILE) + b), ((1,), (1,)))
        out_ref[pl.ds(b * RANK * SLOTS + SHARE, RANK, stride=SLOTS), :] = part


def pack(table, core, total, qt):
    return pl.pallas_call(
        pack_kernel,
        out_shape=jax.ShapeDtypeStruct((HOLDERS * SLOTS, TILE), jnp.float32),
        in_specs=[
            pl.BlockSpec(memory_space=pltpu.SMEM),
            pl.BlockSpec(memory_space=pltpu.SMEM),
            pl.BlockSpec(memory_space=pltpu.VMEM),
            pl.BlockSpec(memory_space=pltpu.VMEM),
        ],
        out_specs=pl.BlockSpec(memory_space=pltpu.VMEM),
        compiler_params=pltpu.CompilerParams(vmem_limit_bytes=VMEM),
    )(table, core, total, qt)


def sum_kernel(parts_ref, out_ref):
    for k in range(SLOTS):
        row = jnp.sum(parts_ref[pl.ds(k, HOLDERS, stride=SLOTS), :], axis=0, keepdims=True)
        out_ref[pl.ds(k, HOLDERS, stride=SLOTS), :] = jnp.broadcast_to(row, (HOLDERS, TILE))


def sum_parts(parts):
    return pl.pallas_call(
        sum_kernel,
        out_shape=jax.ShapeDtypeStruct(parts.shape, jnp.float32),
        in_specs=[pl.BlockSpec(memory_space=pltpu.VMEM)],
        out_specs=pl.BlockSpec(memory_space=pltpu.VMEM),
        compiler_params=pltpu.CompilerParams(vmem_limit_bytes=VMEM),
    )(parts)


def inverse_factor(gram):
    shape = (RANK, 2 * RANK)
    row = lax.broadcasted_iota(jnp.int32, shape, 0)
    lane = lax.broadcasted_iota(jnp.int32, shape, 1)
    eye = jnp.where(lane == row + RANK, 1.0, 0.0).astype(jnp.float32)
    work = jnp.concatenate([gram, eye[:, RANK:]], axis=1)
    for j in range(RANK):
        scale = lax.rsqrt(work[j : j + 1, j : j + 1])
        pivot = work[j : j + 1, :] * scale
        column = work[:, j : j + 1] * scale
        work = jnp.where(row > j, work - column * pivot, jnp.where(row == j, pivot, work))
    return work[:, RANK:]


def iterate_kernel(core, own_table, other_table, own_ref, other_ref, total_ref, basis_ref, right_ref, high, low, left_ref):
    half = ROWS // 2
    high_scale = 1.0 / REPLICAS**2
    for table, blocks, place in ((own_table, own_ref, core[0]), (other_table, other_ref, 1 - core[0])):
        for k in range(SHARE):
            i = pl.ds(pl.multiple_of(table[k, 0] * TILE, TILE), TILE)
            j = pl.ds(pl.multiple_of(table[k, 1] * TILE, TILE), TILE)
            block = blocks[pl.ds(k, TILE, stride=SLOTS), :] * high_scale
            for at, value in (((i, j), block), ((j, i), block.T)):
                top = value.astype(jnp.bfloat16)
                high[at] = top
                low[at] = (value - top.astype(jnp.float32)).astype(jnp.bfloat16)
        for b in range(half // TILE):
            at = pl.ds(pl.multiple_of(place * half + b * TILE, TILE), TILE)
            left_ref[:, at] = blocks[pl.ds(b * RANK * SLOTS + SHARE, RANK, stride=SLOTS), :] / REPLICAS
    for step in range(ITERS):
        left = left_ref[...]
        gram = dot(left, left, ((1,), (1,)), lax.Precision.HIGHEST)
        basis = dot(inverse_factor(gram), left, ((1,), (0,)), lax.Precision.HIGHEST)
        pbt = basis.astype(jnp.bfloat16)
        if step < ITERS - 1:
            left_ref[...] = dot(pbt, high[...], ((1,), (0,))) + dot(pbt, low[...], ((1,), (0,)))
    basis_ref[...] = basis
    right_ref[...] = dot(pbt, total_ref[...], ((1,), (0,))) / REPLICAS


def iterate(core, own_table, other_table, own, other, total):
    smem = pl.BlockSpec(memory_space=pltpu.SMEM)
    vmem = pl.BlockSpec(memory_space=pltpu.VMEM)
    return pl.pallas_call(
        iterate_kernel,
        out_shape=(
            jax.ShapeDtypeStruct((RANK, ROWS), jnp.float32),
            jax.ShapeDtypeStruct((RANK, TILE), jnp.float32),
        ),
        in_specs=[smem] * 3 + [vmem] * 3,
        out_specs=(vmem, vmem),
        scratch_shapes=[
            pltpu.VMEM((ROWS, ROWS), jnp.bfloat16),
            pltpu.VMEM((ROWS, ROWS), jnp.bfloat16),
            pltpu.VMEM((RANK, ROWS), jnp.float32),
        ],
        compiler_params=pltpu.CompilerParams(vmem_limit_bytes=VMEM),
    )(core, own_table, other_table, own, other, total)


def over_chips(value):
    value = value.reshape(HOLDERS, SLOTS, 1, TILE)
    return lax.all_to_all(value, CHIPS, 0, 0, tiled=True).reshape(HOLDERS * SLOTS, TILE)


def shards(grad, error, q_init):
    core, y, zl = (lax.axis_index(a) for a in ("c", "y", "zl"))
    mine = reduce_replicas(grad[0], error[0])
    width = mine.shape[1]
    total = jnp.concatenate(join_cores(mine), axis=0)
    qt = lax.dynamic_slice(q_init, ((y * 4 + zl) * width, 0), (width, RANK)).T
    table = jnp.asarray(TABLE)
    own_table = lax.dynamic_index_in_dim(table, core, 0, False)
    other_table = lax.dynamic_index_in_dim(table, 1 - core, 0, False)
    which = core.reshape(1)
    own = over_chips(sum_parts(over_chips(pack(own_table, which, total, qt))))
    other = lax.ppermute(own, "c", SWAP)
    basis, right = iterate(which, own_table, other_table, own, other, total)
    pbt = basis.astype(jnp.bfloat16)
    gathered = lax.all_to_all(
        jnp.broadcast_to(right[None], (16,) + right.shape), ("y", "zl"), 0, 0, tiled=True
    )
    right = gathered.transpose(0, 2, 1).reshape(q_init.shape)
    qb = right.astype(jnp.bfloat16)
    approx = dot(pbt, qb, ((0,), (1,)))
    corrected = (grad[0].astype(jnp.float32) + error[0].astype(jnp.float32)).astype(jnp.bfloat16)
    new_error = (corrected.astype(jnp.float32) - approx).astype(jnp.bfloat16)[None]
    own_rows = ROWS // 256
    start = lax.axis_index(("zl", "y", "c", "x", "zh")) * own_rows
    own_basis = lax.dynamic_slice(basis, (0, start), (RANK, own_rows)).T
    return (own_basis * math.sqrt(ROWS), right / math.sqrt(ROWS), new_error)


def solution(mesh):
    fine = Mesh(mesh.devices.reshape(4, 4, 2, 4, 2), ("zl", "y", "c", "x", "zh"))
    dp, tensor = ("zl", "y", "c"), ("x", "zh")
    placed = (P(dp, None, tensor), P(dp, None, tensor), P(tensor, None))
    return jax.shard_map(
        shards,
        mesh=fine,
        in_specs=placed,
        out_specs=(P(dp + tensor, None), P(tensor, None), P(dp, None, tensor)),
        check_vma=False,
    )
```

time: 226 us -> 182 us (0.81)
  waiting for transfers between devices: 67.2 us -> 32.2 us
  other arithmetic: 33.3 us -> 9.47 us
  blocking collectives: 63.6 us -> 84.3 us
  starting transfers between devices: 45.5 us -> 31 us
  Pallas kernels: 0 us -> 14.1 us
  local copies, waits for them, and re-layouts: 6.53 us -> 2.79 us
    all_to_all x4 -> x2, blocking collectives: 63.6 us -> 84.3 us  [over_chips(): lax.all_to_all(value, CHIPS, 0, 0, tiled=True)]
    another operation x15 -> x2, other arithmetic: 20 us -> 0.08 us  [the longest x9 10.8 us: shards(): jnp.linalg.cholesky(gram)]
    all_to_all x2 -> x0, starting transfers between devices: 19 us -> none  [the longest x1 12.6 us: sum_chips(): parts = lax.all_to_all(value, CHIPS, 0, 0, tiled=True)]
    all_to_all x2 -> x0, waiting for transfers between devices: 18.3 us -> none  [the longest x1 10 us: sum_chips(): lax.all_to_all(jnp.broadcast_to(total, value.shape), CHIPS, 0, 0, tiled=T...]
    ppermute x7 -> x15, starting transfers between devices: 10.8 us -> 25.9 us  [the longest x12 17.7 us: exchange_sum(): total = total + lax.ppermute(sent, axis, shift(n, d)).astype(jnp.float32)]
    ppermute x7 -> x15, waiting for transfers between devices: 37.1 us -> 22.1 us  [the longest x12 17.4 us: exchange_sum(): total = total + lax.ppermute(sent, axis, shift(n, d)).astype(jnp.float32)]
    pallas_call x0 -> x3, Pallas kernels: none -> 14.1 us  [the longest x1 12.7 us: iterate(): pl.pallas_call(iterate_kernel, out_shape=(jax.ShapeDtypeStruct((RANK, ROW...]
    ppermute x4 -> x1, starting transfers between devices: 12.3 us -> 1.63 us  [join_cores(): got = lax.ppermute(value, 'c', SWAP)]
  transfers between devices with their start and end apart: 14 -> 17, of which waited for: 13 -> 8; matrix products, arithmetic and copies ran while one was open for 1% -> 4% of each run, Pallas kernels for 0% -> 0%
where the time goes in v2:
time: 182 us
  blocking collectives  84.3 us (46%)
  waiting for transfers between devices  32.2 us (18%)
  starting transfers between devices  31 us (17%)
  Pallas kernels  14.1 us (8%)
  other arithmetic  9.47 us (5%)
  matrix products  6.85 us (4%)
  local copies, waits for them, and re-layouts  2.79 us (2%)
    all_to_all x2, blocking collectives, over_chips(): lax.all_to_all(value, CHIPS, 0, 0, tiled=True)  84.3 us
    ppermute x12, starting transfers between devices, exchange_sum(): total = total + lax.ppermute(sent, axis, shift(n, d)).astype(jnp.float32)  17.7 us
    ppermute x12, waiting for transfers between devices, exchange_sum(): total = total + lax.ppermute(sent, axis, shift(n, d)).astype(jnp.float32)  17.4 us
    pallas_call x1, Pallas kernels, iterate(): pl.pallas_call(iterate_kernel, out_shape=(jax.ShapeDtypeStruct((RANK, ROW...  12.7 us
    all_to_all x1, waiting for transfers between devices, shards(): lax.all_to_all(jnp.broadcast_to(right[None], (16,) + right.shape), ('y',...  9.2 us
    dot_general x1, matrix products, dot(): lax.dot_general(a, b, (contract, ((), ())), precision=precision, preferre...  6.85 us
    ppermute x1, starting transfers between devices, shards(): other = lax.ppermute(own, 'c', SWAP)  4.8 us
    convert_element_type x2, other arithmetic, corrected(): return sum(parts).astype(jnp.bfloat16)  4.64 us
  transfers between devices with their start and end apart: 17, of which 8 were waited for; matrix products, arithmetic and copies ran while one was open for 4% of the time, Pallas kernels for 0%

profile of v2, /device:TPU:1, one launch (start us, length us, event | category | flops | bytes accessed | tf_op | source)
XLA Modules:
  0.0 181.6 jit_solution(3714377067174065145)
XLA Ops:
  0.7 2.5 %fusion.4 = bf16[384,2048]{1,0:T(8,128)(2,1)S(1)} fusion(bf16[1,1024,2048]{2,1,0:T(8,128)(2,1)} %param.5, s32[]{:T(128)S(6)} %select_n.129, bf16[1,1024,2048]{2,1,0:T(8,128)(2,1)} %param.4), kind=kLoop, calls=%fused_computation.9 | loop fusion | flops 3145728 | bytes 4718596 | tf_op jit(solution)/shard_map/convert_element_type | solution.py:55
  3.2 3.3 %collective-permute-start = (bf16[384,2048]{1,0:T(8,128)(2,1)S(1)}, bf16[384,2048]{1,0:T(8,128)(2,1)S(1)}, u32[]{:S(2)}, u32[]{:S(2)}) collective-permute-start(bf16[384,2048]{1,0:T(8,128)(2,1)S(1)} %fusion.4), channel_id=1, source_target_pairs={{0,8},{8,0},{1,9},{9,1},{2,10},{10,2},{3,11},{11,3},{4,12},{12,4},... | collective-permute-start | bytes 4718600 | tf_op jit(solution)/shard_map/ppermute | solution.py:58
  6.5 2.1 %fusion.6 = bf16[128,2048]{1,0:T(8,128)(2,1)} fusion(bf16[1,1024,2048]{2,1,0:T(8,128)(2,1)} %param.5, s32[]{:T(128)S(6)} %select_n.139, bf16[1,1024,2048]{2,1,0:T(8,128)(2,1)} %param.4), kind=kLoop, calls=%fused_computation.18 | loop fusion | flops 1048576 | bytes 1572868 | tf_op jit(solution)/shard_map/convert_element_type | solution.py:55
  8.6 0.0 collective-permute-start.7
  8.7 2.2 %collective-permute-done.7 = bf16[128,2048]{1,0:T(8,128)(2,1)} collective-permute-done((bf16[128,2048]{1,0:T(8,128)(2,1)}, bf16[128,2048]{1,0:T(8,128)(2,1)}, u32[]{:S(2)}, u32[]{:S(2)}) %collective-permute-start.7) | collective-permute-done | bytes 524320 | tf_op jit(solution)/shard_map/ppermute | solution.py:58
  10.9 1.6 convert_add_fusion.1
  12.5 0.1 dynamic-slice_convert_fusion.20
  12.6 1.3 collective-permute-start.8
  14.0 1.7 collective-permute-start.9
  15.7 1.7 collective-permute-start.10
  17.4 2.7 %convert_add_fusion = f32[384,2048]{1,0:T(8,128)S(1)} fusion(bf16[384,2048]{1,0:T(8,128)(2,1)S(1)} %collective-permute-done, bf16[1,1024,2048]{2,1,0:T(8,128)(2,1)} %param.5, s32[]{:T(128)S(6)} %select_n.128, bf16[1,1024,2048]{2,1,0:T(8,128)(2,1)} %param.4), kind=kLoop, calls=%fused_computation.5 | loop fusion | flops 5505024 | bytes 7864324 | tf_op jit(solution)/shard_map/add | solution.py:60
  20.1 0.2 dynamic-slice_convert_fusion.2
  20.3 3.0 %collective-permute-start.1 = (bf16[384,512]{1,0:T(8,128)(2,1)S(1)}, bf16[384,512]{1,0:T(8,128)(2,1)S(1)}, u32[]{:S(2)}, u32[]{:S(2)}) collective-permute-start(bf16[384,512]{1,0:T(8,128)(2,1)S(1)} %get-tuple-element.19), channel_id=1, source_target_pairs={{0,32},{16,48},{32,0},{48,16},{1,33},{17,49},{33,1},{49,17},{2,34}... | collective-permute-start | bytes 1179656 | tf_op jit(solution)/shard_map/ppermute | solution.py:39
  23.3 0.4 collective-permute-start.2
  23.7 0.8 collective-permute-done.8
  24.5 1.6 collective-permute-start.3
  26.2 0.1 fusion.8
  26.3 1.4 collective-permute-start.11
  27.6 0.4 collective-permute-start.12
  28.0 3.5 %collective-permute-done.1 = bf16[384,512]{1,0:T(8,128)(2,1)S(1)} collective-permute-done((bf16[384,512]{1,0:T(8,128)(2,1)S(1)}, bf16[384,512]{1,0:T(8,128)(2,1)S(1)}, u32[]{:S(2)}, u32[]{:S(2)}) %collective-permute-start.1) | collective-permute-done | bytes 393248 | tf_op jit(solution)/shard_map/ppermute | solution.py:39
  31.5 2.7 %collective-permute-start.13 = (bf16[128,128]{1,0:T(8,128)(2,1)S(1)}, bf16[128,128]{1,0:T(8,128)(2,1)S(1)}, u32[]{:S(2)}, u32[]{:S(2)}) collective-permute-start(bf16[128,128]{1,0:T(8,128)(2,1)S(1)} %get-tuple-element.46), channel_id=1, source_target_pairs={{0,48},{16,0},{32,16},{48,32},{1,49},{17,1},{33,17},{49,33},{2,50}... | collective-permute-start | bytes 98312 | tf_op jit(solution)/shard_map/ppermute | solution.py:39
  34.3 7.4 %collective-permute-done.2 = bf16[384,512]{1,0:T(8,128)(2,1)S(1)} collective-permute-done((bf16[384,512]{1,0:T(8,128)(2,1)S(1)}, bf16[384,512]{1,0:T(8,128)(2,1)S(1)}, u32[]{:S(2)}, u32[]{:S(2)}) %collective-permute-start.2) | collective-permute-done | bytes 393248 | tf_op jit(solution)/shard_map/ppermute | solution.py:39
  41.7 0.2 convert_add_fusion.2
  41.9 0.1 dynamic-slice_convert_fusion.5
  42.0 0.1 collective-permute-start.4
  42.1 0.3 collective-permute-start.5
  42.4 3.0 %collective-permute-start.6 = (bf16[384,128]{1,0:T(8,128)(2,1)S(1)}, bf16[384,128]{1,0:T(8,128)(2,1)S(1)}, u32[]{:S(2)}, u32[]{:S(2)}) collective-permute-start(bf16[384,128]{1,0:T(8,128)(2,1)S(1)} %get-tuple-element.39), channel_id=1, source_target_pairs={{0,192},{64,0},{128,64},{192,128},{1,193},{65,1},{129,65},{193,129... | collective-permute-start | bytes 294920 | tf_op jit(solution)/shard_map/ppermute | solution.py:39
  45.5 5.6 %collective-permute-done.4 = bf16[384,128]{1,0:T(8,128)(2,1)S(1)} collective-permute-done((bf16[384,128]{1,0:T(8,128)(2,1)S(1)}, bf16[384,128]{1,0:T(8,128)(2,1)S(1)}, u32[]{:S(2)}, u32[]{:S(2)}) %collective-permute-start.4) | collective-permute-done | bytes 98336 | tf_op jit(solution)/shard_map/ppermute | solution.py:39
  51.1 0.1 add_convert_fusion.5
  51.2 1.6 collective-permute-start.14
  52.8 0.1 copy.24.table.own_table
  53.0 0.9 collective-permute-done.14
  53.8 0.1 broadcast_select_fusion.1
  53.9 1.3 shard_map.67
  55.2 46.2 %all_to_all.15 = f32[128,19,1,128]{3,2,1,0:T(1,128)S(1)} all-to-all(f32[128,19,1,128]{3,2,1,0:T(1,128)S(1)} %bitcast.50), channel_id=1, replica_groups=mesh['zl'=4,'y'=4,'c'=2,'x'=4,'zh'=2] {'zl','y','x','zh'}, dimensions={0} | all-to-all | bytes 2490368 | tf_op jit(solution)/shard_map/all_to_all | solution.py:192
  101.5 0.1 shard_map.68
  101.6 38.1 %all_to_all.16 = f32[128,19,1,128]{3,2,1,0:T(1,128)S(1)} all-to-all(f32[128,19,1,128]{3,2,1,0:T(1,128)S(1)} %bitcast.52), channel_id=1, replica_groups=mesh['zl'=4,'y'=4,'c'=2,'x'=4,'zh'=2] {'zl','y','x','zh'}, dimensions={0} | all-to-all | bytes 2490368 | tf_op jit(solution)/shard_map/all_to_all | solution.py:192
  139.7 4.8 %collective-permute-start.15 = (f32[2432,128]{1,0:T(8,128)S(1)}, f32[2432,128]{1,0:T(8,128)S(1)}, u32[]{:S(2)}, u32[]{:S(2)}) collective-permute-start(f32[2432,128]{1,0:T(8,128)S(1)} %bitcast.48), channel_id=1, source_target_pairs={{0,8},{8,0},{1,9},{9,1},{2,10},{10,2},{3,11},{11,3},{4,12},{12,4},... | collective-permute-start | bytes 3735560 | tf_op jit(solution)/shard_map/ppermute | solution.py:206
  144.5 0.1 copy.25.other_table
  144.6 2.5 %collective-permute-done.15.other_ref = f32[2432,128]{1,0:T(8,128)S(1)} collective-permute-done((f32[2432,128]{1,0:T(8,128)S(1)}, f32[2432,128]{1,0:T(8,128)S(1)}, u32[]{:S(2)}, u32[]{:S(2)}) %collective-permute-start.15) | collective-permute-done | bytes 1245216 | tf_op jit(solution)/shard_map/ppermute | solution.py:206
  147.0 12.7 %shard_map.69 = (f32[32,1024]{1,0:T(8,128)S(1)}, f32[32,128]{1,0:T(8,128)S(1)}) custom-call(s32[1]{0:T(128)} %bitcast.core, s32[18,2]{1,0:T(8,128)S(1)} %copy.24.table.own_table, s32[18,2]{1,0:T(8,128)S(1)} %copy.25.other_table, f32[2432,128]{1,0:T(8,128)S(1)} %bitcast.49, f32[2432,128]{1,0:T(8,128)S(1)} %collective-permute-done.15.other_ref, ...), custom_call_target="tpu_custom_call" | custom-call | tf_op jit(solution)/shard_map/pallas_call | solution.py:173
  159.7 0.7 broadcast_in_dim.4
  160.5 3.5 %all-to-all-start.2 = ((f32[16,32,128]{2,1,0:T(8,128)}), f32[16,32,128]{2,1,0:T(8,128)S(1)}, u32[]{:S(2)}, u32[]{:S(2)}) async-start(f32[16,32,128]{2,1,0:T(8,128)} %broadcast_in_dim.4), calls=%async_computation.2 | async-start | bytes 524288 | tf_op jit(solution)/shard_map/all_to_all | solution.py:209
  164.0 0.1 multiply_bitcast_fusion.1
  164.1 0.7 copy.28
  164.8 9.2 %all-to-all-done.2 = f32[16,32,128]{2,1,0:T(8,128)S(1)} async-done(((f32[16,32,128]{2,1,0:T(8,128)}), f32[16,32,128]{2,1,0:T(8,128)S(1)}, u32[]{:S(2)}, u32[]{:S(2)}) %all-to-all-start.2) | async-done | bytes 262176 | tf_op jit(solution)/shard_map/all_to_all | solution.py:209
  174.0 6.8 %fusion.2 = bf16[1,1024,2048]{2,1,0:T(8,128)(2,1)} fusion(bf16[1,1024,2048]{2,1,0:T(8,128)(2,1)} %param.5, bf16[1,1024,2048]{2,1,0:T(8,128)(2,1)} %param.4, bf16[16,4,8,128]{3,2,1,0:T(8,128)(2,1)S(1)} %get-tuple-element.41, f32[32,1024]{1,0:T(8,128)S(1)} %get-tuple-element.5), kind=kOutput, calls=%fused_computation.4 | convolution fusion | flops 148930560 | bytes 12845056 | tf_op jit(solution)/shard_map/dot_general | solution.py:81
  180.9 0.7 copy.36
  (24 shorter events, 0.3 us)
Async XLA Ops:
  0.6 52.3 %copy-start = (bf16[2048,32]{0,1:T(8,128)(2,1)S(1)}, bf16[2048,32]{0,1:T(8,128)(2,1)}, u32[]{:S(2)}) copy-start(bf16[2048,32]{0,1:T(8,128)(2,1)} %param.6) | copy-start | bytes 393220
  3.2 14.2 %collective-permute-start = (bf16[384,2048]{1,0:T(8,128)(2,1)S(1)}, bf16[384,2048]{1,0:T(8,128)(2,1)S(1)}, u32[]{:S(2)}, u32[]{:S(2)}) collective-permute-start(bf16[384,2048]{1,0:T(8,128)(2,1)S(1)} %fusion.4), channel_id=1, source_target_pairs={{0,8},{8,0},{1,9},{9,1},{2,10},{10,2},{3,11},{11,3},{4,12},{12,4},... | collective-permute-start | bytes 4718600 | tf_op jit(solution)/shard_map/ppermute | solution.py:58
  8.6 2.3 %collective-permute-start.7 = (bf16[128,2048]{1,0:T(8,128)(2,1)}, bf16[128,2048]{1,0:T(8,128)(2,1)}, u32[]{:S(2)}, u32[]{:S(2)}) collective-permute-start(bf16[128,2048]{1,0:T(8,128)(2,1)} %fusion.6), channel_id=1, source_target_pairs={{0,8},{8,0},{1,9},{9,1},{2,10},{10,2},{3,11},{11,3},{4,12},{12,4},... | collective-permute-start | bytes 1572872 | tf_op jit(solution)/shard_map/ppermute | solution.py:58
  12.6 11.9 %collective-permute-start.8 = (bf16[128,512]{1,0:T(8,128)(2,1)S(1)}, bf16[128,512]{1,0:T(8,128)(2,1)S(1)}, u32[]{:S(2)}, u32[]{:S(2)}) collective-permute-start(bf16[128,512]{1,0:T(8,128)(2,1)S(1)} %pad_maximum_fusion.1), channel_id=1, source_target_pairs={{0,128},{64,192},{128,0},{192,64},{1,129},{65,193},{129,1},{193,65... | collective-permute-start | bytes 393224 | tf_op jit(solution)/shard_map/ppermute | solution.py:39
  14.0 12.2 %collective-permute-start.9 = (bf16[128,512]{1,0:T(8,128)(2,1)S(1)}, bf16[128,512]{1,0:T(8,128)(2,1)S(1)}, u32[]{:S(2)}, u32[]{:S(2)}) collective-permute-start(bf16[128,512]{1,0:T(8,128)(2,1)S(1)} %pad_maximum_fusion.2), channel_id=1, source_target_pairs={{0,64},{64,128},{128,192},{192,0},{1,65},{65,129},{129,193},{193,1... | collective-permute-start | bytes 393224 | tf_op jit(solution)/shard_map/ppermute | solution.py:39
  15.7 10.4 %collective-permute-start.10 = (bf16[128,512]{1,0:T(8,128)(2,1)S(1)}, bf16[128,512]{1,0:T(8,128)(2,1)S(1)}, u32[]{:S(2)}, u32[]{:S(2)}) collective-permute-start(bf16[128,512]{1,0:T(8,128)(2,1)S(1)} %pad_maximum_fusion.3), channel_id=1, source_target_pairs={{0,192},{64,0},{128,64},{192,128},{1,193},{65,1},{129,65},{193,129... | collective-permute-start | bytes 393224 | tf_op jit(solution)/shard_map/ppermute | solution.py:39
  20.3 32.6 %copy-start.1 = (s32[2,18,2]{1,2,0:T(2,128)S(1)}, s32[2,18,2]{1,2,0:T(2,128)}, u32[]{:S(2)}) copy-start(s32[2,18,2]{1,2,0:T(2,128)} %constant.99.clone) | copy-start | bytes 868
  20.3 11.3 %collective-permute-start.1 = (bf16[384,512]{1,0:T(8,128)(2,1)S(1)}, bf16[384,512]{1,0:T(8,128)(2,1)S(1)}, u32[]{:S(2)}, u32[]{:S(2)}) collective-permute-start(bf16[384,512]{1,0:T(8,128)(2,1)S(1)} %get-tuple-element.19), channel_id=1, source_target_pairs={{0,32},{16,48},{32,0},{48,16},{1,33},{17,49},{33,1},{49,17},{2,34}... | collective-permute-start | bytes 1179656 | tf_op jit(solution)/shard_map/ppermute | solution.py:39
  23.3 18.4 %collective-permute-start.2 = (bf16[384,512]{1,0:T(8,128)(2,1)S(1)}, bf16[384,512]{1,0:T(8,128)(2,1)S(1)}, u32[]{:S(2)}, u32[]{:S(2)}) collective-permute-start(bf16[384,512]{1,0:T(8,128)(2,1)S(1)} %get-tuple-element.21), channel_id=1, source_target_pairs={{0,16},{16,32},{32,48},{48,0},{1,17},{17,33},{33,49},{49,1},{2,18}... | collective-permute-start | bytes 1179656 | tf_op jit(solution)/shard_map/ppermute | solution.py:39
  24.5 17.2 %collective-permute-start.3 = (bf16[384,512]{1,0:T(8,128)(2,1)S(1)}, bf16[384,512]{1,0:T(8,128)(2,1)S(1)}, u32[]{:S(2)}, u32[]{:S(2)}) collective-permute-start(bf16[384,512]{1,0:T(8,128)(2,1)S(1)} %get-tuple-element.20), channel_id=1, source_target_pairs={{0,48},{16,0},{32,16},{48,32},{1,49},{17,1},{33,17},{49,33},{2,50}... | collective-permute-start | bytes 1179656 | tf_op jit(solution)/shard_map/ppermute | solution.py:39
  26.3 16.1 %collective-permute-start.11 = (bf16[128,128]{1,0:T(8,128)(2,1)S(1)}, bf16[128,128]{1,0:T(8,128)(2,1)S(1)}, u32[]{:S(2)}, u32[]{:S(2)}) collective-permute-start(bf16[128,128]{1,0:T(8,128)(2,1)S(1)} %get-tuple-element.45), channel_id=1, source_target_pairs={{0,32},{16,48},{32,0},{48,16},{1,33},{17,49},{33,1},{49,17},{2,34}... | collective-permute-start | bytes 98312 | tf_op jit(solution)/shard_map/ppermute | solution.py:39
  27.6 17.8 %collective-permute-start.12 = (bf16[128,128]{1,0:T(8,128)(2,1)S(1)}, bf16[128,128]{1,0:T(8,128)(2,1)S(1)}, u32[]{:S(2)}, u32[]{:S(2)}) collective-permute-start(bf16[128,128]{1,0:T(8,128)(2,1)S(1)} %get-tuple-element.47), channel_id=1, source_target_pairs={{0,16},{16,32},{32,48},{48,0},{1,17},{17,33},{33,49},{49,1},{2,18}... | collective-permute-start | bytes 98312 | tf_op jit(solution)/shard_map/ppermute | solution.py:39
  31.5 13.9 %collective-permute-start.13 = (bf16[128,128]{1,0:T(8,128)(2,1)S(1)}, bf16[128,128]{1,0:T(8,128)(2,1)S(1)}, u32[]{:S(2)}, u32[]{:S(2)}) collective-permute-start(bf16[128,128]{1,0:T(8,128)(2,1)S(1)} %get-tuple-element.46), channel_id=1, source_target_pairs={{0,48},{16,0},{32,16},{48,32},{1,49},{17,1},{33,17},{49,33},{2,50}... | collective-permute-start | bytes 98312 | tf_op jit(solution)/shard_map/ppermute | solution.py:39
  42.0 9.1 %collective-permute-start.4 = (bf16[384,128]{1,0:T(8,128)(2,1)S(1)}, bf16[384,128]{1,0:T(8,128)(2,1)S(1)}, u32[]{:S(2)}, u32[]{:S(2)}) collective-permute-start(bf16[384,128]{1,0:T(8,128)(2,1)S(1)} %get-tuple-element.38), channel_id=1, source_target_pairs={{0,128},{64,192},{128,0},{192,64},{1,129},{65,193},{129,1},{193,65... | collective-permute-start | bytes 294920 | tf_op jit(solution)/shard_map/ppermute | solution.py:39
  42.1 9.0 %collective-permute-start.5 = (bf16[384,128]{1,0:T(8,128)(2,1)S(1)}, bf16[384,128]{1,0:T(8,128)(2,1)S(1)}, u32[]{:S(2)}, u32[]{:S(2)}) collective-permute-start(bf16[384,128]{1,0:T(8,128)(2,1)S(1)} %get-tuple-element.40), channel_id=1, source_target_pairs={{0,64},{64,128},{128,192},{192,0},{1,65},{65,129},{129,193},{193,1... | collective-permute-start | bytes 294920 | tf_op jit(solution)/shard_map/ppermute | solution.py:39
  42.4 8.7 %collective-permute-start.6 = (bf16[384,128]{1,0:T(8,128)(2,1)S(1)}, bf16[384,128]{1,0:T(8,128)(2,1)S(1)}, u32[]{:S(2)}, u32[]{:S(2)}) collective-permute-start(bf16[384,128]{1,0:T(8,128)(2,1)S(1)} %get-tuple-element.39), channel_id=1, source_target_pairs={{0,192},{64,0},{128,64},{192,128},{1,193},{65,1},{129,65},{193,129... | collective-permute-start | bytes 294920 | tf_op jit(solution)/shard_map/ppermute | solution.py:39
  51.2 2.6 %collective-permute-start.14 = (bf16[512,128]{1,0:T(8,128)(2,1)S(1)}, bf16[512,128]{1,0:T(8,128)(2,1)S(1)}, u32[]{:S(2)}, u32[]{:S(2)}) collective-permute-start(bf16[512,128]{1,0:T(8,128)(2,1)S(1)} %pad_maximum_fusion.4), channel_id=1, source_target_pairs={{0,8},{8,0},{1,9},{9,1},{2,10},{10,2},{3,11},{11,3},{4,12},{12,4},... | collective-permute-start | bytes 393224 | tf_op jit(solution)/shard_map/ppermute | solution.py:76
  139.7 7.4 %collective-permute-start.15 = (f32[2432,128]{1,0:T(8,128)S(1)}, f32[2432,128]{1,0:T(8,128)S(1)}, u32[]{:S(2)}, u32[]{:S(2)}) collective-permute-start(f32[2432,128]{1,0:T(8,128)S(1)} %bitcast.48), channel_id=1, source_target_pairs={{0,8},{8,0},{1,9},{9,1},{2,10},{10,2},{3,11},{11,3},{4,12},{12,4},... | collective-permute-start | bytes 3735560 | tf_op jit(solution)/shard_map/ppermute | solution.py:206
  160.5 13.5 %all-to-all-start.2 = ((f32[16,32,128]{2,1,0:T(8,128)}), f32[16,32,128]{2,1,0:T(8,128)S(1)}, u32[]{:S(2)}, u32[]{:S(2)}) async-start(f32[16,32,128]{2,1,0:T(8,128)} %broadcast_in_dim.4), calls=%async_computation.2 | async-start | bytes 524288 | tf_op jit(solution)/shard_map/all_to_all | solution.py:209

commit v3 on v2

v3 whole, which is shorter than its diff:
```python
import functools
import math

import jax
import jax.numpy as jnp
import numpy as np
from jax import lax
from jax.experimental import pallas as pl
from jax.experimental.pallas import tpu as pltpu
from jax.sharding import Mesh, PartitionSpec as P

ROWS = 1024
RANK = 32
ITERS = 3
PIVOTS = 8
REPLICAS = 32
HEAD = 256
SWAP = [(0, 1), (1, 0)]
PLANE = ("x", "y")
RING = ("zh", "zl")
HOLDERS = 128
RING_SIZE = 8
PLANE_SIZE = HOLDERS // RING_SIZE
TILE = 128
SIDE = ROWS // TILE
UPPER = [(i, j) for i in range(SIDE) for j in range(i, SIDE)]
SHARE = len(UPPER) // 2
SLOTS = SHARE + 1
TABLE = np.array([UPPER[:SHARE], UPPER[SHARE:]], np.int32)
MIB = 1024 * 1024


def shift(n, d):
    return [(i, (i + d) % n) for i in range(n)]


def exchange_sum(axis, piece):
    n = lax.axis_size(axis)
    me = lax.axis_index(axis)
    total = piece(me).astype(jnp.float32)
    for d in (1, 3, 2):
        sent = piece(lax.rem(me + d, n))
        total = total + lax.ppermute(sent, axis, shift(n, d)).astype(jnp.float32)
    return total.astype(jnp.bfloat16)


def columns(value, start, width):
    return lax.dynamic_slice(value, (0, start), (value.shape[0], width))


def add_kernel(place, grad_ref, error_ref, out_ref):
    value = grad_ref[...].astype(jnp.float32) + error_ref[...].astype(jnp.float32)
    out_ref[...] = value.astype(jnp.bfloat16)


def corrected_rows(place, side, first, arrays, rows):
    cols = arrays[0].shape[1]

    def block(i, p):
        return (p[side] * (ROWS // 2 // TILE) + first // TILE + i, 0)

    return pl.pallas_call(
        add_kernel,
        out_shape=jax.ShapeDtypeStruct((rows, cols), jnp.bfloat16),
        grid_spec=pltpu.PrefetchScalarGridSpec(
            num_scalar_prefetch=1,
            grid=(rows // TILE,),
            in_specs=[pl.BlockSpec((TILE, cols), block)] * 2,
            out_specs=pl.BlockSpec((TILE, cols), lambda i, p: (i, 0)),
        ),
        compiler_params=pltpu.CompilerParams(vmem_limit_bytes=16 * MIB),
        cost_estimate=pl.CostEstimate(flops=2 * rows * cols, bytes_accessed=6 * rows * cols, transcendentals=0),
    )(place, *arrays)


def pair_kernel(first, place, own_ref, got_ref, *out_refs):
    rows, width = out_refs[0].shape
    for d, out_ref in enumerate(out_refs):
        at = pl.ds(pl.multiple_of(lax.rem(place[2] + d, 4) * width, width), width)
        own = own_ref[first : first + rows, at].astype(jnp.float32)
        out_ref[...] = (own + got_ref[:, at].astype(jnp.float32)).astype(jnp.bfloat16)


def pair_pieces(place, own, got, first):
    rows, cols = got.shape
    vmem = pl.BlockSpec(memory_space=pltpu.VMEM)
    return pl.pallas_call(
        functools.partial(pair_kernel, first),
        out_shape=[jax.ShapeDtypeStruct((rows, cols // 4), jnp.bfloat16)] * 4,
        in_specs=[pl.BlockSpec(memory_space=pltpu.SMEM), vmem, vmem],
        out_specs=[vmem] * 4,
        compiler_params=pltpu.CompilerParams(vmem_limit_bytes=8 * MIB),
        cost_estimate=pl.CostEstimate(flops=rows * cols, bytes_accessed=6 * rows * cols, transcendentals=0),
    )(place, own, got)


def reduce_replicas(grad, error):
    core, y = lax.axis_index("c"), lax.axis_index("y")
    half, narrow = grad.shape[0] // 2, grad.shape[1] // 16
    place = jnp.stack([1 - core, core, y]).astype(jnp.int32)
    both = (grad, error)

    def rows(side, first, count=HEAD):
        return corrected_rows(place, side, first, both, count)

    got = [lax.ppermute(rows(0, first), "c", SWAP) for first in (0, HEAD)]
    own = rows(1, 0, half)
    pieces = [pair_pieces(place, own, value, k * HEAD) for k, value in enumerate(got)]
    sums = []
    for mine, *others in pieces:
        total = mine.astype(jnp.float32)
        for d in (1, 3, 2):
            total = total + lax.ppermute(others[d - 1], "y", shift(4, d)).astype(jnp.float32)
        sums.append(total.astype(jnp.bfloat16))
    sums = [exchange_sum("zl", lambda i, v=v: columns(v, i * narrow, narrow)) for v in sums]
    return jnp.concatenate(sums, axis=0)


def join_cores(value):
    core = lax.axis_index("c")
    got = lax.ppermute(value, "c", SWAP)
    return jnp.where(core == 0, value, got), jnp.where(core == 0, got, value)


def dot(a, b, contract, precision=None):
    return lax.dot_general(
        a, b, (contract, ((), ())), precision=precision, preferred_element_type=jnp.float32
    )


def pack_kernel(table, core, total_ref, qt_ref, out_ref):
    def rows(index):
        return total_ref[pl.ds(pl.multiple_of(index * TILE, TILE), TILE), :]

    for k in range(SHARE):
        block = dot(rows(table[k, 0]), rows(table[k, 1]), ((1,), (1,)))
        out_ref[pl.ds(k, TILE, stride=SLOTS), :] = block
    half = ROWS // 2
    for b in range(half // TILE):
        part = dot(qt_ref[...], rows(core[0] * (half // TILE) + b), ((1,), (1,)))
        out_ref[pl.ds(b * RANK * SLOTS + SHARE, RANK, stride=SLOTS), :] = part


def pack(table, core, total, qt):
    return pl.pallas_call(
        pack_kernel,
        out_shape=jax.ShapeDtypeStruct((HOLDERS * SLOTS, TILE), jnp.float32),
        in_specs=[
            pl.BlockSpec(memory_space=pltpu.SMEM),
            pl.BlockSpec(memory_space=pltpu.SMEM),
            pl.BlockSpec(memory_space=pltpu.VMEM),
            pl.BlockSpec(memory_space=pltpu.VMEM),
        ],
        out_specs=pl.BlockSpec(memory_space=pltpu.VMEM),
        compiler_params=pltpu.CompilerParams(vmem_limit_bytes=4 * MIB),
    )(table, core, total, qt)


def small_kernel(body, rows, *args):
    vmem = pl.BlockSpec(memory_space=pltpu.VMEM)
    return pl.pallas_call(
        body,
        out_shape=jax.ShapeDtypeStruct((rows, TILE), jnp.float32),
        in_specs=[vmem],
        out_specs=vmem,
        compiler_params=pltpu.CompilerParams(vmem_limit_bytes=4 * MIB),
    )(*args)


def sum_kernel(parts_ref, out_ref):
    rows = RING_SIZE * SLOTS
    total = parts_ref[:rows, :]
    for p in range(1, parts_ref.shape[0] // rows):
        total = total + parts_ref[p * rows : (p + 1) * rows, :]
    for p in range(out_ref.shape[0] // rows):
        out_ref[p * rows : (p + 1) * rows, :] = total


def ring_kernel(parts_ref, out_ref):
    for k in range(SLOTS):
        row = jnp.sum(parts_ref[pl.ds(k, RING_SIZE, stride=SLOTS), :], axis=0, keepdims=True)
        out_ref[pl.ds(k, RING_SIZE, stride=SLOTS), :] = jnp.broadcast_to(row, (RING_SIZE, TILE))


def inverse_factor(gram):
    wide = (RANK, 2 * RANK)
    row = lax.broadcasted_iota(jnp.int32, wide, 0)
    lane = lax.broadcasted_iota(jnp.int32, wide, 1)
    eye = jnp.where(lane == row + RANK, 1.0, 0.0).astype(jnp.float32)
    work = jnp.concatenate([gram, eye[:, RANK:]], axis=1)
    result = jnp.zeros(wide, jnp.float32)
    for j in range(0, RANK, PIVOTS):
        rows = [work[j + a : j + a + 1, :] for a in range(PIVOTS)]
        cols = [jnp.broadcast_to(work[:, j + a : j + a + 1], wide) for a in range(PIVOTS)]
        corner = {
            (a, b): jnp.broadcast_to(work[j + a : j + a + 1, j + b : j + b + 1], (1, 2 * RANK))
            for a in range(PIVOTS)
            for b in range(a, PIVOTS)
        }
        for a in range(PIVOTS):
            inverse = 1.0 / corner[a, a]
            result = jnp.where(row == j + a, rows[a] * lax.rsqrt(corner[a, a]), result)
            for b in range(a + 1, PIVOTS):
                factor = corner[a, b] * inverse
                rows[b] = rows[b] - factor * rows[a]
                cols[b] = cols[b] - cols[a] * factor
                for c in range(b, PIVOTS):
                    corner[b, c] = corner[b, c] - factor * corner[a, c]
            cols[a] = cols[a] * inverse
        if j + PIVOTS < RANK:
            work = work - sum(cols[a] * rows[a] for a in range(PIVOTS))
    return result[:, RANK:]


def normal_kernel(left):
    gram = dot(left, left, ((1,), (1,)), lax.Precision.HIGHEST)
    inverse = inverse_factor(gram)
    return inverse, dot(inverse, left, ((1,), (0,)), lax.Precision.HIGHEST)


def iterate_kernel(core, own_table, other_table, own_ref, other_ref, total_ref, last_ref, spread_ref, high, low, left_ref):
    half = ROWS // 2
    high_scale = 1.0 / REPLICAS**2
    for table, blocks, place in ((own_table, own_ref, core[0]), (other_table, other_ref, 1 - core[0])):
        for k in range(SHARE):
            i = pl.ds(pl.multiple_of(table[k, 0] * TILE, TILE), TILE)
            j = pl.ds(pl.multiple_of(table[k, 1] * TILE, TILE), TILE)
            block = blocks[pl.ds(k, TILE, stride=SLOTS), :] * high_scale
            for at, value in (((i, j), block), ((j, i), block.T)):
                top = value.astype(jnp.bfloat16)
                high[at] = top
                low[at] = (value - top.astype(jnp.float32)).astype(jnp.bfloat16)
        for b in range(half // TILE):
            at = pl.ds(pl.multiple_of(place * half + b * TILE, TILE), TILE)
            left_ref[:, at] = blocks[pl.ds(b * RANK * SLOTS + SHARE, RANK, stride=SLOTS), :] / REPLICAS
    left = left_ref[...]
    for step in range(ITERS - 1):
        basis = normal_kernel(left)[1]
        pbt = basis.astype(jnp.bfloat16)
        left = dot(pbt, high[...], ((1,), (0,))) + dot(pbt, low[...], ((1,), (0,)))
    last_ref[...] = left
    total = total_ref[...].astype(jnp.float32)
    spread = dot(left, total, ((1,), (0,)), lax.Precision.HIGHEST) / REPLICAS
    for p in range(spread_ref.shape[0]):
        spread_ref[p] = spread


def iterate(core, own_table, other_table, own, other, total):
    smem = pl.BlockSpec(memory_space=pltpu.SMEM)
    vmem = pl.BlockSpec(memory_space=pltpu.VMEM)
    return pl.pallas_call(
        iterate_kernel,
        out_shape=(
            jax.ShapeDtypeStruct((RANK, ROWS), jnp.float32),
            jax.ShapeDtypeStruct((16, RANK, TILE), jnp.float32),
        ),
        in_specs=[smem] * 3 + [vmem] * 3,
        out_specs=(vmem, vmem),
        scratch_shapes=[
            pltpu.VMEM((ROWS, ROWS), jnp.bfloat16),
            pltpu.VMEM((ROWS, ROWS), jnp.bfloat16),
            pltpu.VMEM((RANK, ROWS), jnp.float32),
        ],
        compiler_params=pltpu.CompilerParams(vmem_limit_bytes=14 * MIB),
    )(core, own_table, other_table, own, other, total)


def last_kernel(left_ref, inverse_ref, basis_ref):
    inverse_ref[...], basis_ref[...] = normal_kernel(left_ref[...])


def last_basis(left):
    vmem = pl.BlockSpec(memory_space=pltpu.VMEM)
    return pl.pallas_call(
        last_kernel,
        out_shape=(
            jax.ShapeDtypeStruct((RANK, RANK), jnp.float32),
            jax.ShapeDtypeStruct(left.shape, jnp.float32),
        ),
        in_specs=[vmem],
        out_specs=(vmem, vmem),
        compiler_params=pltpu.CompilerParams(vmem_limit_bytes=4 * MIB),
        cost_estimate=pl.CostEstimate(flops=1000, bytes_accessed=1000, transcendentals=0),
    )(left)


def corrected_kernel(grad_ref, error_ref, out_ref):
    value = grad_ref[...].astype(jnp.float32) + error_ref[...].astype(jnp.float32)
    out_ref[...] = value.astype(jnp.bfloat16)


def corrected_sum(grad, error):
    rows = pl.BlockSpec((2 * TILE, grad.shape[1]), lambda i: (i, 0))
    return pl.pallas_call(
        corrected_kernel,
        out_shape=jax.ShapeDtypeStruct(grad.shape, grad.dtype),
        grid=(ROWS // TILE // 2,),
        in_specs=[rows, rows],
        out_specs=rows,
        compiler_params=pltpu.CompilerParams(vmem_limit_bytes=60 * MIB),
        cost_estimate=pl.CostEstimate(flops=1000, bytes_accessed=1000, transcendentals=0),
    )(grad, error)


def finish_kernel(inverse_ref, spread_ref, pbt_ref, corrected_ref, factor_ref, out_ref, wide, qbt):
    blocks, _, width = spread_ref.shape
    step = pl.program_id(0)

    @pl.when(step == 0)
    def _():
        for b in range(blocks):
            wide[:, b * width : (b + 1) * width] = spread_ref[b]
        right = dot(inverse_ref[...], wide[...], ((1,), (0,)), lax.Precision.HIGHEST)
        factor_ref[...] = right / math.sqrt(ROWS)
        qbt[...] = right.astype(jnp.bfloat16)

    rows = out_ref.shape[0]
    approx = dot(pbt_ref[...], qbt[...], ((0,), (0,)))
    corrected = corrected_ref[pl.ds(pl.multiple_of(step * rows, rows), rows), :]
    out_ref[...] = (corrected.astype(jnp.float32) - approx).astype(jnp.bfloat16)


def finish(inverse, spread, pbt, corrected):
    vmem = pl.BlockSpec(memory_space=pltpu.VMEM)
    cols = corrected.shape[1]
    rows = 2 * TILE
    return pl.pallas_call(
        finish_kernel,
        out_shape=(
            jax.ShapeDtypeStruct((RANK, cols), jnp.float32),
            jax.ShapeDtypeStruct((ROWS, cols), jnp.bfloat16),
        ),
        grid=(ROWS // rows,),
        in_specs=[vmem, vmem, pl.BlockSpec((RANK, rows), lambda i: (0, i)), vmem],
        out_specs=(pl.BlockSpec((RANK, cols), lambda i: (0, 0)), pl.BlockSpec((rows, cols), lambda i: (i, 0))),
        scratch_shapes=[pltpu.VMEM((RANK, cols), jnp.float32), pltpu.VMEM((RANK, cols), jnp.bfloat16)],
        compiler_params=pltpu.CompilerParams(vmem_limit_bytes=16 * MIB),
    )(inverse, spread, pbt, corrected)


def sum_chips(value):
    rows = RING_SIZE * SLOTS

    def swap(v, axes, size):
        v = lax.all_to_all(v.reshape(size, rows, TILE), axes, 0, 0, tiled=True)
        return v.reshape(size * rows, TILE)

    def ring(v):
        v = lax.all_to_all(v.reshape(RING_SIZE, SLOTS, 1, TILE), RING, 0, 0, tiled=True)
        return v.reshape(rows, TILE)

    part = small_kernel(sum_kernel, rows, swap(value, PLANE, PLANE_SIZE))
    part = ring(small_kernel(ring_kernel, rows, ring(part)))
    return swap(small_kernel(sum_kernel, PLANE_SIZE * rows, part), PLANE, PLANE_SIZE)


def shards(grad, error, q_init):
    core, y, zl = (lax.axis_index(a) for a in ("c", "y", "zl"))
    mine = reduce_replicas(grad[0], error[0])
    width = mine.shape[1]
    total = jnp.concatenate(join_cores(mine), axis=0)
    qt = lax.dynamic_slice(q_init, ((y * 4 + zl) * width, 0), (width, RANK)).T
    table = jnp.asarray(TABLE)
    own_table = lax.dynamic_index_in_dim(table, core, 0, False)
    other_table = lax.dynamic_index_in_dim(table, 1 - core, 0, False)
    which = core.reshape(1)
    packed = pack(own_table, which, total, qt)
    grad, error, packed = lax.optimization_barrier((grad, error, packed))
    corrected = corrected_sum(grad[0], error[0])
    own, corrected = lax.optimization_barrier((sum_chips(packed), corrected))
    other = lax.ppermute(own, "c", SWAP)
    left, spread = iterate(which, own_table, other_table, own, other, total)
    spread = lax.all_to_all(spread, ("y", "zl"), 0, 0, tiled=True)
    inverse, basis = last_basis(left)
    factor, new_error = finish(inverse, spread, basis.astype(jnp.bfloat16), corrected)
    own_rows = ROWS // 256
    start = lax.axis_index(("zl", "y", "c", "x", "zh")) * own_rows
    own_basis = lax.dynamic_slice(basis, (0, start), (RANK, own_rows)).T
    return (own_basis * math.sqrt(ROWS), factor.T, new_error[None])


def solution(mesh):
    fine = Mesh(mesh.devices.reshape(4, 4, 2, 4, 2), ("zl", "y", "c", "x", "zh"))
    dp, tensor = ("zl", "y", "c"), ("x", "zh")
    placed = (P(dp, None, tensor), P(dp, None, tensor), P(tensor, None))
    return jax.shard_map(
        shards,
        mesh=fine,
        in_specs=placed,
        out_specs=(P(dp + tensor, None), P(tensor, None), P(dp, None, tensor)),
        check_vma=False,
    )
```

time: 182 us -> 156 us (0.86)
  blocking collectives: 84.3 us -> 48 us
  Pallas kernels: 14.1 us -> 26.4 us
  other arithmetic: 9.47 us -> 1.73 us
  matrix products: 6.85 us -> 0 us
  waiting for transfers between devices: 32.2 us -> 38.6 us
  local copies, waits for them, and re-layouts: 2.79 us -> 7.53 us
    all_to_all x2 -> x3, blocking collectives: 84.3 us -> 48 us  [the longest x1 24.2 us: swap(): v = lax.all_to_all(v.reshape(size, rows, TILE), axes, 0, 0, tiled=True)]
    pallas_call x1 -> x11, Pallas kernels: 0.12 us -> 18.1 us  [the longest x1 6.02 us: corrected_sum(): pl.pallas_call(corrected_kernel, out_shape=jax.ShapeDtypeStruct(grad.shap...]
    ppermute x2 -> x8, waiting for transfers between devices: 2.23 us -> 15.8 us  [the longest x6 15.5 us: reduce_replicas(): lax.ppermute(others[d - 1], 'y', shift(4, d)).astype(jnp.float32)]
    ppermute x12 -> x6, waiting for transfers between devices: 17.4 us -> 4.78 us  [exchange_sum(): total = total + lax.ppermute(sent, axis, shift(n, d)).astype(jnp.float32)]
    ppermute x12 -> x6, starting transfers between devices: 17.7 us -> 5.92 us  [exchange_sum(): total = total + lax.ppermute(sent, axis, shift(n, d)).astype(jnp.float32)]
    dot_general x1 -> x0, matrix products: 6.85 us -> none  [dot(): lax.dot_general(a, b, (contract, ((), ())), precision=precision, preferre...]
    unnamed x5 -> x11, local copies, waits for them, and re-layouts: 0.67 us -> 7.23 us
    pallas_call x1, Pallas kernels: 12.7 us -> 6.98 us  [iterate(): pl.pallas_call(iterate_kernel, out_shape=(jax.ShapeDtypeStruct((RANK, ROW...]
  transfers between devices with their start and end apart: 17 -> 18, of which waited for: 8 -> 13; matrix products, arithmetic and copies ran while one was open for 4% -> 2% of each run, Pallas kernels for 0% -> 8%
where the time goes in v3:
time: 156 us
  blocking collectives  48 us (31%)
  waiting for transfers between devices  38.6 us (25%)
  starting transfers between devices  32.5 us (21%)
  Pallas kernels  26.4 us (17%)
  local copies, waits for them, and re-layouts  7.53 us (5%)
  other arithmetic  1.73 us (1%)
    all_to_all x1, blocking collectives, swap(): v = lax.all_to_all(v.reshape(size, rows, TILE), axes, 0, 0, tiled=True)  24.2 us
    all_to_all x2, blocking collectives, ring(): lax.all_to_all(v.reshape(RING_SIZE, SLOTS, 1, TILE), RING, 0, 0, tiled=True)  23.7 us
    ppermute x6, waiting for transfers between devices, reduce_replicas(): lax.ppermute(others[d - 1], 'y', shift(4, d)).astype(jnp.float32)  15.5 us
    ppermute x1, starting transfers between devices, shards(): other = lax.ppermute(own, 'c', SWAP)  7.82 us
    all_to_all x1, waiting for transfers between devices, shards(): spread = lax.all_to_all(spread, ('y', 'zl'), 0, 0, tiled=True)  7.79 us
    unnamed x11, local copies, waits for them, and re-layouts  7.23 us
    pallas_call x1, Pallas kernels, iterate(): pl.pallas_call(iterate_kernel, out_shape=(jax.ShapeDtypeStruct((RANK, ROW...  6.98 us
    all_to_all x1, waiting for transfers between devices, swap(): v = lax.all_to_all(v.reshape(size, rows, TILE), axes, 0, 0, tiled=True)  6.94 us
  transfers between devices with their start and end apart: 18, of which 13 were waited for; matrix products, arithmetic and copies ran while one was open for 2% of the time, Pallas kernels for 8%

profile of v3, /device:TPU:1, one launch (start us, length us, event | category | flops | bytes accessed | tf_op | source)
XLA Modules:
  0.0 155.5 jit_solution(15255275275073443408)
XLA Ops:
  0.7 2.2 %copy-done.1 = bf16[1,1024,2048]{2,1,0:T(8,128)(2,1)S(1)} copy-done((bf16[1,1024,2048]{2,1,0:T(8,128)(2,1)S(1)}, bf16[1,1024,2048]{2,1,0:T(8,128)(2,1)}, u32[]{:S(2)}) %copy-start.1) | copy-done | bytes 4194328
  2.9 2.2 %copy-done.2 = bf16[1,1024,2048]{2,1,0:T(8,128)(2,1)S(1)} copy-done((bf16[1,1024,2048]{2,1,0:T(8,128)(2,1)S(1)}, bf16[1,1024,2048]{2,1,0:T(8,128)(2,1)}, u32[]{:S(2)}) %copy-start.2) | copy-done | bytes 4194328
  5.1 0.8 shard_map.70
  5.9 3.3 %collective-permute-start.7 = (bf16[256,2048]{1,0:T(8,128)(2,1)S(1)}, bf16[256,2048]{1,0:T(8,128)(2,1)S(1)}, u32[]{:S(2)}, u32[]{:S(2)}) collective-permute-start(bf16[256,2048]{1,0:T(8,128)(2,1)S(1)} %shard_map.70), channel_id=1, source_target_pairs={{0,8},{8,0},{1,9},{9,1},{2,10},{10,2},{3,11},{11,3},{4,12},{12,4},... | collective-permute-start | bytes 3145736 | tf_op jit(solution)/shard_map/ppermute | solution.py:106
  9.3 0.8 shard_map.68
  10.2 1.1 shard_map.67.own_ref
  11.3 0.2 collective-permute-done.7.got_ref
  11.6 1.5 shard_map.71
  13.1 1.2 collective-permute-start.10
  14.3 0.8 collective-permute-start.9
  15.0 0.7 collective-permute-start.8
  15.7 1.5 shard_map.69
  17.2 1.9 %collective-permute-start.3 = (bf16[256,512]{1,0:T(8,128)(2,1)S(1)}, bf16[256,512]{1,0:T(8,128)(2,1)S(1)}, u32[]{:S(2)}, u32[]{:S(2)}) collective-permute-start(bf16[256,512]{1,0:T(8,128)(2,1)S(1)} %get-tuple-element.25), channel_id=1, source_target_pairs={{0,32},{16,48},{32,0},{48,16},{1,33},{17,49},{33,1},{49,17},{2,34}... | collective-permute-start | bytes 786440 | tf_op jit(solution)/shard_map/ppermute | solution.py:113
  19.1 1.0 collective-permute-start.2
  20.1 2.4 %collective-permute-done.10 = bf16[256,512]{1,0:T(8,128)(2,1)} collective-permute-done((bf16[256,512]{1,0:T(8,128)(2,1)}, bf16[256,512]{1,0:T(8,128)(2,1)}, u32[]{:S(2)}, u32[]{:S(2)}) %collective-permute-start.10) | collective-permute-done | bytes 262176 | tf_op jit(solution)/shard_map/ppermute | solution.py:113
  22.5 4.2 %collective-permute-done.9 = bf16[256,512]{1,0:T(8,128)(2,1)} collective-permute-done((bf16[256,512]{1,0:T(8,128)(2,1)}, bf16[256,512]{1,0:T(8,128)(2,1)}, u32[]{:S(2)}, u32[]{:S(2)}) %collective-permute-start.9) | collective-permute-done | bytes 262176 | tf_op jit(solution)/shard_map/ppermute | solution.py:113
  26.7 2.7 %collective-permute-done.8 = bf16[256,512]{1,0:T(8,128)(2,1)} collective-permute-done((bf16[256,512]{1,0:T(8,128)(2,1)}, bf16[256,512]{1,0:T(8,128)(2,1)}, u32[]{:S(2)}, u32[]{:S(2)}) %collective-permute-start.8) | collective-permute-done | bytes 262176 | tf_op jit(solution)/shard_map/ppermute | solution.py:113
  29.4 1.3 add_convert_fusion
  30.7 1.4 collective-permute-start.13
  32.1 1.4 collective-permute-start.12
  33.6 0.1 collective-permute-start.11
  33.8 4.1 %collective-permute-done.2 = bf16[256,512]{1,0:T(8,128)(2,1)S(1)} collective-permute-done((bf16[256,512]{1,0:T(8,128)(2,1)S(1)}, bf16[256,512]{1,0:T(8,128)(2,1)S(1)}, u32[]{:S(2)}, u32[]{:S(2)}) %collective-permute-start.2) | collective-permute-done | bytes 262176 | tf_op jit(solution)/shard_map/ppermute | solution.py:113
  37.9 2.0 %collective-permute-done.1 = bf16[256,512]{1,0:T(8,128)(2,1)S(1)} collective-permute-done((bf16[256,512]{1,0:T(8,128)(2,1)S(1)}, bf16[256,512]{1,0:T(8,128)(2,1)S(1)}, u32[]{:S(2)}, u32[]{:S(2)}) %collective-permute-start.1) | collective-permute-done | bytes 262176 | tf_op jit(solution)/shard_map/ppermute | solution.py:113
  39.9 0.1 add_convert_fusion.1
  40.1 1.3 collective-permute-start.6
  41.4 1.4 collective-permute-start.5
  42.9 0.2 collective-permute-start.4
  43.1 2.8 %collective-permute-done.6 = bf16[256,128]{1,0:T(8,128)(2,1)S(1)} collective-permute-done((bf16[256,128]{1,0:T(8,128)(2,1)S(1)}, bf16[256,128]{1,0:T(8,128)(2,1)S(1)}, u32[]{:S(2)}, u32[]{:S(2)}) %collective-permute-start.6) | collective-permute-done | bytes 65568 | tf_op jit(solution)/shard_map/ppermute | solution.py:43
  46.0 1.9 %collective-permute-done.4 = bf16[256,128]{1,0:T(8,128)(2,1)S(1)} collective-permute-done((bf16[256,128]{1,0:T(8,128)(2,1)S(1)}, bf16[256,128]{1,0:T(8,128)(2,1)S(1)}, u32[]{:S(2)}, u32[]{:S(2)}) %collective-permute-start.4) | collective-permute-done | bytes 65568 | tf_op jit(solution)/shard_map/ppermute | solution.py:43
  48.0 2.3 %collective-permute-start.14 = (bf16[512,128]{1,0:T(8,128)(2,1)S(1)}, bf16[512,128]{1,0:T(8,128)(2,1)S(1)}, u32[]{:S(2)}, u32[]{:S(2)}) collective-permute-start(bf16[512,128]{1,0:T(8,128)(2,1)S(1)} %pad_maximum_fusion.1), channel_id=1, source_target_pairs={{0,8},{8,0},{1,9},{9,1},{2,10},{10,2},{3,11},{11,3},{4,12},{12,4},... | collective-permute-start | bytes 393224 | tf_op jit(solution)/shard_map/ppermute | solution.py:121
  50.4 0.9 collective-permute-done.14
  51.4 1.3 shard_map.72
  52.7 24.2 %all_to_all.25 = f32[16,152,128]{2,1,0:T(8,128)S(1)} all-to-all(f32[16,152,128]{2,1,0:T(8,128)S(1)} %bitcast.35), channel_id=1, replica_groups=mesh['zl'=4,'y'=4,'c'=2,'x'=4,'zh'=2] {'x','y'}, dimensions={0} | all-to-all | bytes 2490368 | tf_op jit(solution)/shard_map/all_to_all | solution.py:345
  77.0 14.0 %all_to_all.26 = f32[8,19,1,128]{3,2,1,0:T(1,128)S(1)} all-to-all(f32[8,19,1,128]{3,2,1,0:T(1,128)S(1)} %bitcast.37), channel_id=1, replica_groups=mesh['zl'=4,'y'=4,'c'=2,'x'=4,'zh'=2] {'zh','zl'}, dimensions={0} | all-to-all | bytes 155648 | tf_op jit(solution)/shard_map/all_to_all | solution.py:349
  91.0 9.7 %all_to_all.27 = f32[8,19,1,128]{3,2,1,0:T(1,128)S(1)} all-to-all(f32[8,19,1,128]{3,2,1,0:T(1,128)S(1)} %bitcast.40), channel_id=1, replica_groups=mesh['zl'=4,'y'=4,'c'=2,'x'=4,'zh'=2] {'zh','zl'}, dimensions={0} | all-to-all | bytes 155648 | tf_op jit(solution)/shard_map/all_to_all | solution.py:349
  100.8 1.1 shard_map.75
  101.9 3.9 %all-to-all-start.3 = ((f32[16,152,128]{2,1,0:T(8,128)}), f32[16,152,128]{2,1,0:T(8,128)S(1)}, u32[]{:S(2)}, u32[]{:S(2)}) async-start(f32[16,152,128]{2,1,0:T(8,128)} %bitcast.14), calls=%async_computation.3 | async-start | bytes 2490368 | tf_op jit(solution)/shard_map/all_to_all | solution.py:345
  105.8 6.0 %shard_map.76.corrected_ref = bf16[1024,2048]{1,0:T(8,128)(2,1)} custom-call(bf16[1024,2048]{1,0:T(8,128)(2,1)} %bitcast.25, bf16[1024,2048]{1,0:T(8,128)(2,1)} %bitcast.29), custom_call_target="tpu_custom_call" | custom-call | flops 1000 | bytes 1000 | tf_op jit(solution)/shard_map/pallas_call | solution.py:294
  111.8 6.9 %all-to-all-done.3 = f32[16,152,128]{2,1,0:T(8,128)S(1)} async-done(((f32[16,152,128]{2,1,0:T(8,128)}), f32[16,152,128]{2,1,0:T(8,128)S(1)}, u32[]{:S(2)}, u32[]{:S(2)}) %all-to-all-start.3) | async-done | bytes 1245216 | tf_op jit(solution)/shard_map/all_to_all | solution.py:345
  118.8 7.8 %collective-permute-start.15 = (f32[2432,128]{1,0:T(8,128)S(1)}, f32[2432,128]{1,0:T(8,128)S(1)}, u32[]{:S(2)}, u32[]{:S(2)}) collective-permute-start(f32[2432,128]{1,0:T(8,128)S(1)} %bitcast.33), channel_id=1, source_target_pairs={{0,8},{8,0},{1,9},{9,1},{2,10},{10,2},{3,11},{11,3},{4,12},{12,4},... | collective-permute-start | bytes 3735560 | tf_op jit(solution)/shard_map/ppermute | solution.py:371
  126.7 2.5 %collective-permute-done.15.other_ref = f32[2432,128]{1,0:T(8,128)S(1)} collective-permute-done((f32[2432,128]{1,0:T(8,128)S(1)}, f32[2432,128]{1,0:T(8,128)S(1)}, u32[]{:S(2)}, u32[]{:S(2)}) %collective-permute-start.15) | collective-permute-done | bytes 1245216 | tf_op jit(solution)/shard_map/ppermute | solution.py:371
  129.2 7.0 %shard_map.77 = (f32[32,1024]{1,0:T(8,128)S(1)}, f32[16,32,128]{2,1,0:T(8,128)}) custom-call(s32[1]{0:T(128)} %bitcast.core, s32[18,2]{1,0:T(8,128)S(1)} %copy.18.table.own_table, s32[18,2]{1,0:T(8,128)S(1)} %copy.19.other_table, f32[2432,128]{1,0:T(8,128)S(1)} %bitcast.34, f32[2432,128]{1,0:T(8,128)S(1)} %collective-permute-done.15.other_ref, ...), custom_call_target="tpu_custom_call" | custom-call | tf_op jit(solution)/shard_map/pallas_call | solution.py:251
  136.1 3.5 %all-to-all-start.4 = ((f32[16,32,128]{2,1,0:T(8,128)}), f32[16,32,128]{2,1,0:T(8,128)S(1)}, u32[]{:S(2)}, u32[]{:S(2)}) async-start(f32[16,32,128]{2,1,0:T(8,128)} %get-tuple-element.37), calls=%async_computation.4 | async-start | bytes 524288 | tf_op jit(solution)/shard_map/all_to_all | solution.py:373
  139.7 1.4 shard_map.78
  141.2 0.7 copy.20
  141.9 7.8 %all-to-all-done.4.spread_ref = f32[16,32,128]{2,1,0:T(8,128)S(1)} async-done(((f32[16,32,128]{2,1,0:T(8,128)}), f32[16,32,128]{2,1,0:T(8,128)S(1)}, u32[]{:S(2)}, u32[]{:S(2)}) %all-to-all-start.4) | async-done | bytes 262176 | tf_op jit(solution)/shard_map/all_to_all | solution.py:373
  149.6 2.2 %copy-done.3 = bf16[1024,2048]{1,0:T(8,128)(2,1)S(1)} copy-done((bf16[1024,2048]{1,0:T(8,128)(2,1)S(1)}, bf16[1024,2048]{1,0:T(8,128)(2,1)}, u32[]{:S(2)}) %copy-start.3) | copy-done | bytes 4194328
  151.8 3.7 %shard_map.79 = (f32[32,2048]{1,0:T(8,128)}, bf16[1024,2048]{1,0:T(8,128)(2,1)}) custom-call(f32[32,32]{1,0:T(8,128)S(1)} %get-tuple-element.36.inverse_ref, f32[16,32,128]{2,1,0:T(8,128)S(1)} %all-to-all-done.4.spread_ref, bf16[32,1024]{1,0:T(8,128)(2,1)S(1)} %convert_element_type.83.pbt_ref, bf16[1024,2048]{1,0:T(8,128)(2,1)S(1)} %copy-done.3), custom_call_target="tpu_custom_call" | custom-call | tf_op jit(solution)/shard_map/pallas_call | solution.py:327
  (31 shorter events, 0.9 us)
Async XLA Ops:
  0.6 49.8 %copy-start = (bf16[2048,32]{0,1:T(8,128)(2,1)S(1)}, bf16[2048,32]{0,1:T(8,128)(2,1)}, u32[]{:S(2)}) copy-start(bf16[2048,32]{0,1:T(8,128)(2,1)} %param.6) | copy-start | bytes 393220
  0.7 2.2 %copy-start.1 = (bf16[1,1024,2048]{2,1,0:T(8,128)(2,1)S(1)}, bf16[1,1024,2048]{2,1,0:T(8,128)(2,1)}, u32[]{:S(2)}) copy-start(bf16[1,1024,2048]{2,1,0:T(8,128)(2,1)} %param.4) | copy-start | bytes 12582916
  2.9 2.2 %copy-start.2 = (bf16[1,1024,2048]{2,1,0:T(8,128)(2,1)S(1)}, bf16[1,1024,2048]{2,1,0:T(8,128)(2,1)}, u32[]{:S(2)}) copy-start(bf16[1,1024,2048]{2,1,0:T(8,128)(2,1)} %param.5) | copy-start | bytes 12582916
  5.9 5.6 %collective-permute-start.7 = (bf16[256,2048]{1,0:T(8,128)(2,1)S(1)}, bf16[256,2048]{1,0:T(8,128)(2,1)S(1)}, u32[]{:S(2)}, u32[]{:S(2)}) collective-permute-start(bf16[256,2048]{1,0:T(8,128)(2,1)S(1)} %shard_map.70), channel_id=1, source_target_pairs={{0,8},{8,0},{1,9},{9,1},{2,10},{10,2},{3,11},{11,3},{4,12},{12,4},... | collective-permute-start | bytes 3145736 | tf_op jit(solution)/shard_map/ppermute | solution.py:106
  10.1 5.6 %collective-permute-start = (bf16[256,2048]{1,0:T(8,128)(2,1)S(1)}, bf16[256,2048]{1,0:T(8,128)(2,1)}, u32[]{:S(2)}, u32[]{:S(2)}) collective-permute-start(bf16[256,2048]{1,0:T(8,128)(2,1)S(1)} %shard_map.68), channel_id=1, source_target_pairs={{0,8},{8,0},{1,9},{9,1},{2,10},{10,2},{3,11},{11,3},{4,12},{12,4},... | collective-permute-start | bytes 3145736 | tf_op jit(solution)/shard_map/ppermute | solution.py:106
  13.1 9.4 %collective-permute-start.10 = (bf16[256,512]{1,0:T(8,128)(2,1)}, bf16[256,512]{1,0:T(8,128)(2,1)}, u32[]{:S(2)}, u32[]{:S(2)}) collective-permute-start(bf16[256,512]{1,0:T(8,128)(2,1)} %get-tuple-element.29), channel_id=1, source_target_pairs={{0,32},{16,48},{32,0},{48,16},{1,33},{17,49},{33,1},{49,17},{2,34}... | collective-permute-start | bytes 786440 | tf_op jit(solution)/shard_map/ppermute | solution.py:113
  14.3 12.4 %collective-permute-start.9 = (bf16[256,512]{1,0:T(8,128)(2,1)}, bf16[256,512]{1,0:T(8,128)(2,1)}, u32[]{:S(2)}, u32[]{:S(2)}) collective-permute-start(bf16[256,512]{1,0:T(8,128)(2,1)} %get-tuple-element.28), channel_id=1, source_target_pairs={{0,48},{16,0},{32,16},{48,32},{1,49},{17,1},{33,17},{49,33},{2,50}... | collective-permute-start | bytes 786440 | tf_op jit(solution)/shard_map/ppermute | solution.py:113
  15.0 14.4 %collective-permute-start.8 = (bf16[256,512]{1,0:T(8,128)(2,1)}, bf16[256,512]{1,0:T(8,128)(2,1)}, u32[]{:S(2)}, u32[]{:S(2)}) collective-permute-start(bf16[256,512]{1,0:T(8,128)(2,1)} %get-tuple-element.27), channel_id=1, source_target_pairs={{0,16},{16,32},{32,48},{48,0},{1,17},{17,33},{33,49},{49,1},{2,18}... | collective-permute-start | bytes 786440 | tf_op jit(solution)/shard_map/ppermute | solution.py:113
  17.2 16.4 %collective-permute-start.3 = (bf16[256,512]{1,0:T(8,128)(2,1)S(1)}, bf16[256,512]{1,0:T(8,128)(2,1)S(1)}, u32[]{:S(2)}, u32[]{:S(2)}) collective-permute-start(bf16[256,512]{1,0:T(8,128)(2,1)S(1)} %get-tuple-element.25), channel_id=1, source_target_pairs={{0,32},{16,48},{32,0},{48,16},{1,33},{17,49},{33,1},{49,17},{2,34}... | collective-permute-start | bytes 786440 | tf_op jit(solution)/shard_map/ppermute | solution.py:113
  19.1 18.8 %collective-permute-start.2 = (bf16[256,512]{1,0:T(8,128)(2,1)S(1)}, bf16[256,512]{1,0:T(8,128)(2,1)S(1)}, u32[]{:S(2)}, u32[]{:S(2)}) collective-permute-start(bf16[256,512]{1,0:T(8,128)(2,1)S(1)} %get-tuple-element.24), channel_id=1, source_target_pairs={{0,48},{16,0},{32,16},{48,32},{1,49},{17,1},{33,17},{49,33},{2,50}... | collective-permute-start | bytes 786440 | tf_op jit(solution)/shard_map/ppermute | solution.py:113
  22.5 17.4 %collective-permute-start.1 = (bf16[256,512]{1,0:T(8,128)(2,1)S(1)}, bf16[256,512]{1,0:T(8,128)(2,1)S(1)}, u32[]{:S(2)}, u32[]{:S(2)}) collective-permute-start(bf16[256,512]{1,0:T(8,128)(2,1)S(1)} %get-tuple-element.23), channel_id=1, source_target_pairs={{0,16},{16,32},{32,48},{48,0},{1,17},{17,33},{33,49},{49,1},{2,18}... | collective-permute-start | bytes 786440 | tf_op jit(solution)/shard_map/ppermute | solution.py:113
  29.4 20.9 %copy-start.4 = (s32[2,18,2]{1,2,0:T(2,128)S(1)}, s32[2,18,2]{1,2,0:T(2,128)}, u32[]{:S(2)}) copy-start(s32[2,18,2]{1,2,0:T(2,128)} %constant.60.clone) | copy-start | bytes 868
  30.7 12.1 %collective-permute-start.13 = (bf16[256,128]{1,0:T(8,128)(2,1)S(1)}, bf16[256,128]{1,0:T(8,128)(2,1)S(1)}, u32[]{:S(2)}, u32[]{:S(2)}) collective-permute-start(bf16[256,128]{1,0:T(8,128)(2,1)S(1)} %get-tuple-element.56), channel_id=1, source_target_pairs={{0,128},{64,192},{128,0},{192,64},{1,129},{65,193},{129,1},{193,65... | collective-permute-start | bytes 196616 | tf_op jit(solution)/shard_map/ppermute | solution.py:43
  32.1 11.0 %collective-permute-start.12 = (bf16[256,128]{1,0:T(8,128)(2,1)S(1)}, bf16[256,128]{1,0:T(8,128)(2,1)S(1)}, u32[]{:S(2)}, u32[]{:S(2)}) collective-permute-start(bf16[256,128]{1,0:T(8,128)(2,1)S(1)} %get-tuple-element.57), channel_id=1, source_target_pairs={{0,192},{64,0},{128,64},{192,128},{1,193},{65,1},{129,65},{193,129... | collective-permute-start | bytes 196616 | tf_op jit(solution)/shard_map/ppermute | solution.py:43
  33.6 9.4 %collective-permute-start.11 = (bf16[256,128]{1,0:T(8,128)(2,1)S(1)}, bf16[256,128]{1,0:T(8,128)(2,1)S(1)}, u32[]{:S(2)}, u32[]{:S(2)}) collective-permute-start(bf16[256,128]{1,0:T(8,128)(2,1)S(1)} %get-tuple-element.55), channel_id=1, source_target_pairs={{0,64},{64,128},{128,192},{192,0},{1,65},{65,129},{129,193},{193,1... | collective-permute-start | bytes 196616 | tf_op jit(solution)/shard_map/ppermute | solution.py:43
  40.1 5.9 %collective-permute-start.6 = (bf16[256,128]{1,0:T(8,128)(2,1)S(1)}, bf16[256,128]{1,0:T(8,128)(2,1)S(1)}, u32[]{:S(2)}, u32[]{:S(2)}) collective-permute-start(bf16[256,128]{1,0:T(8,128)(2,1)S(1)} %get-tuple-element.53), channel_id=1, source_target_pairs={{0,128},{64,192},{128,0},{192,64},{1,129},{65,193},{129,1},{193,65... | collective-permute-start | bytes 196616 | tf_op jit(solution)/shard_map/ppermute | solution.py:43
  41.4 4.5 %collective-permute-start.5 = (bf16[256,128]{1,0:T(8,128)(2,1)S(1)}, bf16[256,128]{1,0:T(8,128)(2,1)S(1)}, u32[]{:S(2)}, u32[]{:S(2)}) collective-permute-start(bf16[256,128]{1,0:T(8,128)(2,1)S(1)} %get-tuple-element.54), channel_id=1, source_target_pairs={{0,192},{64,0},{128,64},{192,128},{1,193},{65,1},{129,65},{193,129... | collective-permute-start | bytes 196616 | tf_op jit(solution)/shard_map/ppermute | solution.py:43
  42.9 5.0 %collective-permute-start.4 = (bf16[256,128]{1,0:T(8,128)(2,1)S(1)}, bf16[256,128]{1,0:T(8,128)(2,1)S(1)}, u32[]{:S(2)}, u32[]{:S(2)}) collective-permute-start(bf16[256,128]{1,0:T(8,128)(2,1)S(1)} %get-tuple-element.52), channel_id=1, source_target_pairs={{0,64},{64,128},{128,192},{192,0},{1,65},{65,129},{129,193},{193,1... | collective-permute-start | bytes 196616 | tf_op jit(solution)/shard_map/ppermute | solution.py:43
  48.0 3.3 %collective-permute-start.14 = (bf16[512,128]{1,0:T(8,128)(2,1)S(1)}, bf16[512,128]{1,0:T(8,128)(2,1)S(1)}, u32[]{:S(2)}, u32[]{:S(2)}) collective-permute-start(bf16[512,128]{1,0:T(8,128)(2,1)S(1)} %pad_maximum_fusion.1), channel_id=1, source_target_pairs={{0,8},{8,0},{1,9},{9,1},{2,10},{10,2},{3,11},{11,3},{4,12},{12,4},... | collective-permute-start | bytes 393224 | tf_op jit(solution)/shard_map/ppermute | solution.py:121
  101.9 16.9 %all-to-all-start.3 = ((f32[16,152,128]{2,1,0:T(8,128)}), f32[16,152,128]{2,1,0:T(8,128)S(1)}, u32[]{:S(2)}, u32[]{:S(2)}) async-start(f32[16,152,128]{2,1,0:T(8,128)} %bitcast.14), calls=%async_computation.3 | async-start | bytes 2490368 | tf_op jit(solution)/shard_map/all_to_all | solution.py:345
  118.8 10.4 %collective-permute-start.15 = (f32[2432,128]{1,0:T(8,128)S(1)}, f32[2432,128]{1,0:T(8,128)S(1)}, u32[]{:S(2)}, u32[]{:S(2)}) collective-permute-start(f32[2432,128]{1,0:T(8,128)S(1)} %bitcast.33), channel_id=1, source_target_pairs={{0,8},{8,0},{1,9},{9,1},{2,10},{10,2},{3,11},{11,3},{4,12},{12,4},... | collective-permute-start | bytes 3735560 | tf_op jit(solution)/shard_map/ppermute | solution.py:371
  136.1 13.5 %all-to-all-start.4 = ((f32[16,32,128]{2,1,0:T(8,128)}), f32[16,32,128]{2,1,0:T(8,128)S(1)}, u32[]{:S(2)}, u32[]{:S(2)}) async-start(f32[16,32,128]{2,1,0:T(8,128)} %get-tuple-element.37), calls=%async_computation.4 | async-start | bytes 524288 | tf_op jit(solution)/shard_map/all_to_all | solution.py:373
  149.6 2.2 %copy-start.3 = (bf16[1024,2048]{1,0:T(8,128)(2,1)S(1)}, bf16[1024,2048]{1,0:T(8,128)(2,1)}, u32[]{:S(2)}) copy-start(bf16[1024,2048]{1,0:T(8,128)(2,1)} %shard_map.76.corrected_ref) | copy-start | bytes 12582916

commit v4 on v3

--- a/solution.py
+++ b/solution.py
@@ -218,7 +218,7 @@
     return inverse, dot(inverse, left, ((1,), (0,)), lax.Precision.HIGHEST)
 
 
-def iterate_kernel(core, own_table, other_table, own_ref, other_ref, total_ref, last_ref, spread_ref, high, low, left_ref):
+def iterate_kernel(core, own_table, other_table, own_ref, other_ref, total_ref, near_ref, across_ref, last_ref, spread_ref, high, low, left_ref):
     half = ROWS // 2
     high_scale = 1.0 / REPLICAS**2
     for table, blocks, place in ((own_table, own_ref, core[0]), (other_table, other_ref, 1 - core[0])):
@@ -239,22 +239,27 @@
         pbt = basis.astype(jnp.bfloat16)
         left = dot(pbt, high[...], ((1,), (0,))) + dot(pbt, low[...], ((1,), (0,)))
     last_ref[...] = left
-    total = total_ref[...].astype(jnp.float32)
-    spread = dot(left, total, ((1,), (0,)), lax.Precision.HIGHEST) / REPLICAS
-    for p in range(spread_ref.shape[0]):
-        spread_ref[p] = spread
-
-
-def iterate(core, own_table, other_table, own, other, total):
+    left_ref[...] = left
+
+    def product(part, columns_ref):
+        return dot(part, columns_ref.astype(jnp.float32), ((1,), (0,)), lax.Precision.HIGHEST)
+
+    spread_ref[0] = product(left, total_ref[...]) / REPLICAS
+    halves = [left_ref[:, pl.ds(pl.multiple_of(side * half, half), half)] for side in (core[0], 1 - core[0])]
+    for k in range(near_ref.shape[0]):
+        spread_ref[k + 1] = (product(halves[0], near_ref[k]) + product(halves[1], across_ref[k])) / REPLICAS
+
+
+def iterate(core, own_table, other_table, own, other, total, near, across):
     smem = pl.BlockSpec(memory_space=pltpu.SMEM)
     vmem = pl.BlockSpec(memory_space=pltpu.VMEM)
     return pl.pallas_call(
         iterate_kernel,
         out_shape=(
             jax.ShapeDtypeStruct((RANK, ROWS), jnp.float32),
-            jax.ShapeDtypeStruct((16, RANK, TILE), jnp.float32),
+            jax.ShapeDtypeStruct((4, RANK, TILE), jnp.float32),
         ),
-        in_specs=[smem] * 3 + [vmem] * 3,
+        in_specs=[smem] * 3 + [vmem] * 5,
         out_specs=(vmem, vmem),
         scratch_shapes=[
             pltpu.VMEM((ROWS, ROWS), jnp.bfloat16),
@@ -262,7 +267,7 @@
             pltpu.VMEM((RANK, ROWS), jnp.float32),
         ],
         compiler_params=pltpu.CompilerParams(vmem_limit_bytes=14 * MIB),
-    )(core, own_table, other_table, own, other, total)
+    )(core, own_table, other_table, own, other, total, near, across)
 
 
 def last_kernel(left_ref, inverse_ref, basis_ref):
@@ -302,14 +307,17 @@
     )(grad, error)
 
 
-def finish_kernel(inverse_ref, spread_ref, pbt_ref, corrected_ref, factor_ref, out_ref, wide, qbt):
-    blocks, _, width = spread_ref.shape
+def finish_kernel(place, inverse_ref, *refs):
+    *spread_refs, pbt_ref, corrected_ref, factor_ref, out_ref, wide, qbt = refs
     step = pl.program_id(0)
 
     @pl.when(step == 0)
     def _():
-        for b in range(blocks):
-            wide[:, b * width : (b + 1) * width] = spread_ref[b]
+        for d, spread_ref in enumerate(spread_refs):
+            blocks, _, width = spread_ref.shape
+            for k in range(blocks):
+                block = lax.rem(place[0] + 4 - d, 4) * blocks + lax.rem(place[1] + blocks - k, blocks)
+                wide[:, pl.ds(pl.multiple_of(block * width, width), width)] = spread_ref[k]
         right = dot(inverse_ref[...], wide[...], ((1,), (0,)), lax.Precision.HIGHEST)
         factor_ref[...] = right / math.sqrt(ROWS)
         qbt[...] = right.astype(jnp.bfloat16)
@@ -320,7 +328,7 @@
     out_ref[...] = (corrected.astype(jnp.float32) - approx).astype(jnp.bfloat16)
 
 
-def finish(inverse, spread, pbt, corrected):
+def finish(place, inverse, spreads, pbt, corrected):
     vmem = pl.BlockSpec(memory_space=pltpu.VMEM)
     cols = corrected.shape[1]
     rows = 2 * TILE
@@ -331,14 +339,16 @@
             jax.ShapeDtypeStruct((ROWS, cols), jnp.bfloat16),
         ),
         grid=(ROWS // rows,),
-        in_specs=[vmem, vmem, pl.BlockSpec((RANK, rows), lambda i: (0, i)), vmem],
+        in_specs=[pl.BlockSpec(memory_space=pltpu.SMEM), vmem]
+        + [vmem] * len(spreads)
+        + [pl.BlockSpec((RANK, rows), lambda i: (0, i)), vmem],
         out_specs=(pl.BlockSpec((RANK, cols), lambda i: (0, 0)), pl.BlockSpec((rows, cols), lambda i: (i, 0))),
         scratch_shapes=[pltpu.VMEM((RANK, cols), jnp.float32), pltpu.VMEM((RANK, cols), jnp.bfloat16)],
         compiler_params=pltpu.CompilerParams(vmem_limit_bytes=16 * MIB),
-    )(inverse, spread, pbt, corrected)
-
-
-def sum_chips(value):
+    )(place, inverse, *spreads, pbt, corrected)
+
+
+def sum_chips(value, later):
     rows = RING_SIZE * SLOTS
 
     def swap(v, axes, size):
@@ -351,7 +361,8 @@
 
     part = small_kernel(sum_kernel, rows, swap(value, PLANE, PLANE_SIZE))
     part = ring(small_kernel(ring_kernel, rows, ring(part)))
-    return swap(small_kernel(sum_kernel, PLANE_SIZE * rows, part), PLANE, PLANE_SIZE)
+    part, later = lax.optimization_barrier((part, later))
+    return swap(small_kernel(sum_kernel, PLANE_SIZE * rows, part), PLANE, PLANE_SIZE), later
 
 
 def shards(grad, error, q_init):
@@ -367,12 +378,17 @@
     packed = pack(own_table, which, total, qt)
     grad, error, packed = lax.optimization_barrier((grad, error, packed))
     corrected = corrected_sum(grad[0], error[0])
-    own, corrected = lax.optimization_barrier((sum_chips(packed), corrected))
+    own, mine = sum_chips(packed, mine)
+    near = {d: lax.ppermute(mine, "zl", shift(4, d)) for d in (1, 3, 2)}
+    near = jnp.stack([near[1], near[2], near[3]])
+    own, corrected, near = lax.optimization_barrier((own, corrected, near))
+    across = lax.ppermute(near, "c", SWAP)
     other = lax.ppermute(own, "c", SWAP)
-    left, spread = iterate(which, own_table, other_table, own, other, total)
-    spread = lax.all_to_all(spread, ("y", "zl"), 0, 0, tiled=True)
+    left, spread = iterate(which, own_table, other_table, own, other, total, near, across)
+    spreads = {d: lax.ppermute(spread, "y", shift(4, d)) for d in (1, 3, 2)}
+    spreads = [spread, spreads[1], spreads[2], spreads[3]]
     inverse, basis = last_basis(left)
-    factor, new_error = finish(inverse, spread, basis.astype(jnp.bfloat16), corrected)
+    factor, new_error = finish(jnp.stack([y, zl]), inverse, spreads, basis.astype(jnp.bfloat16), corrected)
     own_rows = ROWS // 256
     start = lax.axis_index(("zl", "y", "c", "x", "zh")) * own_rows
     own_basis = lax.dynamic_slice(basis, (0, start), (RANK, own_rows)).T

time: 156 us -> 148 us (0.949)
  waiting for transfers between devices: 38.6 us -> 26 us
  starting transfers between devices: 32.5 us -> 38 us
    all_to_all x1 -> x0, waiting for transfers between devices: 7.79 us -> none  [shards(): spread = lax.all_to_all(spread, ('y', 'zl'), 0, 0, tiled=True)]
    ppermute x0 -> x7, waiting for transfers between devices: none -> 6.35 us  [the longest x1 2.95 us: shards(): across = lax.ppermute(near, 'c', SWAP)]
    ppermute x6, starting transfers between devices: 5.92 us -> 12.2 us  [exchange_sum(): total = total + lax.ppermute(sent, axis, shift(n, d)).astype(jnp.float32)]
    ppermute x6, waiting for transfers between devices: 15.5 us -> 10.3 us  [reduce_replicas(): lax.ppermute(others[d - 1], 'y', shift(4, d)).astype(jnp.float32)]
    ppermute x0 -> x7, starting transfers between devices: none -> 3.69 us  [the longest x3 2.14 us: shards(): spreads = {d: lax.ppermute(spread, 'y', shift(4, d)) for d in (1, 3, 2)}]
    all_to_all x1 -> x0, starting transfers between devices: 3.53 us -> none  [shards(): spread = lax.all_to_all(spread, ('y', 'zl'), 0, 0, tiled=True)]
    all_to_all x1, waiting for transfers between devices: 6.94 us -> 4.12 us  [swap(): v = lax.all_to_all(v.reshape(size, rows, TILE), axes, 0, 0, tiled=True)]
    ppermute x1, waiting for transfers between devices: 2.47 us -> 0.01 us  [shards(): other = lax.ppermute(own, 'c', SWAP)]
  transfers between devices with their start and end apart: 18 -> 24, of which waited for: 13 -> 13; matrix products, arithmetic and copies ran while one was open for 2% -> 2% of each run, Pallas kernels for 8% -> 8%
where the time goes in v4:
time: 148 us
  blocking collectives  46.5 us (31%)
  starting transfers between devices  38 us (26%)
  Pallas kernels  27 us (18%)
  waiting for transfers between devices  26 us (18%)
  local copies, waits for them, and re-layouts  7.53 us (5%)
  other arithmetic  1.85 us (1%)
    all_to_all x2, blocking collectives, ring(): lax.all_to_all(v.reshape(RING_SIZE, SLOTS, 1, TILE), RING, 0, 0, tiled=True)  23.3 us
    all_to_all x1, blocking collectives, swap(): v = lax.all_to_all(v.reshape(size, rows, TILE), axes, 0, 0, tiled=True)  23.2 us
    ppermute x6, starting transfers between devices, exchange_sum(): total = total + lax.ppermute(sent, axis, shift(n, d)).astype(jnp.float32)  12.2 us
    ppermute x6, waiting for transfers between devices, reduce_replicas(): lax.ppermute(others[d - 1], 'y', shift(4, d)).astype(jnp.float32)  10.3 us
    ppermute x1, starting transfers between devices, shards(): other = lax.ppermute(own, 'c', SWAP)  7.82 us
    unnamed x11, local copies, waits for them, and re-layouts  7.23 us
    pallas_call x1, Pallas kernels, iterate(): pl.pallas_call(iterate_kernel, out_shape=(jax.ShapeDtypeStruct((RANK, ROW...  6.97 us
    pallas_call x1, Pallas kernels, corrected_sum(): pl.pallas_call(corrected_kernel, out_shape=jax.ShapeDtypeStruct(grad.shap...  6 us
  transfers between devices with their start and end apart: 24, of which 13 were waited for; matrix products, arithmetic and copies ran while one was open for 2% of the time, Pallas kernels for 8%

profile of v4, /device:TPU:1, one launch (start us, length us, event | category | flops | bytes accessed | tf_op | source)
XLA Modules:
  0.0 147.7 jit_solution(7291215406366541759)
XLA Ops:
  0.7 2.2 %copy-done.1 = bf16[1,1024,2048]{2,1,0:T(8,128)(2,1)S(1)} copy-done((bf16[1,1024,2048]{2,1,0:T(8,128)(2,1)S(1)}, bf16[1,1024,2048]{2,1,0:T(8,128)(2,1)}, u32[]{:S(2)}) %copy-start.1) | copy-done | bytes 4194328
  2.9 2.2 %copy-done.2 = bf16[1,1024,2048]{2,1,0:T(8,128)(2,1)S(1)} copy-done((bf16[1,1024,2048]{2,1,0:T(8,128)(2,1)S(1)}, bf16[1,1024,2048]{2,1,0:T(8,128)(2,1)}, u32[]{:S(2)}) %copy-start.2) | copy-done | bytes 4194328
  5.1 0.8 shard_map.70
  5.9 3.3 %collective-permute-start.7 = (bf16[256,2048]{1,0:T(8,128)(2,1)S(1)}, bf16[256,2048]{1,0:T(8,128)(2,1)S(1)}, u32[]{:S(2)}, u32[]{:S(2)}) collective-permute-start(bf16[256,2048]{1,0:T(8,128)(2,1)S(1)} %shard_map.70), channel_id=1, source_target_pairs={{0,8},{8,0},{1,9},{9,1},{2,10},{10,2},{3,11},{11,3},{4,12},{12,4},... | collective-permute-start | bytes 3145736 | tf_op jit(solution)/shard_map/ppermute | solution.py:106
  9.3 0.8 shard_map.68
  10.2 1.1 shard_map.67.own_ref
  11.3 0.2 collective-permute-done.7.got_ref
  11.6 1.5 %shard_map.71 = (bf16[256,512]{1,0:T(8,128)(2,1)S(1)}, bf16[256,512]{1,0:T(8,128)(2,1)}, bf16[256,512]{1,0:T(8,128)(2,1)}, bf16[256,512]{1,0:T(8,128)(2,1)}) custom-call(s32[3]{0:T(128)S(1)} %pad_add_fusion.place, bf16[512,2048]{1,0:T(8,128)(2,1)S(1)} %shard_map.67.own_ref, bf16[256,2048]{1,0:T(8,128)(2,1)S(1)} %collective-permute-done.7.got_ref), custom_call_target="tpu_custom_call" | custom-call | flops 524288 | bytes 3145728 | tf_op jit(solution)/shard_map/pallas_call | solution.py:87
  13.1 2.7 %collective-permute-start.9 = (bf16[256,512]{1,0:T(8,128)(2,1)}, bf16[256,512]{1,0:T(8,128)(2,1)}, u32[]{:S(2)}, u32[]{:S(2)}) collective-permute-start(bf16[256,512]{1,0:T(8,128)(2,1)} %get-tuple-element.31), channel_id=1, source_target_pairs={{0,48},{16,0},{32,16},{48,32},{1,49},{17,1},{33,17},{49,33},{2,50}... | collective-permute-start | bytes 786440 | tf_op jit(solution)/shard_map/ppermute | solution.py:113
  15.8 1.5 %shard_map.69 = (bf16[256,512]{1,0:T(8,128)(2,1)S(1)}, bf16[256,512]{1,0:T(8,128)(2,1)S(1)}, bf16[256,512]{1,0:T(8,128)(2,1)S(1)}, bf16[256,512]{1,0:T(8,128)(2,1)S(1)}) custom-call(s32[3]{0:T(128)S(1)} %pad_add_fusion.place, bf16[512,2048]{1,0:T(8,128)(2,1)S(1)} %shard_map.67.own_ref, bf16[256,2048]{1,0:T(8,128)(2,1)} %collective-permute-done.got_ref), custom_call_target="tpu_custom_call" | custom-call | flops 524288 | bytes 3145728 | tf_op jit(solution)/shard_map/pallas_call | solution.py:87
  17.3 0.7 collective-permute-start.1
  17.9 2.1 %collective-permute-start.2 = (bf16[256,512]{1,0:T(8,128)(2,1)S(1)}, bf16[256,512]{1,0:T(8,128)(2,1)S(1)}, u32[]{:S(2)}, u32[]{:S(2)}) collective-permute-start(bf16[256,512]{1,0:T(8,128)(2,1)S(1)} %get-tuple-element.27), channel_id=1, source_target_pairs={{0,48},{16,0},{32,16},{48,32},{1,49},{17,1},{33,17},{49,33},{2,50}... | collective-permute-start | bytes 786440 | tf_op jit(solution)/shard_map/ppermute | solution.py:113
  20.0 2.6 %collective-permute-done.8 = bf16[256,512]{1,0:T(8,128)(2,1)} collective-permute-done((bf16[256,512]{1,0:T(8,128)(2,1)}, bf16[256,512]{1,0:T(8,128)(2,1)}, u32[]{:S(2)}, u32[]{:S(2)}) %collective-permute-start.8) | collective-permute-done | bytes 262176 | tf_op jit(solution)/shard_map/ppermute | solution.py:113
  22.6 4.7 %collective-permute-done.10 = bf16[256,512]{1,0:T(8,128)(2,1)} collective-permute-done((bf16[256,512]{1,0:T(8,128)(2,1)}, bf16[256,512]{1,0:T(8,128)(2,1)}, u32[]{:S(2)}, u32[]{:S(2)}) %collective-permute-start.10) | collective-permute-done | bytes 262176 | tf_op jit(solution)/shard_map/ppermute | solution.py:113
  27.3 1.3 add_convert_fusion
  28.6 1.7 %collective-permute-start.11 = (bf16[256,128]{1,0:T(8,128)(2,1)S(1)}, bf16[256,128]{1,0:T(8,128)(2,1)S(1)}, u32[]{:S(2)}, u32[]{:S(2)}) collective-permute-start(bf16[256,128]{1,0:T(8,128)(2,1)S(1)} %get-tuple-element.61), channel_id=1, source_target_pairs={{0,64},{64,128},{128,192},{192,0},{1,65},{65,129},{129,193},{193,1... | collective-permute-start | bytes 196616 | tf_op jit(solution)/shard_map/ppermute | solution.py:43
  30.3 3.0 %collective-permute-start.13 = (bf16[256,128]{1,0:T(8,128)(2,1)S(1)}, bf16[256,128]{1,0:T(8,128)(2,1)S(1)}, u32[]{:S(2)}, u32[]{:S(2)}) collective-permute-start(bf16[256,128]{1,0:T(8,128)(2,1)S(1)} %get-tuple-element.62), channel_id=1, source_target_pairs={{0,128},{64,192},{128,0},{192,64},{1,129},{65,193},{129,1},{193,65... | collective-permute-start | bytes 196616 | tf_op jit(solution)/shard_map/ppermute | solution.py:43
  33.3 0.4 collective-permute-done.1
  33.7 2.0 %collective-permute-start.12 = (bf16[256,128]{1,0:T(8,128)(2,1)S(1)}, bf16[256,128]{1,0:T(8,128)(2,1)S(1)}, u32[]{:S(2)}, u32[]{:S(2)}) collective-permute-start(bf16[256,128]{1,0:T(8,128)(2,1)S(1)} %get-tuple-element.63), channel_id=1, source_target_pairs={{0,192},{64,0},{128,64},{192,128},{1,193},{65,1},{129,65},{193,129... | collective-permute-start | bytes 196616 | tf_op jit(solution)/shard_map/ppermute | solution.py:43
  35.7 2.7 %collective-permute-done.3 = bf16[256,512]{1,0:T(8,128)(2,1)S(1)} collective-permute-done((bf16[256,512]{1,0:T(8,128)(2,1)S(1)}, bf16[256,512]{1,0:T(8,128)(2,1)S(1)}, u32[]{:S(2)}, u32[]{:S(2)}) %collective-permute-start.3) | collective-permute-done | bytes 262176 | tf_op jit(solution)/shard_map/ppermute | solution.py:113
  38.6 1.7 %collective-permute-start.4 = (bf16[256,128]{1,0:T(8,128)(2,1)S(1)}, bf16[256,128]{1,0:T(8,128)(2,1)S(1)}, u32[]{:S(2)}, u32[]{:S(2)}) collective-permute-start(bf16[256,128]{1,0:T(8,128)(2,1)S(1)} %get-tuple-element.58), channel_id=1, source_target_pairs={{0,64},{64,128},{128,192},{192,0},{1,65},{65,129},{129,193},{193,1... | collective-permute-start | bytes 196616 | tf_op jit(solution)/shard_map/ppermute | solution.py:43
  40.3 3.0 %collective-permute-start.6 = (bf16[256,128]{1,0:T(8,128)(2,1)S(1)}, bf16[256,128]{1,0:T(8,128)(2,1)S(1)}, u32[]{:S(2)}, u32[]{:S(2)}) collective-permute-start(bf16[256,128]{1,0:T(8,128)(2,1)S(1)} %get-tuple-element.59), channel_id=1, source_target_pairs={{0,128},{64,192},{128,0},{192,64},{1,129},{65,193},{129,1},{193,65... | collective-permute-start | bytes 196616 | tf_op jit(solution)/shard_map/ppermute | solution.py:43
  43.3 0.7 collective-permute-start.5
  44.1 0.6 collective-permute-done.4
  44.7 3.4 %collective-permute-done.6 = bf16[256,128]{1,0:T(8,128)(2,1)S(1)} collective-permute-done((bf16[256,128]{1,0:T(8,128)(2,1)S(1)}, bf16[256,128]{1,0:T(8,128)(2,1)S(1)}, u32[]{:S(2)}, u32[]{:S(2)}) %collective-permute-start.6) | collective-permute-done | bytes 65568 | tf_op jit(solution)/shard_map/ppermute | solution.py:43
  48.2 1.5 %collective-permute-start.14 = (bf16[512,128]{1,0:T(8,128)(2,1)S(1)}, bf16[512,128]{1,0:T(8,128)(2,1)S(1)}, u32[]{:S(2)}, u32[]{:S(2)}) collective-permute-start(bf16[512,128]{1,0:T(8,128)(2,1)S(1)} %pad_maximum_fusion.2), channel_id=1, source_target_pairs={{0,8},{8,0},{1,9},{9,1},{2,10},{10,2},{3,11},{11,3},{4,12},{12,4},... | collective-permute-start | bytes 393224 | tf_op jit(solution)/shard_map/ppermute | solution.py:121
  49.9 0.9 collective-permute-done.14
  50.9 1.3 shard_map.72
  52.2 23.2 %all_to_all.20 = f32[16,152,128]{2,1,0:T(8,128)S(1)} all-to-all(f32[16,152,128]{2,1,0:T(8,128)S(1)} %bitcast.37), channel_id=1, replica_groups=mesh['zl'=4,'y'=4,'c'=2,'x'=4,'zh'=2] {'x','y'}, dimensions={0} | all-to-all | bytes 2490368 | tf_op jit(solution)/shard_map/all_to_all | solution.py:355
  75.5 13.6 %all_to_all.21 = f32[8,19,1,128]{3,2,1,0:T(1,128)S(1)} all-to-all(f32[8,19,1,128]{3,2,1,0:T(1,128)S(1)} %bitcast.41), channel_id=1, replica_groups=mesh['zl'=4,'y'=4,'c'=2,'x'=4,'zh'=2] {'zh','zl'}, dimensions={0} | all-to-all | bytes 155648 | tf_op jit(solution)/shard_map/all_to_all | solution.py:359
  89.1 9.7 %all_to_all.22 = f32[8,19,1,128]{3,2,1,0:T(1,128)S(1)} all-to-all(f32[8,19,1,128]{3,2,1,0:T(1,128)S(1)} %bitcast.44), channel_id=1, replica_groups=mesh['zl'=4,'y'=4,'c'=2,'x'=4,'zh'=2] {'zh','zl'}, dimensions={0} | all-to-all | bytes 155648 | tf_op jit(solution)/shard_map/all_to_all | solution.py:359
  98.8 1.1 shard_map.75
  99.9 3.9 %all-to-all-start.3 = ((f32[16,152,128]{2,1,0:T(8,128)}), f32[16,152,128]{2,1,0:T(8,128)S(1)}, u32[]{:S(2)}, u32[]{:S(2)}) async-start(f32[16,152,128]{2,1,0:T(8,128)} %bitcast.14), calls=%async_computation.3 | async-start | bytes 2490368 | tf_op jit(solution)/shard_map/all_to_all | solution.py:355
  103.9 0.2 collective-permute-start.17
  104.1 1.2 collective-permute-start.16
  105.4 6.0 %shard_map.76.refs_5_ = bf16[1024,2048]{1,0:T(8,128)(2,1)} custom-call(bf16[1024,2048]{1,0:T(8,128)(2,1)} %bitcast.29, bf16[1024,2048]{1,0:T(8,128)(2,1)} %bitcast.33), custom_call_target="tpu_custom_call" | custom-call | flops 1000 | bytes 1000 | tf_op jit(solution)/shard_map/pallas_call | solution.py:299
  111.4 1.2 collective-permute-done.16
  112.7 4.1 %all-to-all-done.3 = f32[16,152,128]{2,1,0:T(8,128)S(1)} async-done(((f32[16,152,128]{2,1,0:T(8,128)}), f32[16,152,128]{2,1,0:T(8,128)S(1)}, u32[]{:S(2)}, u32[]{:S(2)}) %all-to-all-start.3) | async-done | bytes 1245216 | tf_op jit(solution)/shard_map/all_to_all | solution.py:355
  116.8 7.8 %collective-permute-start.18 = (f32[2432,128]{1,0:T(8,128)S(1)}, f32[2432,128]{1,0:T(8,128)S(1)}, u32[]{:S(2)}, u32[]{:S(2)}) collective-permute-start(f32[2432,128]{1,0:T(8,128)S(1)} %bitcast.39), channel_id=1, source_target_pairs={{0,8},{8,0},{1,9},{9,1},{2,10},{10,2},{3,11},{11,3},{4,12},{12,4},... | collective-permute-start | bytes 3735560 | tf_op jit(solution)/shard_map/ppermute | solution.py:386
  124.8 3.0 %collective-permute-done.19.across_ref = bf16[3,512,128]{2,1,0:T(8,128)(2,1)} collective-permute-done((bf16[3,512,128]{2,1,0:T(8,128)(2,1)S(1)}, bf16[3,512,128]{2,1,0:T(8,128)(2,1)}, u32[]{:S(2)}, u32[]{:S(2)}) %collective-permute-start.19) | collective-permute-done | bytes 393248 | tf_op jit(solution)/shard_map/ppermute | solution.py:385
  127.8 7.0 %shard_map.77 = (f32[32,1024]{1,0:T(8,128)S(1)}, f32[4,32,128]{2,1,0:T(8,128)S(1)}) custom-call(s32[1]{0:T(128)} %bitcast.core, s32[18,2]{1,0:T(8,128)S(1)} %copy.18.table.own_table, s32[18,2]{1,0:T(8,128)S(1)} %copy.19.other_table, f32[2432,128]{1,0:T(8,128)S(1)} %bitcast.40, f32[2432,128]{1,0:T(8,128)S(1)} %collective-permute-done.18.other_ref, ...), custom_call_target="tpu_custom_call" | custom-call | tf_op jit(solution)/shard_map/pallas_call | solution.py:256
  134.8 2.1 %collective-permute-start.21 = (f32[4,32,128]{2,1,0:T(8,128)S(1)}, f32[4,32,128]{2,1,0:T(8,128)S(1)}, u32[]{:S(2)}, u32[]{:S(2)}) collective-permute-start(f32[4,32,128]{2,1,0:T(8,128)S(1)} %get-tuple-element.43.refs_0_), channel_id=1, source_target_pairs={{0,32},{16,48},{32,0},{48,16},{1,33},{17,49},{33,1},{49,17},{2,34}... | collective-permute-start | bytes 196616 | tf_op jit(solution)/shard_map/ppermute | solution.py:388
  136.9 1.4 shard_map.78
  138.4 0.7 copy.20
  139.0 0.5 collective-permute-done.21.refs_2_
  139.5 1.7 %collective-permute-done.20.refs_1_ = f32[4,32,128]{2,1,0:T(8,128)S(1)} collective-permute-done((f32[4,32,128]{2,1,0:T(8,128)S(1)}, f32[4,32,128]{2,1,0:T(8,128)S(1)}, u32[]{:S(2)}, u32[]{:S(2)}) %collective-permute-start.20) | collective-permute-done | bytes 65568 | tf_op jit(solution)/shard_map/ppermute | solution.py:388
  141.2 2.2 %copy-done.3 = bf16[1024,2048]{1,0:T(8,128)(2,1)S(1)} copy-done((bf16[1024,2048]{1,0:T(8,128)(2,1)S(1)}, bf16[1024,2048]{1,0:T(8,128)(2,1)}, u32[]{:S(2)}) %copy-start.3) | copy-done | bytes 4194328
  143.4 4.3 %shard_map.79 = (f32[32,2048]{1,0:T(8,128)}, bf16[1024,2048]{1,0:T(8,128)(2,1)}) custom-call(s32[2]{0:T(128)S(1)} %pad_add_fusion.1.place, f32[32,32]{1,0:T(8,128)S(1)} %get-tuple-element.42.inverse_ref, f32[4,32,128]{2,1,0:T(8,128)S(1)} %get-tuple-element.43.refs_0_, f32[4,32,128]{2,1,0:T(8,128)S(1)} %collective-permute-done.20.refs_1_, ...), custom_call_target="tpu_custom_call" | custom-call | tf_op jit(solution)/shard_map/pallas_call | solution.py:335
  (45 shorter events, 1.3 us)
Async XLA Ops:
  0.6 49.3 %copy-start = (bf16[2048,32]{0,1:T(8,128)(2,1)S(1)}, bf16[2048,32]{0,1:T(8,128)(2,1)}, u32[]{:S(2)}) copy-start(bf16[2048,32]{0,1:T(8,128)(2,1)} %param.6) | copy-start | bytes 393220
  0.7 2.2 %copy-start.1 = (bf16[1,1024,2048]{2,1,0:T(8,128)(2,1)S(1)}, bf16[1,1024,2048]{2,1,0:T(8,128)(2,1)}, u32[]{:S(2)}) copy-start(bf16[1,1024,2048]{2,1,0:T(8,128)(2,1)} %param.4) | copy-start | bytes 12582916
  2.9 2.2 %copy-start.2 = (bf16[1,1024,2048]{2,1,0:T(8,128)(2,1)S(1)}, bf16[1,1024,2048]{2,1,0:T(8,128)(2,1)}, u32[]{:S(2)}) copy-start(bf16[1,1024,2048]{2,1,0:T(8,128)(2,1)} %param.5) | copy-start | bytes 12582916
  5.9 5.6 %collective-permute-start.7 = (bf16[256,2048]{1,0:T(8,128)(2,1)S(1)}, bf16[256,2048]{1,0:T(8,128)(2,1)S(1)}, u32[]{:S(2)}, u32[]{:S(2)}) collective-permute-start(bf16[256,2048]{1,0:T(8,128)(2,1)S(1)} %shard_map.70), channel_id=1, source_target_pairs={{0,8},{8,0},{1,9},{9,1},{2,10},{10,2},{3,11},{11,3},{4,12},{12,4},... | collective-permute-start | bytes 3145736 | tf_op jit(solution)/shard_map/ppermute | solution.py:106
  10.1 5.7 %collective-permute-start = (bf16[256,2048]{1,0:T(8,128)(2,1)S(1)}, bf16[256,2048]{1,0:T(8,128)(2,1)}, u32[]{:S(2)}, u32[]{:S(2)}) collective-permute-start(bf16[256,2048]{1,0:T(8,128)(2,1)S(1)} %shard_map.68), channel_id=1, source_target_pairs={{0,8},{8,0},{1,9},{9,1},{2,10},{10,2},{3,11},{11,3},{4,12},{12,4},... | collective-permute-start | bytes 3145736 | tf_op jit(solution)/shard_map/ppermute | solution.py:106
  13.1 9.5 %collective-permute-start.8 = (bf16[256,512]{1,0:T(8,128)(2,1)}, bf16[256,512]{1,0:T(8,128)(2,1)}, u32[]{:S(2)}, u32[]{:S(2)}) collective-permute-start(bf16[256,512]{1,0:T(8,128)(2,1)} %get-tuple-element.30), channel_id=1, source_target_pairs={{0,16},{16,32},{32,48},{48,0},{1,17},{17,33},{33,49},{49,1},{2,18}... | collective-permute-start | bytes 786440 | tf_op jit(solution)/shard_map/ppermute | solution.py:113
  13.1 9.5 %collective-permute-start.9 = (bf16[256,512]{1,0:T(8,128)(2,1)}, bf16[256,512]{1,0:T(8,128)(2,1)}, u32[]{:S(2)}, u32[]{:S(2)}) collective-permute-start(bf16[256,512]{1,0:T(8,128)(2,1)} %get-tuple-element.31), channel_id=1, source_target_pairs={{0,48},{16,0},{32,16},{48,32},{1,49},{17,1},{33,17},{49,33},{2,50}... | collective-permute-start | bytes 786440 | tf_op jit(solution)/shard_map/ppermute | solution.py:113
  15.8 11.5 %collective-permute-start.10 = (bf16[256,512]{1,0:T(8,128)(2,1)}, bf16[256,512]{1,0:T(8,128)(2,1)}, u32[]{:S(2)}, u32[]{:S(2)}) collective-permute-start(bf16[256,512]{1,0:T(8,128)(2,1)} %get-tuple-element.32), channel_id=1, source_target_pairs={{0,32},{16,48},{32,0},{48,16},{1,33},{17,49},{33,1},{49,17},{2,34}... | collective-permute-start | bytes 786440 | tf_op jit(solution)/shard_map/ppermute | solution.py:113
  17.3 16.4 %collective-permute-start.1 = (bf16[256,512]{1,0:T(8,128)(2,1)S(1)}, bf16[256,512]{1,0:T(8,128)(2,1)S(1)}, u32[]{:S(2)}, u32[]{:S(2)}) collective-permute-start(bf16[256,512]{1,0:T(8,128)(2,1)S(1)} %get-tuple-element.26), channel_id=1, source_target_pairs={{0,16},{16,32},{32,48},{48,0},{1,17},{17,33},{33,49},{49,1},{2,18}... | collective-permute-start | bytes 786440 | tf_op jit(solution)/shard_map/ppermute | solution.py:113
  17.9 17.8 %collective-permute-start.2 = (bf16[256,512]{1,0:T(8,128)(2,1)S(1)}, bf16[256,512]{1,0:T(8,128)(2,1)S(1)}, u32[]{:S(2)}, u32[]{:S(2)}) collective-permute-start(bf16[256,512]{1,0:T(8,128)(2,1)S(1)} %get-tuple-element.27), channel_id=1, source_target_pairs={{0,48},{16,0},{32,16},{48,32},{1,49},{17,1},{33,17},{49,33},{2,50}... | collective-permute-start | bytes 786440 | tf_op jit(solution)/shard_map/ppermute | solution.py:113
  22.6 15.8 %collective-permute-start.3 = (bf16[256,512]{1,0:T(8,128)(2,1)S(1)}, bf16[256,512]{1,0:T(8,128)(2,1)S(1)}, u32[]{:S(2)}, u32[]{:S(2)}) collective-permute-start(bf16[256,512]{1,0:T(8,128)(2,1)S(1)} %get-tuple-element.28), channel_id=1, source_target_pairs={{0,32},{16,48},{32,0},{48,16},{1,33},{17,49},{33,1},{49,17},{2,34}... | collective-permute-start | bytes 786440 | tf_op jit(solution)/shard_map/ppermute | solution.py:113
  27.3 22.5 %copy-start.4 = (s32[2,18,2]{1,2,0:T(2,128)S(1)}, s32[2,18,2]{1,2,0:T(2,128)}, u32[]{:S(2)}) copy-start(s32[2,18,2]{1,2,0:T(2,128)} %constant.60.clone) | copy-start | bytes 868
  28.6 14.7 %collective-permute-start.11 = (bf16[256,128]{1,0:T(8,128)(2,1)S(1)}, bf16[256,128]{1,0:T(8,128)(2,1)S(1)}, u32[]{:S(2)}, u32[]{:S(2)}) collective-permute-start(bf16[256,128]{1,0:T(8,128)(2,1)S(1)} %get-tuple-element.61), channel_id=1, source_target_pairs={{0,64},{64,128},{128,192},{192,0},{1,65},{65,129},{129,193},{193,1... | collective-permute-start | bytes 196616 | tf_op jit(solution)/shard_map/ppermute | solution.py:43
  30.3 13.7 %collective-permute-start.13 = (bf16[256,128]{1,0:T(8,128)(2,1)S(1)}, bf16[256,128]{1,0:T(8,128)(2,1)S(1)}, u32[]{:S(2)}, u32[]{:S(2)}) collective-permute-start(bf16[256,128]{1,0:T(8,128)(2,1)S(1)} %get-tuple-element.62), channel_id=1, source_target_pairs={{0,128},{64,192},{128,0},{192,64},{1,129},{65,193},{129,1},{193,65... | collective-permute-start | bytes 196616 | tf_op jit(solution)/shard_map/ppermute | solution.py:43
  33.7 10.4 %collective-permute-start.12 = (bf16[256,128]{1,0:T(8,128)(2,1)S(1)}, bf16[256,128]{1,0:T(8,128)(2,1)S(1)}, u32[]{:S(2)}, u32[]{:S(2)}) collective-permute-start(bf16[256,128]{1,0:T(8,128)(2,1)S(1)} %get-tuple-element.63), channel_id=1, source_target_pairs={{0,192},{64,0},{128,64},{192,128},{1,193},{65,1},{129,65},{193,129... | collective-permute-start | bytes 196616 | tf_op jit(solution)/shard_map/ppermute | solution.py:43
  38.6 6.2 %collective-permute-start.4 = (bf16[256,128]{1,0:T(8,128)(2,1)S(1)}, bf16[256,128]{1,0:T(8,128)(2,1)S(1)}, u32[]{:S(2)}, u32[]{:S(2)}) collective-permute-start(bf16[256,128]{1,0:T(8,128)(2,1)S(1)} %get-tuple-element.58), channel_id=1, source_target_pairs={{0,64},{64,128},{128,192},{192,0},{1,65},{65,129},{129,193},{193,1... | collective-permute-start | bytes 196616 | tf_op jit(solution)/shard_map/ppermute | solution.py:43
  40.3 7.8 %collective-permute-start.6 = (bf16[256,128]{1,0:T(8,128)(2,1)S(1)}, bf16[256,128]{1,0:T(8,128)(2,1)S(1)}, u32[]{:S(2)}, u32[]{:S(2)}) collective-permute-start(bf16[256,128]{1,0:T(8,128)(2,1)S(1)} %get-tuple-element.59), channel_id=1, source_target_pairs={{0,128},{64,192},{128,0},{192,64},{1,129},{65,193},{129,1},{193,65... | collective-permute-start | bytes 196616 | tf_op jit(solution)/shard_map/ppermute | solution.py:43
  43.3 4.9 %collective-permute-start.5 = (bf16[256,128]{1,0:T(8,128)(2,1)S(1)}, bf16[256,128]{1,0:T(8,128)(2,1)S(1)}, u32[]{:S(2)}, u32[]{:S(2)}) collective-permute-start(bf16[256,128]{1,0:T(8,128)(2,1)S(1)} %get-tuple-element.60), channel_id=1, source_target_pairs={{0,192},{64,0},{128,64},{192,128},{1,193},{65,1},{129,65},{193,129... | collective-permute-start | bytes 196616 | tf_op jit(solution)/shard_map/ppermute | solution.py:43
  48.2 2.5 %collective-permute-start.14 = (bf16[512,128]{1,0:T(8,128)(2,1)S(1)}, bf16[512,128]{1,0:T(8,128)(2,1)S(1)}, u32[]{:S(2)}, u32[]{:S(2)}) collective-permute-start(bf16[512,128]{1,0:T(8,128)(2,1)S(1)} %pad_maximum_fusion.2), channel_id=1, source_target_pairs={{0,8},{8,0},{1,9},{9,1},{2,10},{10,2},{3,11},{11,3},{4,12},{12,4},... | collective-permute-start | bytes 393224 | tf_op jit(solution)/shard_map/ppermute | solution.py:121
  99.9 16.9 %all-to-all-start.3 = ((f32[16,152,128]{2,1,0:T(8,128)}), f32[16,152,128]{2,1,0:T(8,128)S(1)}, u32[]{:S(2)}, u32[]{:S(2)}) async-start(f32[16,152,128]{2,1,0:T(8,128)} %bitcast.14), calls=%async_computation.3 | async-start | bytes 2490368 | tf_op jit(solution)/shard_map/all_to_all | solution.py:355
  103.9 7.6 %collective-permute-start.17 = (bf16[512,128]{1,0:T(8,128)(2,1)S(1)}, bf16[512,128]{1,0:T(8,128)(2,1)S(1)}, u32[]{:S(2)}, u32[]{:S(2)}) collective-permute-start(bf16[512,128]{1,0:T(8,128)(2,1)S(1)} %pad_maximum_fusion.2), channel_id=1, source_target_pairs={{0,192},{64,0},{128,64},{192,128},{1,193},{65,1},{129,65},{193,129... | collective-permute-start | bytes 393224 | tf_op jit(solution)/shard_map/ppermute | solution.py:382
  104.1 8.6 %collective-permute-start.16 = (bf16[512,128]{1,0:T(8,128)(2,1)S(1)}, bf16[512,128]{1,0:T(8,128)(2,1)S(1)}, u32[]{:S(2)}, u32[]{:S(2)}) collective-permute-start(bf16[512,128]{1,0:T(8,128)(2,1)S(1)} %pad_maximum_fusion.2), channel_id=1, source_target_pairs={{0,128},{64,192},{128,0},{192,64},{1,129},{65,193},{129,1},{193,65... | collective-permute-start | bytes 393224 | tf_op jit(solution)/shard_map/ppermute | solution.py:382
  105.3 7.3 %collective-permute-start.15 = (bf16[512,128]{1,0:T(8,128)(2,1)S(1)}, bf16[512,128]{1,0:T(8,128)(2,1)S(1)}, u32[]{:S(2)}, u32[]{:S(2)}) collective-permute-start(bf16[512,128]{1,0:T(8,128)(2,1)S(1)} %pad_maximum_fusion.2), channel_id=1, source_target_pairs={{0,64},{64,128},{128,192},{192,0},{1,65},{65,129},{129,193},{193,1... | collective-permute-start | bytes 393224 | tf_op jit(solution)/shard_map/ppermute | solution.py:382
  116.8 11.0 %collective-permute-start.18 = (f32[2432,128]{1,0:T(8,128)S(1)}, f32[2432,128]{1,0:T(8,128)S(1)}, u32[]{:S(2)}, u32[]{:S(2)}) collective-permute-start(f32[2432,128]{1,0:T(8,128)S(1)} %bitcast.39), channel_id=1, source_target_pairs={{0,8},{8,0},{1,9},{9,1},{2,10},{10,2},{3,11},{11,3},{4,12},{12,4},... | collective-permute-start | bytes 3735560 | tf_op jit(solution)/shard_map/ppermute | solution.py:386
  124.6 3.1 %collective-permute-start.19 = (bf16[3,512,128]{2,1,0:T(8,128)(2,1)S(1)}, bf16[3,512,128]{2,1,0:T(8,128)(2,1)}, u32[]{:S(2)}, u32[]{:S(2)}) collective-permute-start(bf16[3,512,128]{2,1,0:T(8,128)(2,1)S(1)} %pad_maximum_fusion.near_ref), channel_id=1, source_target_pairs={{0,8},{8,0},{1,9},{9,1},{2,10},{10,2},{3,11},{11,3},{4,12},{12,4},... | collective-permute-start | bytes 1179656 | tf_op jit(solution)/shard_map/ppermute | solution.py:385
  134.7 4.3 %collective-permute-start.22 = (f32[4,32,128]{2,1,0:T(8,128)S(1)}, f32[4,32,128]{2,1,0:T(8,128)S(1)}, u32[]{:S(2)}, u32[]{:S(2)}) collective-permute-start(f32[4,32,128]{2,1,0:T(8,128)S(1)} %get-tuple-element.43.refs_0_), channel_id=1, source_target_pairs={{0,48},{16,0},{32,16},{48,32},{1,49},{17,1},{33,17},{49,33},{2,50}... | collective-permute-start | bytes 196616 | tf_op jit(solution)/shard_map/ppermute | solution.py:388
  134.8 4.7 %collective-permute-start.21 = (f32[4,32,128]{2,1,0:T(8,128)S(1)}, f32[4,32,128]{2,1,0:T(8,128)S(1)}, u32[]{:S(2)}, u32[]{:S(2)}) collective-permute-start(f32[4,32,128]{2,1,0:T(8,128)S(1)} %get-tuple-element.43.refs_0_), channel_id=1, source_target_pairs={{0,32},{16,48},{32,0},{48,16},{1,33},{17,49},{33,1},{49,17},{2,34}... | collective-permute-start | bytes 196616 | tf_op jit(solution)/shard_map/ppermute | solution.py:388
  136.9 4.3 %collective-permute-start.20 = (f32[4,32,128]{2,1,0:T(8,128)S(1)}, f32[4,32,128]{2,1,0:T(8,128)S(1)}, u32[]{:S(2)}, u32[]{:S(2)}) collective-permute-start(f32[4,32,128]{2,1,0:T(8,128)S(1)} %get-tuple-element.43.refs_0_), channel_id=1, source_target_pairs={{0,16},{16,32},{32,48},{48,0},{1,17},{17,33},{33,49},{49,1},{2,18}... | collective-permute-start | bytes 196616 | tf_op jit(solution)/shard_map/ppermute | solution.py:388
  141.2 2.2 %copy-start.3 = (bf16[1024,2048]{1,0:T(8,128)(2,1)S(1)}, bf16[1024,2048]{1,0:T(8,128)(2,1)}, u32[]{:S(2)}) copy-start(bf16[1024,2048]{1,0:T(8,128)(2,1)} %shard_map.76.refs_5_) | copy-start | bytes 12582916

commit v5 on v4

--- a/solution.py
+++ b/solution.py
@@ -308,11 +308,18 @@
 
 
 def finish_kernel(place, inverse_ref, *refs):
-    *spread_refs, pbt_ref, corrected_ref, factor_ref, out_ref, wide, qbt = refs
+    *spread_refs, pbt_ref, corrected_ref, factor_ref, out_ref, wide, qbt, held, done = refs
     step = pl.program_id(0)
+    rows = out_ref.shape[0]
+
+    def fetch(k):
+        at = pl.ds(pl.multiple_of(k * rows, rows), rows)
+        return pltpu.make_async_copy(corrected_ref.at[at, :], held.at[k], done.at[k])
 
     @pl.when(step == 0)
     def _():
+        for k in range(held.shape[0]):
+            fetch(k).start()
         for d, spread_ref in enumerate(spread_refs):
             blocks, _, width = spread_ref.shape
             for k in range(blocks):
@@ -322,10 +329,9 @@
         factor_ref[...] = right / math.sqrt(ROWS)
         qbt[...] = right.astype(jnp.bfloat16)
 
-    rows = out_ref.shape[0]
     approx = dot(pbt_ref[...], qbt[...], ((0,), (0,)))
-    corrected = corrected_ref[pl.ds(pl.multiple_of(step * rows, rows), rows), :]
-    out_ref[...] = (corrected.astype(jnp.float32) - approx).astype(jnp.bfloat16)
+    fetch(step).wait()
+    out_ref[...] = (held[step].astype(jnp.float32) - approx).astype(jnp.bfloat16)
 
 
 def finish(place, inverse, spreads, pbt, corrected):
@@ -341,10 +347,15 @@
         grid=(ROWS // rows,),
         in_specs=[pl.BlockSpec(memory_space=pltpu.SMEM), vmem]
         + [vmem] * len(spreads)
-        + [pl.BlockSpec((RANK, rows), lambda i: (0, i)), vmem],
+        + [pl.BlockSpec((RANK, rows), lambda i: (0, i)), pl.BlockSpec(memory_space=pl.ANY)],
         out_specs=(pl.BlockSpec((RANK, cols), lambda i: (0, 0)), pl.BlockSpec((rows, cols), lambda i: (i, 0))),
-        scratch_shapes=[pltpu.VMEM((RANK, cols), jnp.float32), pltpu.VMEM((RANK, cols), jnp.bfloat16)],
-        compiler_params=pltpu.CompilerParams(vmem_limit_bytes=16 * MIB),
+        scratch_shapes=[
+            pltpu.VMEM((RANK, cols), jnp.float32),
+            pltpu.VMEM((RANK, cols), jnp.bfloat16),
+            pltpu.VMEM((ROWS // rows, rows, cols), jnp.bfloat16),
+            pltpu.SemaphoreType.DMA((ROWS // rows,)),
+        ],
+        compiler_params=pltpu.CompilerParams(vmem_limit_bytes=60 * MIB),
     )(place, inverse, *spreads, pbt, corrected)
 
 

time: 148 us -> 148 us (level)
  local copies, waits for them, and re-layouts: 7.53 us -> 5.95 us
  Pallas kernels: 27 us -> 28.5 us
    unnamed x11 -> x19, local copies, waits for them, and re-layouts: 7.23 us -> 5.66 us
  transfers between devices with their start and end apart: 24 -> 24, of which waited for: 13 -> 12; matrix products, arithmetic and copies ran while one was open for 2% -> 3% of each run, Pallas kernels for 8% -> 8%
where the time goes in v5:
time: 148 us
  blocking collectives  46.5 us (31%)
  starting transfers between devices  38 us (26%)
  Pallas kernels  28.5 us (19%)
  waiting for transfers between devices  24.8 us (17%)
  local copies, waits for them, and re-layouts  5.95 us (4%)
  other arithmetic  3 us (2%)
    all_to_all x2, blocking collectives, ring(): lax.all_to_all(v.reshape(RING_SIZE, SLOTS, 1, TILE), RING, 0, 0, tiled=True)  23.3 us
    all_to_all x1, blocking collectives, swap(): v = lax.all_to_all(v.reshape(size, rows, TILE), axes, 0, 0, tiled=True)  23.2 us
    ppermute x6, starting transfers between devices, exchange_sum(): total = total + lax.ppermute(sent, axis, shift(n, d)).astype(jnp.float32)  12.2 us
    ppermute x6, waiting for transfers between devices, reduce_replicas(): lax.ppermute(others[d - 1], 'y', shift(4, d)).astype(jnp.float32)  10.3 us
    ppermute x1, starting transfers between devices, shards(): other = lax.ppermute(own, 'c', SWAP)  7.81 us
    pallas_call x1, Pallas kernels, iterate(): pl.pallas_call(iterate_kernel, out_shape=(jax.ShapeDtypeStruct((RANK, ROW...  6.96 us
    pallas_call x1, Pallas kernels, corrected_sum(): pl.pallas_call(corrected_kernel, out_shape=jax.ShapeDtypeStruct(grad.shap...  6.03 us
    pallas_call x1, Pallas kernels, finish(): pl.pallas_call(finish_kernel, out_shape=(jax.ShapeDtypeStruct((RANK, cols...  5.77 us
  transfers between devices with their start and end apart: 24, of which 12 were waited for; matrix products, arithmetic and copies ran while one was open for 3% of the time, Pallas kernels for 8%

profile of v5, /device:TPU:1, one launch (start us, length us, event | category | flops | bytes accessed | tf_op | source)
XLA Modules:
  0.0 147.8 jit_solution(16926530208271337074)
XLA Ops:
  0.7 2.2 %copy-done.1 = bf16[1,1024,2048]{2,1,0:T(8,128)(2,1)S(1)} copy-done((bf16[1,1024,2048]{2,1,0:T(8,128)(2,1)S(1)}, bf16[1,1024,2048]{2,1,0:T(8,128)(2,1)}, u32[]{:S(2)}) %copy-start.1) | copy-done | bytes 4194328
  2.9 2.2 %copy-done.2 = bf16[1,1024,2048]{2,1,0:T(8,128)(2,1)S(1)} copy-done((bf16[1,1024,2048]{2,1,0:T(8,128)(2,1)S(1)}, bf16[1,1024,2048]{2,1,0:T(8,128)(2,1)}, u32[]{:S(2)}) %copy-start.2) | copy-done | bytes 4194328
  5.1 0.8 shard_map.70
  5.9 3.3 %collective-permute-start.7 = (bf16[256,2048]{1,0:T(8,128)(2,1)S(1)}, bf16[256,2048]{1,0:T(8,128)(2,1)S(1)}, u32[]{:S(2)}, u32[]{:S(2)}) collective-permute-start(bf16[256,2048]{1,0:T(8,128)(2,1)S(1)} %shard_map.70), channel_id=1, source_target_pairs={{0,8},{8,0},{1,9},{9,1},{2,10},{10,2},{3,11},{11,3},{4,12},{12,4},... | collective-permute-start | bytes 3145736 | tf_op jit(solution)/shard_map/ppermute | solution.py:106
  9.3 0.8 shard_map.68
  10.2 1.1 shard_map.67.own_ref
  11.3 0.2 collective-permute-done.7.got_ref
  11.6 1.5 %shard_map.71 = (bf16[256,512]{1,0:T(8,128)(2,1)S(1)}, bf16[256,512]{1,0:T(8,128)(2,1)}, bf16[256,512]{1,0:T(8,128)(2,1)}, bf16[256,512]{1,0:T(8,128)(2,1)}) custom-call(s32[3]{0:T(128)S(1)} %pad_add_fusion.place, bf16[512,2048]{1,0:T(8,128)(2,1)S(1)} %shard_map.67.own_ref, bf16[256,2048]{1,0:T(8,128)(2,1)S(1)} %collective-permute-done.7.got_ref), custom_call_target="tpu_custom_call" | custom-call | flops 524288 | bytes 3145728 | tf_op jit(solution)/shard_map/pallas_call | solution.py:87
  13.1 2.7 %collective-permute-start.9 = (bf16[256,512]{1,0:T(8,128)(2,1)}, bf16[256,512]{1,0:T(8,128)(2,1)}, u32[]{:S(2)}, u32[]{:S(2)}) collective-permute-start(bf16[256,512]{1,0:T(8,128)(2,1)} %get-tuple-element.31), channel_id=1, source_target_pairs={{0,48},{16,0},{32,16},{48,32},{1,49},{17,1},{33,17},{49,33},{2,50}... | collective-permute-start | bytes 786440 | tf_op jit(solution)/shard_map/ppermute | solution.py:113
  15.8 1.5 %shard_map.69 = (bf16[256,512]{1,0:T(8,128)(2,1)S(1)}, bf16[256,512]{1,0:T(8,128)(2,1)S(1)}, bf16[256,512]{1,0:T(8,128)(2,1)S(1)}, bf16[256,512]{1,0:T(8,128)(2,1)S(1)}) custom-call(s32[3]{0:T(128)S(1)} %pad_add_fusion.place, bf16[512,2048]{1,0:T(8,128)(2,1)S(1)} %shard_map.67.own_ref, bf16[256,2048]{1,0:T(8,128)(2,1)} %collective-permute-done.got_ref), custom_call_target="tpu_custom_call" | custom-call | flops 524288 | bytes 3145728 | tf_op jit(solution)/shard_map/pallas_call | solution.py:87
  17.3 0.7 collective-permute-start.1
  17.9 2.1 %collective-permute-start.2 = (bf16[256,512]{1,0:T(8,128)(2,1)S(1)}, bf16[256,512]{1,0:T(8,128)(2,1)S(1)}, u32[]{:S(2)}, u32[]{:S(2)}) collective-permute-start(bf16[256,512]{1,0:T(8,128)(2,1)S(1)} %get-tuple-element.27), channel_id=1, source_target_pairs={{0,48},{16,0},{32,16},{48,32},{1,49},{17,1},{33,17},{49,33},{2,50}... | collective-permute-start | bytes 786440 | tf_op jit(solution)/shard_map/ppermute | solution.py:113
  20.0 2.6 %collective-permute-done.8 = bf16[256,512]{1,0:T(8,128)(2,1)} collective-permute-done((bf16[256,512]{1,0:T(8,128)(2,1)}, bf16[256,512]{1,0:T(8,128)(2,1)}, u32[]{:S(2)}, u32[]{:S(2)}) %collective-permute-start.8) | collective-permute-done | bytes 262176 | tf_op jit(solution)/shard_map/ppermute | solution.py:113
  22.6 4.7 %collective-permute-done.10 = bf16[256,512]{1,0:T(8,128)(2,1)} collective-permute-done((bf16[256,512]{1,0:T(8,128)(2,1)}, bf16[256,512]{1,0:T(8,128)(2,1)}, u32[]{:S(2)}, u32[]{:S(2)}) %collective-permute-start.10) | collective-permute-done | bytes 262176 | tf_op jit(solution)/shard_map/ppermute | solution.py:113
  27.3 1.3 add_convert_fusion
  28.6 1.7 %collective-permute-start.11 = (bf16[256,128]{1,0:T(8,128)(2,1)S(1)}, bf16[256,128]{1,0:T(8,128)(2,1)S(1)}, u32[]{:S(2)}, u32[]{:S(2)}) collective-permute-start(bf16[256,128]{1,0:T(8,128)(2,1)S(1)} %get-tuple-element.61), channel_id=1, source_target_pairs={{0,64},{64,128},{128,192},{192,0},{1,65},{65,129},{129,193},{193,1... | collective-permute-start | bytes 196616 | tf_op jit(solution)/shard_map/ppermute | solution.py:43
  30.3 3.0 %collective-permute-start.13 = (bf16[256,128]{1,0:T(8,128)(2,1)S(1)}, bf16[256,128]{1,0:T(8,128)(2,1)S(1)}, u32[]{:S(2)}, u32[]{:S(2)}) collective-permute-start(bf16[256,128]{1,0:T(8,128)(2,1)S(1)} %get-tuple-element.62), channel_id=1, source_target_pairs={{0,128},{64,192},{128,0},{192,64},{1,129},{65,193},{129,1},{193,65... | collective-permute-start | bytes 196616 | tf_op jit(solution)/shard_map/ppermute | solution.py:43
  33.3 0.4 collective-permute-done.1
  33.7 2.0 %collective-permute-start.12 = (bf16[256,128]{1,0:T(8,128)(2,1)S(1)}, bf16[256,128]{1,0:T(8,128)(2,1)S(1)}, u32[]{:S(2)}, u32[]{:S(2)}) collective-permute-start(bf16[256,128]{1,0:T(8,128)(2,1)S(1)} %get-tuple-element.63), channel_id=1, source_target_pairs={{0,192},{64,0},{128,64},{192,128},{1,193},{65,1},{129,65},{193,129... | collective-permute-start | bytes 196616 | tf_op jit(solution)/shard_map/ppermute | solution.py:43
  35.8 2.7 %collective-permute-done.3 = bf16[256,512]{1,0:T(8,128)(2,1)S(1)} collective-permute-done((bf16[256,512]{1,0:T(8,128)(2,1)S(1)}, bf16[256,512]{1,0:T(8,128)(2,1)S(1)}, u32[]{:S(2)}, u32[]{:S(2)}) %collective-permute-start.3) | collective-permute-done | bytes 262176 | tf_op jit(solution)/shard_map/ppermute | solution.py:113
  38.6 1.7 %collective-permute-start.4 = (bf16[256,128]{1,0:T(8,128)(2,1)S(1)}, bf16[256,128]{1,0:T(8,128)(2,1)S(1)}, u32[]{:S(2)}, u32[]{:S(2)}) collective-permute-start(bf16[256,128]{1,0:T(8,128)(2,1)S(1)} %get-tuple-element.58), channel_id=1, source_target_pairs={{0,64},{64,128},{128,192},{192,0},{1,65},{65,129},{129,193},{193,1... | collective-permute-start | bytes 196616 | tf_op jit(solution)/shard_map/ppermute | solution.py:43
  40.4 3.0 %collective-permute-start.6 = (bf16[256,128]{1,0:T(8,128)(2,1)S(1)}, bf16[256,128]{1,0:T(8,128)(2,1)S(1)}, u32[]{:S(2)}, u32[]{:S(2)}) collective-permute-start(bf16[256,128]{1,0:T(8,128)(2,1)S(1)} %get-tuple-element.59), channel_id=1, source_target_pairs={{0,128},{64,192},{128,0},{192,64},{1,129},{65,193},{129,1},{193,65... | collective-permute-start | bytes 196616 | tf_op jit(solution)/shard_map/ppermute | solution.py:43
  43.3 0.7 collective-permute-start.5
  44.1 0.6 collective-permute-done.4
  44.8 3.4 %collective-permute-done.6 = bf16[256,128]{1,0:T(8,128)(2,1)S(1)} collective-permute-done((bf16[256,128]{1,0:T(8,128)(2,1)S(1)}, bf16[256,128]{1,0:T(8,128)(2,1)S(1)}, u32[]{:S(2)}, u32[]{:S(2)}) %collective-permute-start.6) | collective-permute-done | bytes 65568 | tf_op jit(solution)/shard_map/ppermute | solution.py:43
  48.3 1.5 %collective-permute-start.14 = (bf16[512,128]{1,0:T(8,128)(2,1)S(1)}, bf16[512,128]{1,0:T(8,128)(2,1)S(1)}, u32[]{:S(2)}, u32[]{:S(2)}) collective-permute-start(bf16[512,128]{1,0:T(8,128)(2,1)S(1)} %pad_maximum_fusion.2), channel_id=1, source_target_pairs={{0,8},{8,0},{1,9},{9,1},{2,10},{10,2},{3,11},{11,3},{4,12},{12,4},... | collective-permute-start | bytes 393224 | tf_op jit(solution)/shard_map/ppermute | solution.py:121
  49.9 0.9 collective-permute-done.14
  50.9 1.3 shard_map.72
  52.2 23.2 %all_to_all.20 = f32[16,152,128]{2,1,0:T(8,128)S(1)} all-to-all(f32[16,152,128]{2,1,0:T(8,128)S(1)} %bitcast.37), channel_id=1, replica_groups=mesh['zl'=4,'y'=4,'c'=2,'x'=4,'zh'=2] {'x','y'}, dimensions={0} | all-to-all | bytes 2490368 | tf_op jit(solution)/shard_map/all_to_all | solution.py:366
  75.5 13.6 %all_to_all.21 = f32[8,19,1,128]{3,2,1,0:T(1,128)S(1)} all-to-all(f32[8,19,1,128]{3,2,1,0:T(1,128)S(1)} %bitcast.41), channel_id=1, replica_groups=mesh['zl'=4,'y'=4,'c'=2,'x'=4,'zh'=2] {'zh','zl'}, dimensions={0} | all-to-all | bytes 155648 | tf_op jit(solution)/shard_map/all_to_all | solution.py:370
  89.1 9.7 %all_to_all.22 = f32[8,19,1,128]{3,2,1,0:T(1,128)S(1)} all-to-all(f32[8,19,1,128]{3,2,1,0:T(1,128)S(1)} %bitcast.44), channel_id=1, replica_groups=mesh['zl'=4,'y'=4,'c'=2,'x'=4,'zh'=2] {'zh','zl'}, dimensions={0} | all-to-all | bytes 155648 | tf_op jit(solution)/shard_map/all_to_all | solution.py:370
  98.8 1.1 shard_map.75
  99.9 3.9 %all-to-all-start.3 = ((f32[16,152,128]{2,1,0:T(8,128)}), f32[16,152,128]{2,1,0:T(8,128)S(1)}, u32[]{:S(2)}, u32[]{:S(2)}) async-start(f32[16,152,128]{2,1,0:T(8,128)} %bitcast.14), calls=%async_computation.3 | async-start | bytes 2490368 | tf_op jit(solution)/shard_map/all_to_all | solution.py:366
  104.0 1.2 collective-permute-start.16
  105.4 6.0 %shard_map.76.refs_5_ = bf16[1024,2048]{1,0:T(8,128)(2,1)} custom-call(bf16[1024,2048]{1,0:T(8,128)(2,1)} %bitcast.29, bf16[1024,2048]{1,0:T(8,128)(2,1)} %bitcast.33), custom_call_target="tpu_custom_call" | custom-call | flops 1000 | bytes 1000 | tf_op jit(solution)/shard_map/pallas_call | solution.py:299
  111.4 1.2 collective-permute-done.16
  112.7 4.1 %all-to-all-done.3 = f32[16,152,128]{2,1,0:T(8,128)S(1)} async-done(((f32[16,152,128]{2,1,0:T(8,128)}), f32[16,152,128]{2,1,0:T(8,128)S(1)}, u32[]{:S(2)}, u32[]{:S(2)}) %all-to-all-start.3) | async-done | bytes 1245216 | tf_op jit(solution)/shard_map/all_to_all | solution.py:366
  116.8 7.8 %collective-permute-start.18 = (f32[2432,128]{1,0:T(8,128)S(1)}, f32[2432,128]{1,0:T(8,128)S(1)}, u32[]{:S(2)}, u32[]{:S(2)}) collective-permute-start(f32[2432,128]{1,0:T(8,128)S(1)} %bitcast.39), channel_id=1, source_target_pairs={{0,8},{8,0},{1,9},{9,1},{2,10},{10,2},{3,11},{11,3},{4,12},{12,4},... | collective-permute-start | bytes 3735560 | tf_op jit(solution)/shard_map/ppermute | solution.py:397
  124.7 0.6 pad_add_fusion.1.place
  125.3 2.4 %collective-permute-done.19.across_ref = bf16[3,512,128]{2,1,0:T(8,128)(2,1)} collective-permute-done((bf16[3,512,128]{2,1,0:T(8,128)(2,1)S(1)}, bf16[3,512,128]{2,1,0:T(8,128)(2,1)}, u32[]{:S(2)}, u32[]{:S(2)}) %collective-permute-start.19) | collective-permute-done | bytes 393248 | tf_op jit(solution)/shard_map/ppermute | solution.py:396
  127.7 7.0 %shard_map.77 = (f32[32,1024]{1,0:T(8,128)S(1)}, f32[4,32,128]{2,1,0:T(8,128)S(1)}) custom-call(s32[1]{0:T(128)} %bitcast.core, s32[18,2]{1,0:T(8,128)S(1)} %copy.18.table.own_table, s32[18,2]{1,0:T(8,128)S(1)} %copy.19.other_table, f32[2432,128]{1,0:T(8,128)S(1)} %bitcast.40, f32[2432,128]{1,0:T(8,128)S(1)} %collective-permute-done.18.other_ref, ...), custom_call_target="tpu_custom_call" | custom-call | tf_op jit(solution)/shard_map/pallas_call | solution.py:256
  134.8 2.1 %collective-permute-start.21 = (f32[4,32,128]{2,1,0:T(8,128)S(1)}, f32[4,32,128]{2,1,0:T(8,128)S(1)}, u32[]{:S(2)}, u32[]{:S(2)}) collective-permute-start(f32[4,32,128]{2,1,0:T(8,128)S(1)} %get-tuple-element.43.refs_0_), channel_id=1, source_target_pairs={{0,32},{16,48},{32,0},{48,16},{1,33},{17,49},{33,1},{49,17},{2,34}... | collective-permute-start | bytes 196616 | tf_op jit(solution)/shard_map/ppermute | solution.py:399
  136.9 1.4 shard_map.78
  138.3 0.7 convert_element_type.83.refs_4_
  139.0 0.7 copy.20
  139.7 1.5 %collective-permute-done.20.refs_1_ = f32[4,32,128]{2,1,0:T(8,128)S(1)} collective-permute-done((f32[4,32,128]{2,1,0:T(8,128)S(1)}, f32[4,32,128]{2,1,0:T(8,128)S(1)}, u32[]{:S(2)}, u32[]{:S(2)}) %collective-permute-start.20) | collective-permute-done | bytes 65568 | tf_op jit(solution)/shard_map/ppermute | solution.py:399
  141.2 0.6 copy-done.7
  141.8 5.8 %shard_map.79 = (f32[32,2048]{1,0:T(8,128)}, bf16[1024,2048]{1,0:T(8,128)(2,1)}) custom-call(s32[2]{0:T(128)} %pad_add_fusion.1.place, f32[32,32]{1,0:T(8,128)} %copy-done.4, f32[4,32,128]{2,1,0:T(8,128)} %copy-done.3, f32[4,32,128]{2,1,0:T(8,128)} %copy-done.7, f32[4,32,128]{2,1,0:T(8,128)} %copy-done.6, f32[4,32,128]{2,1,0:T(8,128)} %copy-done.5, ...), custom_call_target="tpu_custom_call" | custom-call | tf_op jit(solution)/shard_map/pallas_call | solution.py:341
  (53 shorter events, 1.4 us)
Async XLA Ops:
  0.6 49.3 %copy-start = (bf16[2048,32]{0,1:T(8,128)(2,1)S(1)}, bf16[2048,32]{0,1:T(8,128)(2,1)}, u32[]{:S(2)}) copy-start(bf16[2048,32]{0,1:T(8,128)(2,1)} %param.6) | copy-start | bytes 393220
  0.7 2.2 %copy-start.1 = (bf16[1,1024,2048]{2,1,0:T(8,128)(2,1)S(1)}, bf16[1,1024,2048]{2,1,0:T(8,128)(2,1)}, u32[]{:S(2)}) copy-start(bf16[1,1024,2048]{2,1,0:T(8,128)(2,1)} %param.4) | copy-start | bytes 12582916
  2.9 2.2 %copy-start.2 = (bf16[1,1024,2048]{2,1,0:T(8,128)(2,1)S(1)}, bf16[1,1024,2048]{2,1,0:T(8,128)(2,1)}, u32[]{:S(2)}) copy-start(bf16[1,1024,2048]{2,1,0:T(8,128)(2,1)} %param.5) | copy-start | bytes 12582916
  5.9 5.6 %collective-permute-start.7 = (bf16[256,2048]{1,0:T(8,128)(2,1)S(1)}, bf16[256,2048]{1,0:T(8,128)(2,1)S(1)}, u32[]{:S(2)}, u32[]{:S(2)}) collective-permute-start(bf16[256,2048]{1,0:T(8,128)(2,1)S(1)} %shard_map.70), channel_id=1, source_target_pairs={{0,8},{8,0},{1,9},{9,1},{2,10},{10,2},{3,11},{11,3},{4,12},{12,4},... | collective-permute-start | bytes 3145736 | tf_op jit(solution)/shard_map/ppermute | solution.py:106
  10.1 5.7 %collective-permute-start = (bf16[256,2048]{1,0:T(8,128)(2,1)S(1)}, bf16[256,2048]{1,0:T(8,128)(2,1)}, u32[]{:S(2)}, u32[]{:S(2)}) collective-permute-start(bf16[256,2048]{1,0:T(8,128)(2,1)S(1)} %shard_map.68), channel_id=1, source_target_pairs={{0,8},{8,0},{1,9},{9,1},{2,10},{10,2},{3,11},{11,3},{4,12},{12,4},... | collective-permute-start | bytes 3145736 | tf_op jit(solution)/shard_map/ppermute | solution.py:106
  13.1 9.5 %collective-permute-start.8 = (bf16[256,512]{1,0:T(8,128)(2,1)}, bf16[256,512]{1,0:T(8,128)(2,1)}, u32[]{:S(2)}, u32[]{:S(2)}) collective-permute-start(bf16[256,512]{1,0:T(8,128)(2,1)} %get-tuple-element.30), channel_id=1, source_target_pairs={{0,16},{16,32},{32,48},{48,0},{1,17},{17,33},{33,49},{49,1},{2,18}... | collective-permute-start | bytes 786440 | tf_op jit(solution)/shard_map/ppermute | solution.py:113
  13.1 9.5 %collective-permute-start.9 = (bf16[256,512]{1,0:T(8,128)(2,1)}, bf16[256,512]{1,0:T(8,128)(2,1)}, u32[]{:S(2)}, u32[]{:S(2)}) collective-permute-start(bf16[256,512]{1,0:T(8,128)(2,1)} %get-tuple-element.31), channel_id=1, source_target_pairs={{0,48},{16,0},{32,16},{48,32},{1,49},{17,1},{33,17},{49,33},{2,50}... | collective-permute-start | bytes 786440 | tf_op jit(solution)/shard_map/ppermute | solution.py:113
  15.8 11.5 %collective-permute-start.10 = (bf16[256,512]{1,0:T(8,128)(2,1)}, bf16[256,512]{1,0:T(8,128)(2,1)}, u32[]{:S(2)}, u32[]{:S(2)}) collective-permute-start(bf16[256,512]{1,0:T(8,128)(2,1)} %get-tuple-element.32), channel_id=1, source_target_pairs={{0,32},{16,48},{32,0},{48,16},{1,33},{17,49},{33,1},{49,17},{2,34}... | collective-permute-start | bytes 786440 | tf_op jit(solution)/shard_map/ppermute | solution.py:113
  17.3 16.4 %collective-permute-start.1 = (bf16[256,512]{1,0:T(8,128)(2,1)S(1)}, bf16[256,512]{1,0:T(8,128)(2,1)S(1)}, u32[]{:S(2)}, u32[]{:S(2)}) collective-permute-start(bf16[256,512]{1,0:T(8,128)(2,1)S(1)} %get-tuple-element.26), channel_id=1, source_target_pairs={{0,16},{16,32},{32,48},{48,0},{1,17},{17,33},{33,49},{49,1},{2,18}... | collective-permute-start | bytes 786440 | tf_op jit(solution)/shard_map/ppermute | solution.py:113
  17.9 17.8 %collective-permute-start.2 = (bf16[256,512]{1,0:T(8,128)(2,1)S(1)}, bf16[256,512]{1,0:T(8,128)(2,1)S(1)}, u32[]{:S(2)}, u32[]{:S(2)}) collective-permute-start(bf16[256,512]{1,0:T(8,128)(2,1)S(1)} %get-tuple-element.27), channel_id=1, source_target_pairs={{0,48},{16,0},{32,16},{48,32},{1,49},{17,1},{33,17},{49,33},{2,50}... | collective-permute-start | bytes 786440 | tf_op jit(solution)/shard_map/ppermute | solution.py:113
  22.6 15.8 %collective-permute-start.3 = (bf16[256,512]{1,0:T(8,128)(2,1)S(1)}, bf16[256,512]{1,0:T(8,128)(2,1)S(1)}, u32[]{:S(2)}, u32[]{:S(2)}) collective-permute-start(bf16[256,512]{1,0:T(8,128)(2,1)S(1)} %get-tuple-element.28), channel_id=1, source_target_pairs={{0,32},{16,48},{32,0},{48,16},{1,33},{17,49},{33,1},{49,17},{2,34}... | collective-permute-start | bytes 786440 | tf_op jit(solution)/shard_map/ppermute | solution.py:113
  27.3 22.5 %copy-start.8 = (s32[2,18,2]{1,2,0:T(2,128)S(1)}, s32[2,18,2]{1,2,0:T(2,128)}, u32[]{:S(2)}) copy-start(s32[2,18,2]{1,2,0:T(2,128)} %constant.60.clone) | copy-start | bytes 868
  28.6 14.7 %collective-permute-start.11 = (bf16[256,128]{1,0:T(8,128)(2,1)S(1)}, bf16[256,128]{1,0:T(8,128)(2,1)S(1)}, u32[]{:S(2)}, u32[]{:S(2)}) collective-permute-start(bf16[256,128]{1,0:T(8,128)(2,1)S(1)} %get-tuple-element.61), channel_id=1, source_target_pairs={{0,64},{64,128},{128,192},{192,0},{1,65},{65,129},{129,193},{193,1... | collective-permute-start | bytes 196616 | tf_op jit(solution)/shard_map/ppermute | solution.py:43
  30.3 13.7 %collective-permute-start.13 = (bf16[256,128]{1,0:T(8,128)(2,1)S(1)}, bf16[256,128]{1,0:T(8,128)(2,1)S(1)}, u32[]{:S(2)}, u32[]{:S(2)}) collective-permute-start(bf16[256,128]{1,0:T(8,128)(2,1)S(1)} %get-tuple-element.62), channel_id=1, source_target_pairs={{0,128},{64,192},{128,0},{192,64},{1,129},{65,193},{129,1},{193,65... | collective-permute-start | bytes 196616 | tf_op jit(solution)/shard_map/ppermute | solution.py:43
  33.7 10.4 %collective-permute-start.12 = (bf16[256,128]{1,0:T(8,128)(2,1)S(1)}, bf16[256,128]{1,0:T(8,128)(2,1)S(1)}, u32[]{:S(2)}, u32[]{:S(2)}) collective-permute-start(bf16[256,128]{1,0:T(8,128)(2,1)S(1)} %get-tuple-element.63), channel_id=1, source_target_pairs={{0,192},{64,0},{128,64},{192,128},{1,193},{65,1},{129,65},{193,129... | collective-permute-start | bytes 196616 | tf_op jit(solution)/shard_map/ppermute | solution.py:43
  38.6 6.2 %collective-permute-start.4 = (bf16[256,128]{1,0:T(8,128)(2,1)S(1)}, bf16[256,128]{1,0:T(8,128)(2,1)S(1)}, u32[]{:S(2)}, u32[]{:S(2)}) collective-permute-start(bf16[256,128]{1,0:T(8,128)(2,1)S(1)} %get-tuple-element.58), channel_id=1, source_target_pairs={{0,64},{64,128},{128,192},{192,0},{1,65},{65,129},{129,193},{193,1... | collective-permute-start | bytes 196616 | tf_op jit(solution)/shard_map/ppermute | solution.py:43
  40.4 7.8 %collective-permute-start.6 = (bf16[256,128]{1,0:T(8,128)(2,1)S(1)}, bf16[256,128]{1,0:T(8,128)(2,1)S(1)}, u32[]{:S(2)}, u32[]{:S(2)}) collective-permute-start(bf16[256,128]{1,0:T(8,128)(2,1)S(1)} %get-tuple-element.59), channel_id=1, source_target_pairs={{0,128},{64,192},{128,0},{192,64},{1,129},{65,193},{129,1},{193,65... | collective-permute-start | bytes 196616 | tf_op jit(solution)/shard_map/ppermute | solution.py:43
  43.3 4.9 %collective-permute-start.5 = (bf16[256,128]{1,0:T(8,128)(2,1)S(1)}, bf16[256,128]{1,0:T(8,128)(2,1)S(1)}, u32[]{:S(2)}, u32[]{:S(2)}) collective-permute-start(bf16[256,128]{1,0:T(8,128)(2,1)S(1)} %get-tuple-element.60), channel_id=1, source_target_pairs={{0,192},{64,0},{128,64},{192,128},{1,193},{65,1},{129,65},{193,129... | collective-permute-start | bytes 196616 | tf_op jit(solution)/shard_map/ppermute | solution.py:43
  48.3 2.5 %collective-permute-start.14 = (bf16[512,128]{1,0:T(8,128)(2,1)S(1)}, bf16[512,128]{1,0:T(8,128)(2,1)S(1)}, u32[]{:S(2)}, u32[]{:S(2)}) collective-permute-start(bf16[512,128]{1,0:T(8,128)(2,1)S(1)} %pad_maximum_fusion.2), channel_id=1, source_target_pairs={{0,8},{8,0},{1,9},{9,1},{2,10},{10,2},{3,11},{11,3},{4,12},{12,4},... | collective-permute-start | bytes 393224 | tf_op jit(solution)/shard_map/ppermute | solution.py:121
  99.9 16.9 %all-to-all-start.3 = ((f32[16,152,128]{2,1,0:T(8,128)}), f32[16,152,128]{2,1,0:T(8,128)S(1)}, u32[]{:S(2)}, u32[]{:S(2)}) async-start(f32[16,152,128]{2,1,0:T(8,128)} %bitcast.14), calls=%async_computation.3 | async-start | bytes 2490368 | tf_op jit(solution)/shard_map/all_to_all | solution.py:366
  103.8 7.6 %collective-permute-start.17 = (bf16[512,128]{1,0:T(8,128)(2,1)S(1)}, bf16[512,128]{1,0:T(8,128)(2,1)S(1)}, u32[]{:S(2)}, u32[]{:S(2)}) collective-permute-start(bf16[512,128]{1,0:T(8,128)(2,1)S(1)} %pad_maximum_fusion.2), channel_id=1, source_target_pairs={{0,192},{64,0},{128,64},{192,128},{1,193},{65,1},{129,65},{193,129... | collective-permute-start | bytes 393224 | tf_op jit(solution)/shard_map/ppermute | solution.py:393
  104.0 8.6 %collective-permute-start.16 = (bf16[512,128]{1,0:T(8,128)(2,1)S(1)}, bf16[512,128]{1,0:T(8,128)(2,1)S(1)}, u32[]{:S(2)}, u32[]{:S(2)}) collective-permute-start(bf16[512,128]{1,0:T(8,128)(2,1)S(1)} %pad_maximum_fusion.2), channel_id=1, source_target_pairs={{0,128},{64,192},{128,0},{192,64},{1,129},{65,193},{129,1},{193,65... | collective-permute-start | bytes 393224 | tf_op jit(solution)/shard_map/ppermute | solution.py:393
  105.3 7.3 %collective-permute-start.15 = (bf16[512,128]{1,0:T(8,128)(2,1)S(1)}, bf16[512,128]{1,0:T(8,128)(2,1)S(1)}, u32[]{:S(2)}, u32[]{:S(2)}) collective-permute-start(bf16[512,128]{1,0:T(8,128)(2,1)S(1)} %pad_maximum_fusion.2), channel_id=1, source_target_pairs={{0,64},{64,128},{128,192},{192,0},{1,65},{65,129},{129,193},{193,1... | collective-permute-start | bytes 393224 | tf_op jit(solution)/shard_map/ppermute | solution.py:393
  116.8 10.9 %collective-permute-start.18 = (f32[2432,128]{1,0:T(8,128)S(1)}, f32[2432,128]{1,0:T(8,128)S(1)}, u32[]{:S(2)}, u32[]{:S(2)}) collective-permute-start(f32[2432,128]{1,0:T(8,128)S(1)} %bitcast.39), channel_id=1, source_target_pairs={{0,8},{8,0},{1,9},{9,1},{2,10},{10,2},{3,11},{11,3},{4,12},{12,4},... | collective-permute-start | bytes 3735560 | tf_op jit(solution)/shard_map/ppermute | solution.py:397
  124.6 3.1 %collective-permute-start.19 = (bf16[3,512,128]{2,1,0:T(8,128)(2,1)S(1)}, bf16[3,512,128]{2,1,0:T(8,128)(2,1)}, u32[]{:S(2)}, u32[]{:S(2)}) collective-permute-start(bf16[3,512,128]{2,1,0:T(8,128)(2,1)S(1)} %pad_maximum_fusion.near_ref), channel_id=1, source_target_pairs={{0,8},{8,0},{1,9},{9,1},{2,10},{10,2},{3,11},{11,3},{4,12},{12,4},... | collective-permute-start | bytes 1179656 | tf_op jit(solution)/shard_map/ppermute | solution.py:396
  134.7 6.5 %copy-start.3 = (f32[4,32,128]{2,1,0:T(8,128)}, f32[4,32,128]{2,1,0:T(8,128)S(1)}, u32[]{:S(2)}) copy-start(f32[4,32,128]{2,1,0:T(8,128)S(1)} %get-tuple-element.43.refs_0_) | copy-start | bytes 196612
  134.7 4.9 %collective-permute-start.22 = (f32[4,32,128]{2,1,0:T(8,128)S(1)}, f32[4,32,128]{2,1,0:T(8,128)S(1)}, u32[]{:S(2)}, u32[]{:S(2)}) collective-permute-start(f32[4,32,128]{2,1,0:T(8,128)S(1)} %get-tuple-element.43.refs_0_), channel_id=1, source_target_pairs={{0,48},{16,0},{32,16},{48,32},{1,49},{17,1},{33,17},{49,33},{2,50}... | collective-permute-start | bytes 196616 | tf_op jit(solution)/shard_map/ppermute | solution.py:399
  134.8 4.8 %collective-permute-start.21 = (f32[4,32,128]{2,1,0:T(8,128)S(1)}, f32[4,32,128]{2,1,0:T(8,128)S(1)}, u32[]{:S(2)}, u32[]{:S(2)}) collective-permute-start(f32[4,32,128]{2,1,0:T(8,128)S(1)} %get-tuple-element.43.refs_0_), channel_id=1, source_target_pairs={{0,32},{16,48},{32,0},{48,16},{1,33},{17,49},{33,1},{49,17},{2,34}... | collective-permute-start | bytes 196616 | tf_op jit(solution)/shard_map/ppermute | solution.py:399
  136.9 4.3 %collective-permute-start.20 = (f32[4,32,128]{2,1,0:T(8,128)S(1)}, f32[4,32,128]{2,1,0:T(8,128)S(1)}, u32[]{:S(2)}, u32[]{:S(2)}) collective-permute-start(f32[4,32,128]{2,1,0:T(8,128)S(1)} %get-tuple-element.43.refs_0_), channel_id=1, source_target_pairs={{0,16},{16,32},{32,48},{48,0},{1,17},{17,33},{33,49},{49,1},{2,18}... | collective-permute-start | bytes 196616 | tf_op jit(solution)/shard_map/ppermute | solution.py:399
  138.3 2.9 %copy-start.4 = (f32[32,32]{1,0:T(8,128)}, f32[32,32]{1,0:T(8,128)S(1)}, u32[]{:S(2)}) copy-start(f32[32,32]{1,0:T(8,128)S(1)} %get-tuple-element.42.inverse_ref) | copy-start | bytes 12292
  139.6 1.6 %copy-start.5 = (f32[4,32,128]{2,1,0:T(8,128)}, f32[4,32,128]{2,1,0:T(8,128)S(1)}, u32[]{:S(2)}) copy-start(f32[4,32,128]{2,1,0:T(8,128)S(1)} %collective-permute-done.22.refs_3_) | copy-start | bytes 196612
  139.7 1.6 %copy-start.6 = (f32[4,32,128]{2,1,0:T(8,128)}, f32[4,32,128]{2,1,0:T(8,128)S(1)}, u32[]{:S(2)}) copy-start(f32[4,32,128]{2,1,0:T(8,128)S(1)} %collective-permute-done.21.refs_2_) | copy-start | bytes 196612
  141.2 0.6 copy-start.7
